TPU v7x, 32 devices: a whole 2x2x4 slice. The times are simulated.
32 devices in a mesh: grp: 4 (over z), blk: 8 (over y, x, core).
Axes of the slice: x: 2, y: 2, z: 4, core: 2. Of those that a mesh axis runs over, the one named last changes fastest.
Arguments:
- integrals: bfloat16 [32, 2048, 2048], P('blk', None, 'grp'), as said below
- tile_mask: int32 [16, 16], replicated, may hold values from 0 to 1, as said below
- tile_owner: int32 [16], replicated, may hold values from 0 to 15, as said below
- occupied_tiles: bfloat16 [16384, 128], P(('grp', 'blk')), may hold values from -0.1875 to 0.1875
- occupied_offsets: int32 [8], replicated, may hold values from 0 to 15, as said below
- virtual_tiles: bfloat16 [16384, 128], P(('grp', 'blk')), may hold values from -0.1875 to 0.1875
- virtual_offsets: int32 [8], replicated, may hold values from 0 to 15, as said below
Outputs:
- polarizability: float32 [32, 32], P('blk')
Inputs may be any that keep to these rules, and one draw needn't show every extreme that they name: `integrals`: after column slot s is placed at basis tile tile_owner[s], the tensor is symmetric in its two basis indices. `tile_mask`: symmetric, with ones on the diagonal. `tile_owner`: each tile exactly once. `occupied_offsets`: 8 different tile offsets, among them 0 and 15. `virtual_offsets`: 8 different tile offsets, among them 0 and 15.
All inputs are finite; a program needn't handle non-finite values.
Results may differ from a plain program's by a relative error of at most 0.004.
Values may be sent and summed in bfloat16 or wider, within the bound.
No kernel may reach another device: no remote copies, remote signals or barrier semaphores. Data moves between devices by JAX's collectives and lax.ppermute only.
A program may use at most 256 MiB of HBM per device.

v0:
```python
import jax
import jax.numpy as jnp
from jax import lax
from jax.sharding import PartitionSpec as P

NT = 16


def body(
    integrals,
    tile_mask,
    tile_owner,
    occupied_tiles,
    occupied_offsets,
    virtual_tiles,
    virtual_offsets,
):
    aux_local, basis_size, local_width = integrals.shape
    tile_width = basis_size // NT
    kcount = occupied_offsets.shape[0]
    local_tiles = local_width // tile_width
    group_index = lax.axis_index("grp")
    local_owner = lax.dynamic_slice_in_dim(tile_owner, group_index * local_tiles, local_tiles)
    matches = (local_owner[None, :, None] == jnp.arange(NT, dtype=jnp.int32)[None, None, :]).astype(
        jnp.int32
    )
    column_mask = jnp.sum(tile_mask[:, None, :] * matches, axis=2)
    blocked = integrals.reshape(aux_local, NT, tile_width, local_tiles, tile_width)
    masked = blocked * column_mask.astype(jnp.bfloat16)[None, :, None, :, None]
    masked = masked.reshape(aux_local, NT, tile_width, local_width)
    occupied_all, virtual_all = (
        lax.all_gather(occupied_tiles, ("grp", "blk"), axis=0, tiled=True),
        lax.all_gather(virtual_tiles, ("grp", "blk"), axis=0, tiled=True),
    )
    occupied_all = occupied_all.reshape(NT, kcount, tile_width, tile_width)
    virtual_all = virtual_all.reshape(NT, kcount, tile_width, tile_width)
    source_rows = (tile_owner[:, None] - occupied_offsets[None, :]) % NT
    partner_rows = (tile_owner[:, None] + virtual_offsets[None, :]) % NT
    virtual_pick = virtual_all[tile_owner]
    occupied_sum = jnp.zeros((aux_local, NT, tile_width, local_width), jnp.float32)
    virtual_sum = jnp.zeros((aux_local, local_width, NT, tile_width), jnp.float32)
    for slot in range(kcount):
        occupied_pick = occupied_all[source_rows[:, slot], slot]
        occupied_inputs = masked[:, source_rows[:, slot]]
        occupied_sum = occupied_sum + jnp.einsum(
            "tmn,ptml->ptnl", occupied_pick, occupied_inputs, preferred_element_type=jnp.float32
        )
        virtual_inputs = masked[:, partner_rows[:, slot]]
        virtual_sum = virtual_sum + jnp.einsum(
            "tnm,ptml->pltn",
            virtual_pick[:, slot],
            virtual_inputs,
            preferred_element_type=jnp.float32,
        )
    occupied_part = occupied_sum.astype(jnp.bfloat16)
    virtual_part = virtual_sum.astype(jnp.bfloat16).reshape(
        aux_local, local_tiles, tile_width, basis_size
    )
    occupied_moved = lax.all_to_all(occupied_part, "grp", split_axis=1, concat_axis=3, tiled=True)
    occupied_full, virtual_full = (
        lax.all_to_all(occupied_moved, "blk", split_axis=2, concat_axis=0, tiled=True),
        lax.all_to_all(virtual_part, "blk", split_axis=2, concat_axis=0, tiled=True),
    )
    left_side = occupied_full.reshape(occupied_full.shape[0], -1)
    right_side = virtual_full.reshape(virtual_full.shape[0], -1)
    partial_sum = jnp.einsum(
        "pe,qe->pq", left_side, right_side, preferred_element_type=jnp.float32
    ) * (1.0 / basis_size)
    total = lax.psum(partial_sum, ("grp", "blk"))
    return lax.dynamic_slice_in_dim(total, lax.axis_index("blk") * aux_local, aux_local, 0)


def solution(mesh):
    in_specs = (
        P("blk", None, "grp"),
        P(),
        P(),
        P(("grp", "blk"), None),
        P(),
        P(("grp", "blk"), None),
        P(),
    )
    out_specs = P("blk", None)
    return jax.shard_map(body, mesh=mesh, in_specs=in_specs, out_specs=out_specs, check_vma=False)
```

profile of v0, /device:TPU:0, one launch (start us, length us, event | category | flops | bytes accessed | tf_op | source)
XLA Modules:
  0.0 755.2 jit_solution(1096373729819921566)
XLA Ops:
  11.3 7.1 broadcast_multiply_fusion
  18.4 8.3 %gather_fusion.12 = bf16[16,4,128,512]{3,2,1,0:T(8,128)(2,1)} fusion(bf16[4,16,128,512]{3,2,1,0:T(8,128)(2,1)} %broadcast_multiply_fusion, s32[1024]{0:T(1024)S(1)} %get-tuple-element.32), kind=kCustom, calls=%fused_computation.12 | custom fusion | bytes 16777280 | tf_op jit(solution)/shard_map/gather | solution.py:44
  26.7 8.2 %gather_fusion.10 = bf16[16,4,128,512]{3,2,1,0:T(8,128)(2,1)} fusion(bf16[4,16,128,512]{3,2,1,0:T(8,128)(2,1)} %broadcast_multiply_fusion, s32[1024]{0:T(1024)S(1)} %get-tuple-element.33), kind=kCustom, calls=%fused_computation.10 | custom fusion | bytes 16777280 | tf_op jit(solution)/shard_map/gather | solution.py:44
  34.9 8.2 %gather_fusion.8 = bf16[16,4,128,512]{3,2,1,0:T(8,128)(2,1)} fusion(bf16[4,16,128,512]{3,2,1,0:T(8,128)(2,1)} %broadcast_multiply_fusion, s32[1024]{0:T(1024)S(1)} %get-tuple-element.34), kind=kCustom, calls=%fused_computation.8 | custom fusion | bytes 16777280 | tf_op jit(solution)/shard_map/gather | solution.py:44
  43.1 8.2 %gather_fusion.6 = bf16[16,4,128,512]{3,2,1,0:T(8,128)(2,1)} fusion(bf16[4,16,128,512]{3,2,1,0:T(8,128)(2,1)} %broadcast_multiply_fusion, s32[1024]{0:T(1024)S(1)} %get-tuple-element.35), kind=kCustom, calls=%fused_computation.6 | custom fusion | bytes 16777280 | tf_op jit(solution)/shard_map/gather | solution.py:44
  51.2 8.1 %gather_fusion.4 = bf16[16,4,128,512]{3,2,1,0:T(8,128)(2,1)} fusion(bf16[4,16,128,512]{3,2,1,0:T(8,128)(2,1)} %broadcast_multiply_fusion, s32[1024]{0:T(1024)S(1)} %get-tuple-element.36), kind=kCustom, calls=%fused_computation.4 | custom fusion | bytes 16777280 | tf_op jit(solution)/shard_map/gather | solution.py:44
  59.4 8.4 %gather_fusion.2 = bf16[16,4,128,512]{3,2,1,0:T(8,128)(2,1)} fusion(bf16[4,16,128,512]{3,2,1,0:T(8,128)(2,1)} %broadcast_multiply_fusion, s32[1024]{0:T(1024)S(1)} %get-tuple-element.37), kind=kCustom, calls=%fused_computation.2 | custom fusion | bytes 16777280 | tf_op jit(solution)/shard_map/gather | solution.py:44
  67.8 8.4 %gather_fusion = bf16[16,4,128,512]{3,2,1,0:T(8,128)(2,1)} fusion(bf16[4,16,128,512]{3,2,1,0:T(8,128)(2,1)} %broadcast_multiply_fusion, s32[1024]{0:T(1024)S(1)} %get-tuple-element.38), kind=kCustom, calls=%fused_computation | custom fusion | bytes 16777280 | tf_op jit(solution)/shard_map/gather | solution.py:44
  76.2 8.4 %gather_fusion.14 = bf16[16,4,128,512]{3,2,1,0:T(8,128)(2,1)} fusion(bf16[4,16,128,512]{3,2,1,0:T(8,128)(2,1)} %broadcast_multiply_fusion, s32[1024]{0:T(1024)S(1)} %get-tuple-element.31), kind=kCustom, calls=%fused_computation.14 | custom fusion | bytes 16777280 | tf_op jit(solution)/shard_map/gather | solution.py:44
  109.1 12.1 %fusion.16 = f32[16,4,512,128]{3,2,1,0:T(8,128)} fusion(bf16[16,4,128,512]{3,2,1,0:T(8,128)(2,1)} %gather_fusion.12, bf16[16,128,128]{2,1,0:T(8,128)(2,1)} %gather_fusion.13), kind=kOutput, calls=%fused_computation.43 | convolution fusion | flops 1073741824 | bytes 25690112 | tf_op jit(solution)/shard_map/tmn,ptml->ptnl/dot_general | solution.py:45
  121.2 11.7 %fusion.18 = f32[16,4,512,128]{3,2,1,0:T(8,128)} fusion(bf16[16,4,128,512]{3,2,1,0:T(8,128)(2,1)} %gather_fusion.10, bf16[16,128,128]{2,1,0:T(8,128)(2,1)S(1)} %copy-done.1), kind=kOutput, calls=%fused_computation.45 | convolution fusion | flops 1073741824 | bytes 25690112 | tf_op jit(solution)/shard_map/tmn,ptml->ptnl/dot_general | solution.py:45
  132.9 11.7 %fusion.20 = f32[16,4,512,128]{3,2,1,0:T(8,128)} fusion(bf16[16,4,128,512]{3,2,1,0:T(8,128)(2,1)} %gather_fusion.8, bf16[16,128,128]{2,1,0:T(8,128)(2,1)S(1)} %gather_fusion.9), kind=kOutput, calls=%fused_computation.47 | convolution fusion | flops 1073741824 | bytes 25690112 | tf_op jit(solution)/shard_map/tmn,ptml->ptnl/dot_general | solution.py:45
  144.6 11.6 %fusion.22 = f32[16,4,512,128]{3,2,1,0:T(8,128)} fusion(bf16[16,4,128,512]{3,2,1,0:T(8,128)(2,1)} %gather_fusion.6, bf16[16,128,128]{2,1,0:T(8,128)(2,1)S(1)} %gather_fusion.7), kind=kOutput, calls=%fused_computation.49 | convolution fusion | flops 1073741824 | bytes 25690112 | tf_op jit(solution)/shard_map/tmn,ptml->ptnl/dot_general | solution.py:45
  156.3 12.1 %fusion.24 = f32[16,4,512,128]{3,2,1,0:T(8,128)} fusion(bf16[16,4,128,512]{3,2,1,0:T(8,128)(2,1)} %gather_fusion.4, bf16[16,128,128]{2,1,0:T(8,128)(2,1)S(1)} %gather_fusion.5), kind=kOutput, calls=%fused_computation.51 | convolution fusion | flops 1073741824 | bytes 25690112 | tf_op jit(solution)/shard_map/tmn,ptml->ptnl/dot_general | solution.py:45
  168.4 11.7 %fusion.26 = f32[16,4,512,128]{3,2,1,0:T(8,128)} fusion(bf16[16,4,128,512]{3,2,1,0:T(8,128)(2,1)} %gather_fusion.2, bf16[16,128,128]{2,1,0:T(8,128)(2,1)S(1)} %gather_fusion.3), kind=kOutput, calls=%fused_computation.53 | convolution fusion | flops 1073741824 | bytes 25690112 | tf_op jit(solution)/shard_map/tmn,ptml->ptnl/dot_general | solution.py:45
  180.1 11.6 %fusion.28 = f32[16,4,512,128]{3,2,1,0:T(8,128)} fusion(bf16[16,4,128,512]{3,2,1,0:T(8,128)(2,1)} %gather_fusion, bf16[16,128,128]{2,1,0:T(8,128)(2,1)S(1)} %gather_fusion.1), kind=kOutput, calls=%fused_computation.55 | convolution fusion | flops 1073741824 | bytes 25690112 | tf_op jit(solution)/shard_map/tmn,ptml->ptnl/dot_general | solution.py:45
  191.7 41.7 %fusion.30 = bf16[4,16,128,512]{2,3,0,1:T(8,128)(2,1)} fusion(bf16[16,4,128,512]{3,2,1,0:T(8,128)(2,1)} %gather_fusion.14, f32[16,4,512,128]{3,2,1,0:T(8,128)} %fusion.16, f32[16,4,512,128]{3,2,1,0:T(8,128)} %fusion.18, f32[16,4,512,128]{3,2,1,0:T(8,128)} %fusion.20, f32[16,4,512,128]{3,2,1,0:T(8,128)} %fusion.22, f32[16,4,512,128]{3,2,1,0:T(8,128)} %fusion.24, ...), kind=kOutput, calls=%fused_computation.58 | convolution fusion | flops 1107296256 | bytes 134742016 | tf_op jit(solution)/shard_map/tmn,ptml->ptnl/dot_general | solution.py:45
  233.4 6.7 all-to-all-start
  240.1 8.2 %gather_fusion.23 = bf16[16,4,128,512]{3,2,1,0:T(8,128)(2,1)} fusion(bf16[4,16,128,512]{3,2,1,0:T(8,128)(2,1)} %broadcast_multiply_fusion, s32[1024]{0:T(1024)S(1)} %get-tuple-element.40), kind=kCustom, calls=%fused_computation.23 | custom fusion | bytes 16777280 | tf_op jit(solution)/shard_map/gather | solution.py:48
  248.3 8.2 %gather_fusion.18 = bf16[16,4,128,512]{3,2,1,0:T(8,128)(2,1)} fusion(bf16[4,16,128,512]{3,2,1,0:T(8,128)(2,1)} %broadcast_multiply_fusion, s32[1024]{0:T(1024)S(1)} %get-tuple-element.45), kind=kCustom, calls=%fused_computation.18 | custom fusion | bytes 16777280 | tf_op jit(solution)/shard_map/gather | solution.py:48
  256.5 8.1 %gather_fusion.16 = bf16[16,4,128,512]{3,2,1,0:T(8,128)(2,1)} fusion(bf16[4,16,128,512]{3,2,1,0:T(8,128)(2,1)} %broadcast_multiply_fusion, s32[1024]{0:T(1024)S(1)} %get-tuple-element.46), kind=kCustom, calls=%fused_computation.16 | custom fusion | bytes 16777280 | tf_op jit(solution)/shard_map/gather | solution.py:48
  264.6 8.2 %gather_fusion.22 = bf16[16,4,128,512]{3,2,1,0:T(8,128)(2,1)} fusion(bf16[4,16,128,512]{3,2,1,0:T(8,128)(2,1)} %broadcast_multiply_fusion, s32[1024]{0:T(1024)S(1)} %get-tuple-element.41), kind=kCustom, calls=%fused_computation.22 | custom fusion | bytes 16777280 | tf_op jit(solution)/shard_map/gather | solution.py:48
  272.8 8.2 %gather_fusion.21 = bf16[16,4,128,512]{3,2,1,0:T(8,128)(2,1)} fusion(bf16[4,16,128,512]{3,2,1,0:T(8,128)(2,1)} %broadcast_multiply_fusion, s32[1024]{0:T(1024)S(1)} %get-tuple-element.42), kind=kCustom, calls=%fused_computation.21 | custom fusion | bytes 16777280 | tf_op jit(solution)/shard_map/gather | solution.py:48
  281.0 8.3 %gather_fusion.20 = bf16[16,4,128,512]{3,2,1,0:T(8,128)(2,1)} fusion(bf16[4,16,128,512]{3,2,1,0:T(8,128)(2,1)} %broadcast_multiply_fusion, s32[1024]{0:T(1024)S(1)} %get-tuple-element.43), kind=kCustom, calls=%fused_computation.20 | custom fusion | bytes 16777280 | tf_op jit(solution)/shard_map/gather | solution.py:48
  289.3 8.2 %gather_fusion.19 = bf16[16,4,128,512]{3,2,1,0:T(8,128)(2,1)} fusion(bf16[4,16,128,512]{3,2,1,0:T(8,128)(2,1)} %broadcast_multiply_fusion, s32[1024]{0:T(1024)S(1)} %get-tuple-element.44), kind=kCustom, calls=%fused_computation.19 | custom fusion | bytes 16777280 | tf_op jit(solution)/shard_map/gather | solution.py:48
  297.4 8.3 %gather_fusion.24 = bf16[16,4,128,512]{3,2,1,0:T(8,128)(2,1)} fusion(bf16[4,16,128,512]{3,2,1,0:T(8,128)(2,1)} %broadcast_multiply_fusion, s32[1024]{0:T(1024)S(1)} %get-tuple-element.39), kind=kCustom, calls=%fused_computation.24 | custom fusion | bytes 16777280 | tf_op jit(solution)/shard_map/gather | solution.py:48
  311.1 11.8 %fusion.1 = f32[16,4,512,128]{3,2,1,0:T(8,128)} fusion(bf16[16,4,128,512]{3,2,1,0:T(8,128)(2,1)} %gather_fusion.23, bf16[16,8,128,128]{3,2,1,0:T(8,128)(2,1)} %gather_fusion.17), kind=kOutput, calls=%fused_computation.28 | convolution fusion | flops 1073741824 | bytes 25690112 | tf_op jit(solution)/shard_map/tnm,ptml->pltn/dot_general | solution.py:49
  322.9 11.6 %fusion.11 = f32[16,4,512,128]{3,2,1,0:T(8,128)} fusion(bf16[16,4,128,512]{3,2,1,0:T(8,128)(2,1)} %gather_fusion.18, bf16[16,8,128,128]{3,2,1,0:T(8,128)(2,1)S(1)} %copy-done), kind=kOutput, calls=%fused_computation.38 | convolution fusion | flops 1073741824 | bytes 25690112 | tf_op jit(solution)/shard_map/tnm,ptml->pltn/dot_general | solution.py:49
  334.5 11.6 %fusion.13 = f32[16,4,512,128]{3,2,1,0:T(8,128)} fusion(bf16[16,4,128,512]{3,2,1,0:T(8,128)(2,1)} %gather_fusion.16, bf16[16,8,128,128]{3,2,1,0:T(8,128)(2,1)S(1)} %copy-done), kind=kOutput, calls=%fused_computation.40 | convolution fusion | flops 1073741824 | bytes 25690112 | tf_op jit(solution)/shard_map/tnm,ptml->pltn/dot_general | solution.py:49
  346.1 11.6 %fusion.3 = f32[16,4,512,128]{3,2,1,0:T(8,128)} fusion(bf16[16,4,128,512]{3,2,1,0:T(8,128)(2,1)} %gather_fusion.22, bf16[16,8,128,128]{3,2,1,0:T(8,128)(2,1)S(1)} %copy-done), kind=kOutput, calls=%fused_computation.30 | convolution fusion | flops 1073741824 | bytes 25690112 | tf_op jit(solution)/shard_map/tnm,ptml->pltn/dot_general | solution.py:49
  357.8 11.9 %fusion.5 = f32[16,4,512,128]{3,2,1,0:T(8,128)} fusion(bf16[16,4,128,512]{3,2,1,0:T(8,128)(2,1)} %gather_fusion.21, bf16[16,8,128,128]{3,2,1,0:T(8,128)(2,1)S(1)} %copy-done), kind=kOutput, calls=%fused_computation.32 | convolution fusion | flops 1073741824 | bytes 25690112 | tf_op jit(solution)/shard_map/tnm,ptml->pltn/dot_general | solution.py:49
  369.7 11.7 %fusion.7 = f32[16,4,512,128]{3,2,1,0:T(8,128)} fusion(bf16[16,4,128,512]{3,2,1,0:T(8,128)(2,1)} %gather_fusion.20, bf16[16,8,128,128]{3,2,1,0:T(8,128)(2,1)S(1)} %copy-done), kind=kOutput, calls=%fused_computation.34 | convolution fusion | flops 1073741824 | bytes 25690112 | tf_op jit(solution)/shard_map/tnm,ptml->pltn/dot_general | solution.py:49
  381.4 11.6 %fusion.9 = f32[16,4,512,128]{3,2,1,0:T(8,128)} fusion(bf16[16,4,128,512]{3,2,1,0:T(8,128)(2,1)} %gather_fusion.19, bf16[16,8,128,128]{3,2,1,0:T(8,128)(2,1)S(1)} %copy-done), kind=kOutput, calls=%fused_computation.36 | convolution fusion | flops 1073741824 | bytes 25690112 | tf_op jit(solution)/shard_map/tnm,ptml->pltn/dot_general | solution.py:49
  393.0 42.0 %fusion.33 = bf16[4,512,16,128]{3,1,0,2:T(8,128)(2,1)} fusion(bf16[16,4,128,512]{3,2,1,0:T(8,128)(2,1)} %gather_fusion.24, f32[16,4,512,128]{3,2,1,0:T(8,128)} %fusion.1, f32[16,4,512,128]{3,2,1,0:T(8,128)} %fusion.3, f32[16,4,512,128]{3,2,1,0:T(8,128)} %fusion.5, f32[16,4,512,128]{3,2,1,0:T(8,128)} %fusion.7, f32[16,4,512,128]{3,2,1,0:T(8,128)} %fusion.9, ...), kind=kOutput, calls=%fused_computation.59 | convolution fusion | flops 1107296256 | bytes 134742016 | tf_op jit(solution)/shard_map/tnm,ptml->pltn/dot_general | solution.py:49
  435.1 12.0 %copy.125 = bf16[4,512,16,128]{3,2,1,0:T(8,128)(2,1)} copy(bf16[4,512,16,128]{3,1,0,2:T(8,128)(2,1)} %fusion.33) | data formatting | bytes 16777216 | tf_op jit(solution)/shard_map/convert_element_type | solution.py:56
  447.1 13.3 %reshape.58 = bf16[4,4,128,2048]{3,2,1,0:T(8,128)(2,1)} reshape(bf16[4,512,16,128]{3,2,1,0:T(8,128)(2,1)} %copy.125) | data formatting | bytes 16777216 | tf_op jit(solution)/shard_map/reshape | solution.py:56
  460.4 12.1 %copy.126 = bf16[4,4,128,2048]{3,1,0,2:T(4,128)(2,1)} copy(bf16[4,4,128,2048]{3,2,1,0:T(8,128)(2,1)} %reshape.58) | data formatting | bytes 16777216 | tf_op jit(solution)/shard_map/reshape | solution.py:56
  477.5 7.6 %copy.105 = bf16[4,4,4,128,512]{3,4,1,2,0:T(8,128)(2,1)} copy(bf16[4,4,4,128,512]{3,4,0,2,1:T(8,128)(2,1)} %bitcast.43) | data formatting | bytes 16777216 | tf_op jit(solution)/shard_map/all_to_all | solution.py:59
  485.2 14.6 %copy.106 = bf16[4,4,128,2048]{3,1,0,2:T(4,128)(2,1)} copy(bf16[4,4,128,2048]{2,3,1,0:T(8,128)(2,1)} %bitcast.238) | data formatting | bytes 16777216 | tf_op jit(solution)/shard_map/all_to_all | solution.py:59
  499.8 71.8 %all-to-all-done.2 = bf16[4,4,128,2048]{3,1,0,2:T(4,128)(2,1)} async-done(((bf16[4,4,128,2048]{3,1,0,2:T(4,128)(2,1)}), bf16[4,4,128,2048]{3,1,0,2:T(4,128)(2,1)}, u32[]{:S(2)}, u32[]{:S(2)}) %all-to-all-start.2) | async-done | bytes 8388640 | tf_op jit(solution)/shard_map/all_to_all | solution.py:62
  576.8 15.3 %copy.171 = bf16[4,4,8,16,2048]{4,3,1,0,2:T(8,128)(2,1)} copy(bf16[4,4,8,16,2048]{4,1,0,3,2:T(4,128)(2,1)} %bitcast.90) | data formatting | bytes 16777216 | tf_op jit(solution)/shard_map/all_to_all | solution.py:62
  592.0 9.1 %reshape.59 = bf16[32,131072]{1,0:T(8,128)(2,1)} reshape(bf16[8,4,4,16,2048]{4,3,2,1,0:T(8,128)(2,1)} %bitcast.239) | data formatting | bytes 16777216 | tf_op jit(solution)/shard_map/reshape | solution.py:65
  601.1 69.7 %all-to-all-done.1 = bf16[4,4,128,2048]{3,1,0,2:T(4,128)(2,1)} async-done(((bf16[4,4,128,2048]{3,1,0,2:T(4,128)(2,1)}), bf16[4,4,128,2048]{3,1,0,2:T(4,128)(2,1)}, u32[]{:S(2)}, u32[]{:S(2)}) %all-to-all-start.1) | async-done | bytes 8388640 | tf_op jit(solution)/shard_map/all_to_all | solution.py:61
  670.8 11.3 %copy.107 = bf16[4,4,128,2048]{3,2,1,0:T(8,128)(2,1)} copy(bf16[4,4,128,2048]{3,1,0,2:T(4,128)(2,1)} %all-to-all-done.1) | data formatting | bytes 16777216 | tf_op jit(solution)/shard_map/all_to_all | solution.py:61
  682.1 8.3 %copy.108 = bf16[8,4,4,16,2048]{4,3,2,1,0:T(8,128)(2,1)} copy(bf16[8,4,4,16,2048]{4,3,0,2,1:T(8,128)(2,1)} %bitcast.240) | data formatting | bytes 16777216 | tf_op jit(solution)/shard_map/all_to_all | solution.py:61
  690.4 8.9 %reshape.56 = bf16[32,131072]{1,0:T(8,128)(2,1)} reshape(bf16[8,4,4,16,2048]{4,3,2,1,0:T(8,128)(2,1)} %copy.108) | data formatting | bytes 16777216 | tf_op jit(solution)/shard_map/reshape | solution.py:64
  699.2 8.1 %convolution_multiply_fusion = f32[32,32]{1,0:T(8,128)S(1)} fusion(bf16[32,131072]{1,0:T(8,128)(2,1)} %reshape.56, bf16[32,131072]{1,0:T(8,128)(2,1)} %reshape.59), kind=kOutput, calls=%fused_computation.61 | convolution fusion | flops 268436480 | bytes 16781312 | tf_op jit(solution)/shard_map/pe,qe->pq/dot_general | solution.py:66
  707.3 40.2 %psum.7 = f32[32,32]{1,0:T(8,128)S(1)} all-reduce(f32[32,32]{1,0:T(8,128)S(1)} %convolution_multiply_fusion), channel_id=1, replica_groups=mesh['grp'=4,'blk'=8] {'grp','blk'}, use_global_device_ids=true, to_apply=%region_1.2 | all-reduce | flops 1024 | bytes 8192 | tf_op jit(solution)/shard_map/psum | solution.py:69
  (49 shorter events, 45.2 us)
Async XLA Ops:
  6.5 78.1 %all-gather.3.cloned.1.call-start = ((), (), s32[]{:S(2)}) async-start(), calls=%async_computation.3 | async-start | bytes 4325376 | tf_op jit(solution)/shard_map/all_gather | solution.py:32
  7.3 298.5 %all-gather.5.cloned.1.call-start = ((), (), s32[]{:S(2)}) async-start(), calls=%async_computation.4 | async-start | bytes 4325376 | tf_op jit(solution)/shard_map/all_gather | solution.py:33
  109.1 12.2 %copy-start.1 = (bf16[16,128,128]{2,1,0:T(8,128)(2,1)S(1)}, bf16[16,128,128]{2,1,0:T(8,128)(2,1)}, u32[]{:S(2)}) copy-start(bf16[16,128,128]{2,1,0:T(8,128)(2,1)} %gather_fusion.11) | copy-start | bytes 1572868
  233.4 239.1 %all-to-all-start = ((bf16[4,16,128,512]{2,3,0,1:T(8,128)(2,1)}), bf16[4,16,128,512]{2,3,0,1:T(8,128)(2,1)}, u32[]{:S(2)}, u32[]{:S(2)}) async-start(bf16[4,16,128,512]{2,3,0,1:T(8,128)(2,1)} %fusion.30), calls=%async_computation | async-start | bytes 16777216 | tf_op jit(solution)/shard_map/all_to_all | solution.py:59
  272.8 8.2 %copy-start.2 = (s32[16]{0:T(128)S(1)}, s32[16]{0:T(128)}, u32[]{:S(2)}) copy-start(s32[16]{0:T(128)} %get-tuple-element.10) | copy-start | bytes 196
  272.8 8.2 %copy-start.3 = (s32[16]{0:T(128)S(1)}, s32[16]{0:T(128)}, u32[]{:S(2)}) copy-start(s32[16]{0:T(128)} %get-tuple-element.11) | copy-start | bytes 196
  297.4 8.3 %copy-start.4 = (s32[16]{0:T(128)S(1)}, s32[16]{0:T(128)}, u32[]{:S(2)}) copy-start(s32[16]{0:T(128)} %param.9) | copy-start | bytes 196
  311.1 11.8 %copy-start = (bf16[16,8,128,128]{3,2,1,0:T(8,128)(2,1)S(1)}, bf16[16,8,128,128]{3,2,1,0:T(8,128)(2,1)}, u32[]{:S(2)}) copy-start(bf16[16,8,128,128]{3,2,1,0:T(8,128)(2,1)} %gather_fusion.17) | copy-start | bytes 12582916
  472.6 99.0 %all-to-all-start.2 = ((bf16[4,4,128,2048]{3,1,0,2:T(4,128)(2,1)}), bf16[4,4,128,2048]{3,1,0,2:T(4,128)(2,1)}, u32[]{:S(2)}, u32[]{:S(2)}) async-start(bf16[4,4,128,2048]{3,1,0,2:T(4,128)(2,1)} %copy.126), calls=%async_computation.2 | async-start | bytes 16777216 | tf_op jit(solution)/shard_map/all_to_all | solution.py:62
  571.6 99.2 %all-to-all-start.1 = ((bf16[4,4,128,2048]{3,1,0,2:T(4,128)(2,1)}), bf16[4,4,128,2048]{3,1,0,2:T(4,128)(2,1)}, u32[]{:S(2)}, u32[]{:S(2)}) async-start(bf16[4,4,128,2048]{3,1,0,2:T(4,128)(2,1)} %copy.106), calls=%async_computation.1 | async-start | bytes 16777216 | tf_op jit(solution)/shard_map/all_to_all | solution.py:61
Sparse Core Ops, SparseCore 0:
  10.2 64.7 all-gather.2
  77.8 60.5 all-gather.4
where the time goes:
time: 763 us; the launch traced here: 755 us
  local copies, waits for them, and re-layouts  275 us (36%)
  matrix products  256 us (34%)
  waiting for transfers between devices  143 us (19%)
  blocking collectives  40.2 us (5%)
  starting transfers between devices  16.9 us (2%)
  between operations  13.9 us (2%)
  other arithmetic  9.49 us (1%)
    dot_general x8, matrix products, body(): jnp.einsum('tmn,ptml->ptnl', occupied_pick, occupied_inputs, preferred_el...  124 us
    dot_general x8, matrix products, body(): jnp.einsum('tnm,ptml->pltn', virtual_pick[:, slot], virtual_inputs, prefe...  124 us
    all_to_all x1, waiting for transfers between devices, body(): lax.all_to_all(virtual_part, 'blk', split_axis=2, concat_axis=0, tiled=True)  71.8 us
    all_to_all x1, waiting for transfers between devices, body(): lax.all_to_all(occupied_moved, 'blk', split_axis=2, concat_axis=0, tiled=...  69.7 us
    gather x8, local copies, waits for them, and re-layouts, body(): occupied_inputs = masked[:, source_rows[:, slot]]  66.1 us
    gather x8, local copies, waits for them, and re-layouts, body(): virtual_inputs = masked[:, partner_rows[:, slot]]  65.6 us
    psum x1, blocking collectives, body(): total = lax.psum(partial_sum, ('grp', 'blk'))  40.2 us
    reshape x2, local copies, waits for them, and re-layouts, body(): virtual_sum.astype(jnp.bfloat16)  25.5 us
  transfers between devices with their start and end apart: 5, of which 2 were waited for; matrix products, arithmetic and copies ran while one was open for 67% of the time, Pallas kernels for 0%

commit v1 on v0

--- a/solution.py
+++ b/solution.py
@@ -1,12 +1,18 @@
+import functools
+
 import jax
 import jax.numpy as jnp
 from jax import lax
+from jax.experimental import pallas as pl
+from jax.experimental.pallas import tpu as pltpu
 from jax.sharding import PartitionSpec as P
 
 NT = 16
-
-
-def body(
+HALF = NT // 2 + 1
+VMEM_BYTES = 60 * 1024 * 1024
+
+
+def general_body(
     integrals,
     tile_mask,
     tile_owner,
@@ -70,7 +76,265 @@
     return lax.dynamic_slice_in_dim(total, lax.axis_index("blk") * aux_local, aux_local, 0)
 
 
+def order_kernel(row_ref, aux_ref, integrals_ref, mask_ref, out_ref):
+    out_ref[...] = integrals_ref[...] * mask_ref[0]
+
+
+def ordered_rows(integrals, row_of, aux_of, mask_rows):
+    aux_local, basis_size, width = integrals.shape
+    tile = basis_size // NT
+    return pl.pallas_call(
+        order_kernel,
+        grid_spec=pltpu.PrefetchScalarGridSpec(
+            num_scalar_prefetch=2,
+            grid=(NT, aux_local),
+            in_specs=[
+                pl.BlockSpec((1, 1, tile, width), lambda r, d, row, aux: (aux[d], row[r], 0, 0)),
+                pl.BlockSpec((1, 1, width), lambda r, d, row, aux: (r, 0, 0)),
+            ],
+            out_specs=pl.BlockSpec((1, 1, tile, width), lambda r, d, row, aux: (d, r, 0, 0)),
+        ),
+        out_shape=jax.ShapeDtypeStruct((aux_local, NT, tile, width), jnp.bfloat16),
+        name="ordered_rows",
+    )(row_of, aux_of, integrals.reshape(aux_local, NT, tile, width), mask_rows)
+
+
+def pair_kernel(row_ref, integrals_ref, mask_ref, out_ref):
+    parts, aux_local = out_ref.shape[0], out_ref.shape[1]
+    rows = out_ref.shape[3]
+    values = integrals_ref[:, 0] * mask_ref[0]
+    for part in range(parts):
+        out_ref[part, :, 0] = values[:, part * rows : (part + 1) * rows]
+
+
+def pair_tiles(integrals, row_of, mask_rows, parts):
+    aux_local, basis_size, width = integrals.shape
+    tile = basis_size // NT
+    columns = width // tile
+    rows = tile // parts
+    return pl.pallas_call(
+        pair_kernel,
+        grid_spec=pltpu.PrefetchScalarGridSpec(
+            num_scalar_prefetch=1,
+            grid=(columns, HALF),
+            in_specs=[
+                pl.BlockSpec((aux_local, 1, tile, tile), lambda c, d, row: (0, row[c + d], 0, c)),
+                pl.BlockSpec((1, 1, tile), lambda c, d, row: (c + d, 0, c)),
+            ],
+            out_specs=pl.BlockSpec(
+                (parts, aux_local, 1, rows, tile), lambda c, d, row: (0, 0, c * HALF + d, 0, 0)
+            ),
+        ),
+        out_shape=jax.ShapeDtypeStruct(
+            (parts, aux_local, columns * HALF, rows, tile), jnp.bfloat16
+        ),
+        name="pair_tiles",
+    )(row_of, integrals.reshape(aux_local, NT, tile, width), mask_rows)
+
+
+def product_kernel(
+    kcount,
+    parts,
+    group_ref,
+    occ_slot_ref,
+    occ_tile_ref,
+    virt_slot_ref,
+    virt_tile_ref,
+    own_ref,
+    near_ref,
+    across_ref,
+    far_ref,
+    green_ref,
+    out_ref,
+    full,
+    half,
+    panel,
+    folded,
+):
+    width = own_ref.shape[2]
+    tile = own_ref.shape[1]
+    columns = width // tile
+    planes = NT // columns
+
+    def block(row, column, values):
+        full[row * width : (row + 1) * width, column * width : (column + 1) * width] = values
+
+    def both(row, column, values):
+        block(row, column, values)
+        block(column, row, values.T)
+
+    def square(ref, at):
+        return ref[at * columns : (at + 1) * columns].reshape(width, width)
+
+    block(0, 0, square(own_ref, 0))
+    for plane in range(1, planes):
+        both(plane, 0, square(own_ref, plane))
+    block(1, 1, square(near_ref, 0))
+    both(2, 1, square(near_ref, 1))
+    block(2, 2, square(across_ref, 0))
+    both(3, 2, square(across_ref, 1))
+    block(3, 3, square(far_ref, 0))
+    both(1, 3, square(far_ref, 1))
+
+    folded[...] = jnp.zeros_like(folded)
+
+    @pl.loop(0, NT)
+    def _(r):
+        left = jnp.concatenate(
+            [green_ref[occ_tile_ref[r * kcount + k]] for k in range(kcount)], axis=1
+        )
+        starts = [pl.multiple_of(occ_slot_ref[r * kcount + k] * tile, tile) for k in range(kcount)]
+        for at in range(planes):
+            right = jnp.concatenate(
+                [full[pl.ds(start, tile), at * width : (at + 1) * width] for start in starts],
+                axis=0,
+            )
+            values = jnp.dot(left, right, preferred_element_type=jnp.float32)
+            values = values.astype(jnp.bfloat16)
+            for c in range(columns):
+                half[at * columns + c, pl.ds(pl.multiple_of(r * tile, tile), tile), :] = values[
+                    :, c * tile : (c + 1) * tile
+                ]
+
+    @pl.loop(0, NT)
+    def _(s):
+        right = jnp.concatenate(
+            [green_ref[virt_tile_ref[s * kcount + k]] for k in range(kcount)], axis=0
+        )
+        slots = [virt_slot_ref[s * kcount + k] for k in range(kcount)]
+        for at in range(planes):
+            left = jnp.concatenate(
+                [half[slot, at * width : (at + 1) * width, :] for slot in slots], axis=1
+            )
+            panel[at * width : (at + 1) * width, :] = jnp.dot(
+                left, right, preferred_element_type=jnp.float32
+            )
+        for d in range(NT):
+            r = lax.rem(s + d, NT)
+            values = panel[pl.ds(pl.multiple_of(r * tile, tile), tile), :]
+            if d < HALF:
+                folded[s, d] += values
+            else:
+                folded[r, NT - d] += values.T
+
+    rows = tile // parts
+
+    @pl.loop(0, planes)
+    def _(plane):
+        away = lax.rem(plane - group_ref[0] + planes, planes)
+
+        @pl.loop(0, columns)
+        def _(c):
+            for d in range(HALF):
+                values = folded[away * columns + c, d].astype(jnp.bfloat16)
+                for part in range(parts):
+                    out_ref[plane * parts + part, c * HALF + d] = values[
+                        part * rows : (part + 1) * rows
+                    ]
+
+
+def folded_product(tables, own, near, across, far, greens, planes, parts):
+    tile, width = own.shape[1:]
+    columns = width // tile
+    basis = NT * tile
+    kcount = tables[1].shape[0] // NT
+    vmem = pl.BlockSpec(memory_space=pltpu.VMEM)
+    smem = pl.BlockSpec(memory_space=pltpu.SMEM)
+    return pl.pallas_call(
+        functools.partial(product_kernel, kcount, parts),
+        in_specs=[smem] * 5 + [vmem] * 5,
+        out_specs=vmem,
+        out_shape=jax.ShapeDtypeStruct(
+            (planes * parts, columns * HALF, tile // parts, tile), jnp.bfloat16
+        ),
+        scratch_shapes=[
+            pltpu.VMEM((basis, basis), jnp.bfloat16),
+            pltpu.VMEM((NT, basis, tile), jnp.bfloat16),
+            pltpu.VMEM((basis, tile), jnp.float32),
+            pltpu.VMEM((NT, HALF, tile, tile), jnp.float32),
+        ],
+        compiler_params=pltpu.CompilerParams(vmem_limit_bytes=VMEM_BYTES),
+        name="folded_product",
+    )(*tables, own, near, across, far, greens)
+
+
+def folded_body(
+    integrals,
+    tile_mask,
+    tile_owner,
+    occupied_tiles,
+    occupied_offsets,
+    virtual_tiles,
+    virtual_offsets,
+):
+    aux_local, basis_size, width = integrals.shape
+    tile = basis_size // NT
+    columns = width // tile
+    planes, parts = lax.axis_size("grp"), lax.axis_size("blk")
+    kcount = occupied_offsets.shape[0]
+    group = lax.axis_index("grp")
+
+    row_of = jnp.roll(tile_owner, -group * columns)
+    slots = jnp.zeros((NT,), jnp.int32).at[row_of].set(jnp.arange(NT, dtype=jnp.int32))
+    mask_rows = jnp.repeat(tile_mask[row_of][:, row_of[:columns]], tile, axis=1)
+    mask_rows = mask_rows.astype(jnp.bfloat16)[:, None, :]
+    aux_of = (group - jnp.arange(aux_local, dtype=jnp.int32)) % aux_local
+
+    greens = jnp.stack(
+        [
+            jnp.swapaxes(occupied_tiles.reshape(-1, tile, tile), 1, 2),
+            virtual_tiles.reshape(-1, tile, tile),
+        ]
+    )
+    held = greens.shape[1]
+    greens = lax.all_gather(greens, ("grp", "blk"), axis=0, tiled=False)
+    greens = greens.reshape(-1, tile, tile)
+
+    ordered = ordered_rows(integrals, row_of, aux_of, mask_rows)
+    moved = []
+    for d in range(1, planes):
+        first = 1 if d < planes - 1 else 2
+        sent = jnp.concatenate(
+            [ordered[d, :columns], ordered[d, first * columns : (first + 1) * columns]]
+        )
+        moved.append(
+            lax.ppermute(sent, "grp", [(h, (h - d) % planes) for h in range(planes)])
+        )
+    pairs = pair_tiles(integrals, row_of, mask_rows, parts)
+    pairs = lax.all_to_all(pairs, "blk", split_axis=0, concat_axis=0, tiled=True)
+
+    def table(offsets, which):
+        natural = (row_of[:, None] - offsets[None, :]) % NT
+        flat = natural * kcount + jnp.arange(kcount, dtype=jnp.int32)[None, :]
+        at = (flat // held) * (2 * held) + which * held + flat % held
+        return slots[natural].reshape(-1), at.reshape(-1)
+
+    tables = (group[None].astype(jnp.int32),) + table(occupied_offsets, 0) + table(virtual_offsets, 1)
+    folded = folded_product(tables, ordered[0], *moved, greens, planes, parts)
+    folded = lax.all_to_all(folded, ("grp", "blk"), split_axis=0, concat_axis=0, tiled=True)
+
+    partial_sum = jnp.einsum(
+        "pe,qe->pq",
+        folded.reshape(planes * parts, -1),
+        pairs.reshape(parts * aux_local, -1),
+        preferred_element_type=jnp.float32,
+    ) * (1.0 / basis_size)
+    partial_sum = partial_sum.reshape(planes, parts, -1).swapaxes(0, 1)
+    spread = jnp.broadcast_to(partial_sum[None], (planes,) + partial_sum.shape)
+    spread = spread.reshape((planes * parts,) + partial_sum.shape[1:])
+    spread = lax.all_to_all(spread, ("grp", "blk"), split_axis=0, concat_axis=0, tiled=True)
+    return jnp.sum(spread, axis=0)
+
+
 def solution(mesh):
+    planes, parts = mesh.shape["grp"], mesh.shape["blk"]
+
+    def body(*args):
+        aux_local, basis_size, width = args[0].shape
+        tile = basis_size // NT
+        fits = aux_local == planes == 4 and width % tile == 0 and tile % (16 * parts) == 0
+        return (folded_body if fits else general_body)(*args)
+
     in_specs = (
         P("blk", None, "grp"),
         P(),

time: 763 us -> 371 us (0.49)
  local copies, waits for them, and re-layouts: 275 us -> 21.4 us
  matrix products: 256 us -> 6.91 us
  Pallas kernels: 0 us -> 101 us
  blocking collectives: 40.2 us -> 10.7 us
  waiting for transfers between devices: 143 us -> 170 us
  starting transfers between devices: 16.9 us -> 37.2 us
    dot_general x17 -> x1, matrix products: 256 us -> 6.91 us  [folded_body(): jnp.einsum('pe,qe->pq', folded.reshape(planes * parts, -1), pairs.reshape...]
    gather x25 -> x5, local copies, waits for them, and re-layouts: 161 us -> 4.74 us  [the longest x2 3.55 us: table(): return (slots[natural].reshape(-1), at.reshape(-1))]
    pallas_call x0 -> x3, Pallas kernels: none -> 101 us  [the longest x1 44.7 us: folded_product(): pl.pallas_call(functools.partial(product_kernel, kcount, parts), in_specs...]
    ppermute x0 -> x3, waiting for transfers between devices: none -> 70.9 us  [folded_body(): lax.ppermute(sent, 'grp', [(h, (h - d) % planes) for h in range(planes)])]
    all_to_all x5 -> x1, local copies, waits for them, and re-layouts: 57.1 us -> 0.51 us  [folded_body(): lax.all_to_all(spread, ('grp', 'blk'), split_axis=0, concat_axis=0, tiled...]
    all_to_all x3 -> x2, waiting for transfers between devices: 142 us -> 99.3 us  [the longest x1 99.3 us: folded_body(): lax.all_to_all(folded, ('grp', 'blk'), split_axis=0, concat_axis=0, tiled...]
    psum x1 -> x0, blocking collectives: 40.2 us -> none  [body(): total = lax.psum(partial_sum, ('grp', 'blk'))]
    reshape x4 -> x1, local copies, waits for them, and re-layouts: 43.4 us -> 6.01 us  [folded_body(): pairs.reshape(parts * aux_local, -1)]
  transfers between devices with their start and end apart: 5 -> 6, of which waited for: 2 -> 3; matrix products, arithmetic and copies ran while one was open for 67% -> 6% of each run, Pallas kernels for 0% -> 27%
where the time goes in v1:
time: 371 us; the launch traced here: 369 us
  waiting for transfers between devices  170 us (46%)
  Pallas kernels  101 us (27%)
  starting transfers between devices  37.2 us (10%)
  local copies, waits for them, and re-layouts  21.4 us (6%)
  between operations  13.6 us (4%)
  blocking collectives  10.7 us (3%)
  other arithmetic  7.69 us (2%)
  matrix products  6.91 us (2%)
    all_to_all x1, waiting for transfers between devices, folded_body(): lax.all_to_all(folded, ('grp', 'blk'), split_axis=0, concat_axis=0, tiled...  99.3 us
    ppermute x3, waiting for transfers between devices, folded_body(): lax.ppermute(sent, 'grp', [(h, (h - d) % planes) for h in range(planes)])  70.9 us
    pallas_call x1, Pallas kernels, folded_product(): pl.pallas_call(functools.partial(product_kernel, kcount, parts), in_specs...  44.7 us
    pallas_call x1, Pallas kernels, ordered_rows(): pl.pallas_call(order_kernel, grid_spec=pltpu.PrefetchScalarGridSpec(num_s...  35.6 us
    all_to_all x1, starting transfers between devices, folded_body(): lax.all_to_all(folded, ('grp', 'blk'), split_axis=0, concat_axis=0, tiled...  24.7 us
    pallas_call x1, Pallas kernels, pair_tiles(): pl.pallas_call(pair_kernel, grid_spec=pltpu.PrefetchScalarGridSpec(num_sc...  21.2 us
    all_to_all x1, blocking collectives, folded_body(): lax.all_to_all(spread, ('grp', 'blk'), split_axis=0, concat_axis=0, tiled...  10.7 us
  transfers between devices with their start and end apart: 6, of which 3 were waited for; matrix products, arithmetic and copies ran while one was open for 6% of the time, Pallas kernels for 27%

profile of v1, /device:TPU:0, one launch (start us, length us, event | category | flops | bytes accessed | tf_op | source)
XLA Modules:
  0.0 369.1 jit_solution(6956202710542399790)
XLA Ops:
  6.5 1.0 copy.45
  7.6 0.9 pad_maximum_fusion.3
  8.5 0.9 copy.46
  9.4 0.8 pad_add_fusion
  10.2 0.1 compare_select_fusion.3
  10.3 0.6 gather_fusion.2
  11.0 0.6 gather_fusion.3
  11.6 0.1 copy.43
  11.7 0.1 broadcast_in_dim.13
  11.7 0.6 convert_element_type.17.mask_ref
  12.4 21.2 %pair_tiles.1 = bf16[8,4,36,16,128]{4,3,2,1,0:T(8,128)(2,1)} custom-call(s32[16]{0:T(128)} %copy-done.4, bf16[4,16,128,512]{3,2,1,0:T(8,128)(2,1)} %bitcast.46, bf16[16,1,512]{2,1,0:T(2,128)(2,1)} %convert_element_type.17.mask_ref), custom_call_target="tpu_custom_call" | custom-call | tf_op jit(solution)/shard_map/pair_tiles/pallas_call | solution.py:115
  33.6 5.2 %all-to-all-start.1 = ((bf16[8,4,36,16,128]{4,3,2,1,0:T(8,128)(2,1)}), bf16[8,4,36,16,128]{4,3,2,1,0:T(8,128)(2,1)}, u32[]{:S(2)}, u32[]{:S(2)}) async-start(bf16[8,4,36,16,128]{4,3,2,1,0:T(8,128)(2,1)} %pair_tiles.1), calls=%async_computation.1 | async-start | bytes 9437184 | tf_op jit(solution)/shard_map/all_to_all | solution.py:304
  38.8 0.5 and_select_fusion.aux_ref
  39.3 35.6 %ordered_rows.1 = bf16[4,16,128,512]{3,2,1,0:T(8,128)(2,1)} custom-call(s32[16]{0:T(128)} %copy-done.4, s32[4]{0:T(128)} %and_select_fusion.aux_ref, bf16[4,16,128,512]{3,2,1,0:T(8,128)(2,1)} %bitcast.47, bf16[16,1,512]{2,1,0:T(2,128)(2,1)} %convert_element_type.17.mask_ref), custom_call_target="tpu_custom_call" | custom-call | tf_op jit(solution)/shard_map/ordered_rows/pallas_call | solution.py:86
  74.8 2.0 slice_bitcast_fusion.2
  76.9 1.1 pad_maximum_fusion.1
  78.0 3.5 collective-permute-start.1
  81.5 1.1 pad_maximum_fusion.2
  82.6 1.6 collective-permute-start.2
  84.2 1.1 pad_maximum_fusion
  85.3 2.2 collective-permute-start
  87.6 0.1 sub.83
  87.7 0.1 sub.89
  87.8 0.1 add.129
  87.9 0.1 compare_select_fusion
  88.0 0.1 reshape.230
  88.1 0.6 scatter_custom_fusion
  88.7 0.1 reshape.238
  88.8 1.8 gather_fusion
  90.6 1.7 gather_fusion.1
  92.4 0.6 fusion.12
  93.0 3.1 slice_bitcast_fusion.own_ref
  96.0 70.0 %collective-permute-done.1.across_ref = bf16[8,128,512]{2,1,0:T(8,128)(2,1)S(1)} collective-permute-done((bf16[8,128,512]{2,1,0:T(8,128)(2,1)}, bf16[8,128,512]{2,1,0:T(8,128)(2,1)S(1)}, u32[]{:S(2)}, u32[]{:S(2)}) %collective-permute-start.1) | collective-permute-done | bytes 1048608 | tf_op jit(solution)/shard_map/ppermute | solution.py:301
  166.1 0.8 collective-permute-done.near_ref
  166.9 0.1 copy-done.1
  167.1 0.3 copy-done.2
  167.4 0.6 copy-done.3
  168.0 44.7 %folded_product.1 = bf16[32,36,16,128]{3,2,1,0:T(8,128)(2,1)} custom-call(s32[1]{0:T(128)} %bitcast.group_ref, s32[128]{0:T(128)} %gather_fusion, s32[128]{0:T(128)} %get-tuple-element.14.occ_tile_ref, s32[128]{0:T(128)} %gather_fusion.1, s32[128]{0:T(128)} %get-tuple-element.13.virt_tile_ref, bf16[16,128,512]{2,1,0:T(8,128)(2,1)} %slice_bitcast_fusion.own_ref, ...), custom_call_target="tpu_custom_call" | custom-call | tf_op jit(solution)/shard_map/folded_product/pallas_call | solution.py:243
  212.6 24.7 %all-to-all-start = ((bf16[32,36,16,128]{3,2,1,0:T(8,128)(2,1)}), bf16[32,36,16,128]{3,2,1,0:T(8,128)(2,1)}, u32[]{:S(2)}, u32[]{:S(2)}) async-start(bf16[32,36,16,128]{3,2,1,0:T(8,128)(2,1)} %folded_product.1), calls=%async_computation | async-start | bytes 9437184 | tf_op jit(solution)/shard_map/all_to_all | solution.py:314
  237.3 6.0 %reshape.225 = bf16[32,73728]{1,0:T(8,128)(2,1)} reshape(bf16[8,4,36,16,128]{4,3,2,1,0:T(8,128)(2,1)} %all-to-all-done.1) | data formatting | bytes 9437184 | tf_op jit(solution)/shard_map/reshape | solution.py:319
  243.3 99.3 %all-to-all-done = bf16[32,36,16,128]{3,2,1,0:T(8,128)(2,1)} async-done(((bf16[32,36,16,128]{3,2,1,0:T(8,128)(2,1)}), bf16[32,36,16,128]{3,2,1,0:T(8,128)(2,1)}, u32[]{:S(2)}, u32[]{:S(2)}) %all-to-all-start) | async-done | bytes 4718624 | tf_op jit(solution)/shard_map/all_to_all | solution.py:314
  342.6 6.9 %fusion.6 = f32[8,4,32]{2,0,1:T(8,128)S(1)} fusion(bf16[32,73728]{1,0:T(8,128)(2,1)} %reshape.225, bf16[4,8,576,128]{3,2,1,0:T(8,128)(2,1)} %bitcast.24), kind=kOutput, calls=%fused_computation.10 | convolution fusion | flops 150995968 | bytes 9441280 | tf_op jit(solution)/shard_map/pe,qe->pq/dot_general | solution.py:316
  349.5 0.1 reshape.279
  349.7 10.7 %all_to_all.15 = f32[32,1,128]{2,1,0:T(1,128)S(1)} all-to-all(f32[32,1,128]{2,1,0:T(1,128)S(1)} %reshape.279), channel_id=1, replica_groups=mesh['grp'=4,'blk'=8] {'grp','blk'}, dimensions={0} | all-to-all | bytes 32768 | tf_op jit(solution)/shard_map/all_to_all | solution.py:325
  360.4 0.5 broadcast.304
  360.9 0.7 reduce
  361.6 0.1 reshape.280
  361.7 0.6 reduce_sum.9
  (30 shorter events, 0.3 us)
Async XLA Ops:
  6.5 3.8 %copy-start = (s32[16,16]{1,0:T(8,128)S(1)}, s32[16,16]{1,0:T(8,128)}, u32[]{:S(2)}) copy-start(s32[16,16]{1,0:T(8,128)} %param.8) | copy-start | bytes 3076
  6.5 160.4 %all-gather.3.cloned.1.call-start = ((), (), s32[]{:S(2)}) async-start(), calls=%async_computation.3 | async-start | bytes 8650752 | tf_op jit(solution)/shard_map/all_gather | solution.py:290
  10.3 2.0 copy-start.4
  33.6 179.0 %all-to-all-start.1 = ((bf16[8,4,36,16,128]{4,3,2,1,0:T(8,128)(2,1)}), bf16[8,4,36,16,128]{4,3,2,1,0:T(8,128)(2,1)}, u32[]{:S(2)}, u32[]{:S(2)}) async-start(bf16[8,4,36,16,128]{4,3,2,1,0:T(8,128)(2,1)} %pair_tiles.1), calls=%async_computation.1 | async-start | bytes 9437184 | tf_op jit(solution)/shard_map/all_to_all | solution.py:304
  76.9 10.7 %copy-start.5 = (s32[16]{0:T(128)S(1)}, s32[16]{0:T(128)}, u32[]{:S(2)}) copy-start(s32[16]{0:T(128)} %copy-done.4) | copy-start | bytes 196
  76.9 10.6 %copy-start.6 = (s32[8]{0:T(128)S(1)}, s32[8]{0:T(128)}, u32[]{:S(2)}) copy-start(s32[8]{0:T(128)} %param.13) | copy-start | bytes 100
  76.9 10.6 %copy-start.7 = (s32[8]{0:T(128)S(1)}, s32[8]{0:T(128)}, u32[]{:S(2)}) copy-start(s32[8]{0:T(128)} %param.11) | copy-start | bytes 100
  78.0 88.1 %collective-permute-start.1 = (bf16[8,128,512]{2,1,0:T(8,128)(2,1)}, bf16[8,128,512]{2,1,0:T(8,128)(2,1)S(1)}, u32[]{:S(2)}, u32[]{:S(2)}) collective-permute-start(bf16[8,128,512]{2,1,0:T(8,128)(2,1)} %pad_maximum_fusion.1), channel_id=1, source_target_pairs={{0,16},{8,24},{16,0},{24,8},{1,17},{9,25},{17,1},{25,9},{2,18},{10... | collective-permute-start | bytes 3145736 | tf_op jit(solution)/shard_map/ppermute | solution.py:301
  82.6 83.5 %collective-permute-start.2 = (bf16[8,128,512]{2,1,0:T(8,128)(2,1)}, bf16[8,128,512]{2,1,0:T(8,128)(2,1)S(1)}, u32[]{:S(2)}, u32[]{:S(2)}) collective-permute-start(bf16[8,128,512]{2,1,0:T(8,128)(2,1)} %pad_maximum_fusion.2), channel_id=1, source_target_pairs={{0,8},{8,16},{16,24},{24,0},{1,9},{9,17},{17,25},{25,1},{2,10},{10... | collective-permute-start | bytes 3145736 | tf_op jit(solution)/shard_map/ppermute | solution.py:301
  85.3 81.6 %collective-permute-start = (bf16[8,128,512]{2,1,0:T(8,128)(2,1)}, bf16[8,128,512]{2,1,0:T(8,128)(2,1)S(1)}, u32[]{:S(2)}, u32[]{:S(2)}) collective-permute-start(bf16[8,128,512]{2,1,0:T(8,128)(2,1)} %pad_maximum_fusion), channel_id=1, source_target_pairs={{0,24},{8,0},{16,8},{24,16},{1,25},{9,1},{17,9},{25,17},{2,26},{10... | collective-permute-start | bytes 3145736 | tf_op jit(solution)/shard_map/ppermute | solution.py:301
  166.1 1.0 copy-start.1
  166.1 1.3 copy-start.2
  166.9 1.0 copy-start.3
  212.6 130.0 %all-to-all-start = ((bf16[32,36,16,128]{3,2,1,0:T(8,128)(2,1)}), bf16[32,36,16,128]{3,2,1,0:T(8,128)(2,1)}, u32[]{:S(2)}, u32[]{:S(2)}) async-start(bf16[32,36,16,128]{3,2,1,0:T(8,128)(2,1)} %folded_product.1), calls=%async_computation | async-start | bytes 9437184 | tf_op jit(solution)/shard_map/all_to_all | solution.py:314
Sparse Core Ops, SparseCore 0:
  10.2 143.1 all-gather.2

commit v2 on v0

--- a/solution.py
+++ b/solution.py
@@ -1,12 +1,19 @@
+import functools
+
 import jax
 import jax.numpy as jnp
 from jax import lax
+from jax.experimental import pallas as pl
+from jax.experimental.pallas import tpu as pltpu
 from jax.sharding import PartitionSpec as P
 
 NT = 16
-
-
-def body(
+CHUNKS = ((0, NT // 2, 1), (2, 3, 4, 5, 6, 7))
+OFFSETS = CHUNKS[0] + CHUNKS[1]
+VMEM_BYTES = 60 * 1024 * 1024
+
+
+def general_body(
     integrals,
     tile_mask,
     tile_owner,
@@ -70,7 +77,464 @@
     return lax.dynamic_slice_in_dim(total, lax.axis_index("blk") * aux_local, aux_local, 0)
 
 
+def place(refs, tile_row, column):
+    owner_ref, mask_ref = refs
+    return mask_ref[tile_row * NT + owner_ref[column]]
+
+
+def masked_tile(values, kept):
+    return values * jnp.full(values.shape, kept, jnp.int32).astype(values.dtype)
+
+
+def picked_kernel(columns, planes_of, where_ref, owner_ref, mask_ref, *refs):
+    inputs, out_ref = refs[:-1], refs[-1]
+    tile = out_ref.shape[1]
+    group = where_ref[0]
+    row_plane = planes_of(pl.program_id(0)) ^ group
+    for q in range(columns):
+        tile_row = owner_ref[row_plane * columns + q]
+        for c in range(columns):
+            lanes = slice(c * tile, (c + 1) * tile)
+            kept = place((owner_ref, mask_ref), tile_row, group * columns + c)
+            out_ref[q, :, lanes] = masked_tile(inputs[q][0, 0, :, lanes], kept)
+
+
+def picked_rows(scalars, integrals, away, row_planes):
+    aux_local, basis_size, width = integrals.shape
+    tile = basis_size // NT
+    columns = width // tile
+
+    def planes_of(i):
+        return sum(jnp.where(i == at, plane, 0) for at, plane in enumerate(row_planes))
+
+    def row_map(q):
+        def index(i, where, owner, mask):
+            plane = planes_of(i) ^ where[0]
+            return (where[0] ^ away, owner[plane * columns + q], 0, 0)
+
+        return index
+
+    return pl.pallas_call(
+        functools.partial(picked_kernel, columns, planes_of),
+        grid_spec=pltpu.PrefetchScalarGridSpec(
+            num_scalar_prefetch=3,
+            grid=(len(row_planes),),
+            in_specs=[pl.BlockSpec((1, 1, tile, width), row_map(q)) for q in range(columns)],
+            out_specs=pl.BlockSpec((columns, tile, width), lambda i, *_: (i, 0, 0)),
+        ),
+        out_shape=jax.ShapeDtypeStruct((len(row_planes) * columns, tile, width), jnp.bfloat16),
+        compiler_params=pltpu.CompilerParams(vmem_limit_bytes=VMEM_BYTES),
+        cost_estimate=pl.CostEstimate(flops=0, bytes_accessed=0, transcendentals=0),
+        name="picked_rows",
+    )(*scalars, *([integrals.reshape(aux_local, NT, tile, width)] * columns))
+
+
+def offset_at(i):
+    return sum(jnp.where(i == at, offset, 0) for at, offset in enumerate(OFFSETS))
+
+
+def pair_kernel(columns, where_ref, owner_ref, mask_ref, *refs):
+    inputs, out_refs = refs[:columns], refs[columns:]
+    rows = out_refs[0].shape[3]
+    first = where_ref[0] * columns
+    for c in range(columns):
+        tile_row = owner_ref[lax.rem(first + c + offset_at(pl.program_id(0)), NT)]
+        kept = place((owner_ref, mask_ref), tile_row, first + c)
+        for part, out_ref in enumerate(out_refs):
+            start = pl.multiple_of((part ^ where_ref[1]) * rows, rows)
+            out_ref[:, 0, c] = masked_tile(inputs[c][:, 0, pl.ds(start, rows), :], kept)
+
+
+def pair_tiles(scalars, integrals, parts):
+    aux_local, basis_size, width = integrals.shape
+    tile = basis_size // NT
+    columns = width // tile
+    rows = tile // parts
+
+    def row_map(c):
+        def index(d, where, owner, mask):
+            return (0, owner[lax.rem(where[0] * columns + c + offset_at(d), NT)], 0, c)
+
+        return index
+
+    return pl.pallas_call(
+        functools.partial(pair_kernel, columns),
+        grid_spec=pltpu.PrefetchScalarGridSpec(
+            num_scalar_prefetch=3,
+            grid=(len(OFFSETS),),
+            in_specs=[
+                pl.BlockSpec((aux_local, 1, tile, tile), row_map(c)) for c in range(columns)
+            ],
+            out_specs=[
+                pl.BlockSpec((aux_local, 1, columns, rows, tile), lambda d, *_: (0, d, 0, 0, 0))
+            ]
+            * parts,
+        ),
+        out_shape=[
+            jax.ShapeDtypeStruct((aux_local, len(OFFSETS), columns, rows, tile), jnp.bfloat16)
+        ]
+        * parts,
+        compiler_params=pltpu.CompilerParams(vmem_limit_bytes=VMEM_BYTES),
+        cost_estimate=pl.CostEstimate(flops=0, bytes_accessed=0, transcendentals=0),
+        name="pair_tiles",
+    )(*scalars, *([integrals.reshape(aux_local, NT, tile, width)] * columns))
+
+
+def start_all(copies):
+    for copy in copies:
+        copy.start()
+
+
+def wait_all(copies):
+    for copy in copies:
+        copy.wait()
+
+
+def green_copies(green_refs, which, green, sems):
+    planes, held = green_refs[0].shape[0], green_refs[0].shape[2]
+    copies = []
+    for part, ref in enumerate(green_refs):
+        for plane in range(planes):
+            at = part * planes + plane
+            copies.append(
+                pltpu.make_async_copy(
+                    ref.at[plane, which], green.at[pl.ds(at * held, held)], sems.at[at]
+                )
+            )
+    return copies
+
+
+def occupied_columns(kcount, column_blocks, slot_ref, tile_ref, block_refs, green, full, half):
+    tile = green.shape[1]
+    width = full.shape[1] // len(column_blocks)
+    columns = width // tile
+    for at, blocks in enumerate(column_blocks):
+        for plane, (ref, first, turned) in enumerate(blocks):
+            values = block_refs[ref][first * columns : (first + 1) * columns]
+            values = values.reshape(width, width)
+            full[plane * width : (plane + 1) * width, at * width : (at + 1) * width] = (
+                values.T if turned else values
+            )
+
+    @pl.loop(0, NT)
+    def _(r):
+        left = jnp.concatenate([green[tile_ref[r * kcount + k]] for k in range(kcount)], axis=1)
+        starts = [pl.multiple_of(slot_ref[r * kcount + k] * tile, tile) for k in range(kcount)]
+        rows = pl.ds(pl.multiple_of(r * tile, tile), tile)
+        for at in range(len(column_blocks)):
+            right = jnp.concatenate(
+                [full[pl.ds(start, tile), at * width : (at + 1) * width] for start in starts],
+                axis=0,
+            )
+            values = jnp.dot(left, right, preferred_element_type=jnp.float32)
+            values = values.astype(jnp.bfloat16)
+            for c in range(columns):
+                half[at * columns + c, rows, :] = values[:, c * tile : (c + 1) * tile]
+
+
+def folded_pairs(kcount, columns, offsets, group, slot_ref, tile_ref, green, half, folded, out_ref):
+    tile = green.shape[1]
+    folded[...] = jnp.zeros_like(folded)
+    pieces = [(at, d, False) for at, d in enumerate(offsets)]
+    pieces += [(at, NT - d, True) for at, d in enumerate(offsets) if 0 < d < NT // 2]
+
+    @pl.loop(0, NT)
+    def _(s):
+        right = jnp.concatenate([green[tile_ref[s * kcount + k]] for k in range(kcount)], axis=0)
+        slots = [slot_ref[s * kcount + k] for k in range(kcount)]
+        for first in range(0, len(pieces), 4):
+            some = pieces[first : first + 4]
+            rows = [lax.rem(s + shift, NT) for _, shift, _ in some]
+            left = []
+            for r in rows:
+                start = ((r // columns) ^ group) * columns + lax.rem(r, columns)
+                start = pl.multiple_of(start * tile, tile)
+                left.append(
+                    jnp.concatenate([half[slot, pl.ds(start, tile), :] for slot in slots], axis=1)
+                )
+            values = jnp.dot(
+                jnp.concatenate(left, axis=0), right, preferred_element_type=jnp.float32
+            )
+            for place_at, ((at, _, turned), r) in enumerate(zip(some, rows)):
+                piece = values[place_at * tile : (place_at + 1) * tile]
+                if turned:
+                    folded[r, at] += piece.T
+                else:
+                    folded[s, at] += piece
+
+    rows = out_ref.shape[3]
+    parts = tile // rows
+
+    @pl.loop(0, NT // columns)
+    def _(plane):
+        @pl.loop(0, columns)
+        def _(c):
+            for at in range(len(offsets)):
+                values = folded[plane * columns + c, at].astype(jnp.bfloat16)
+                for part in range(parts):
+                    out_ref[plane * parts + part, at, c] = values[part * rows : (part + 1) * rows]
+
+
+def early_kernel(kcount, column_blocks, parts, slot_ref, tile_ref, *refs):
+    green_refs, refs = refs[:parts], refs[parts:]
+    block_refs, (half_ref, green, full, sems) = refs[:-4], refs[-4:]
+    copies = green_copies(green_refs, 0, green, sems)
+    start_all(copies)
+    wait_all(copies)
+    occupied_columns(kcount, column_blocks, slot_ref, tile_ref, block_refs, green, full, half_ref)
+
+
+def last_kernel(
+    kcount, columns, column_blocks, offsets, parts, group_ref, slot_ref, tile_ref, half_slot_ref,
+    virtual_tile_ref, *refs
+):
+    green_refs, refs = refs[:parts], refs[parts:]
+    held_ref, refs = refs[0], refs[1:]
+    block_refs, refs = refs[:-9], refs[-9:]
+    out_ref, half_ref, green, virtual, full, half, folded, sems, others = refs
+    copies = green_copies(green_refs, 0, green, sems)
+    later = green_copies(green_refs, 1, virtual, others)
+    count = held_ref.shape[0]
+    later.append(
+        pltpu.make_async_copy(held_ref, half.at[pl.ds(0, count)], others.at[others.shape[0] - 1])
+    )
+    start_all(copies + later)
+    wait_all(copies)
+    occupied_columns(kcount, column_blocks, slot_ref, tile_ref, block_refs, green, full, half_ref)
+    wait_all(later)
+    half[count:] = half_ref[...]
+    folded_pairs(
+        kcount, columns, offsets, group_ref[0], half_slot_ref, virtual_tile_ref, virtual, half,
+        folded, out_ref,
+    )
+
+
+def rest_kernel(
+    kcount, columns, offsets, parts, group_ref, half_slot_ref, virtual_tile_ref, *refs
+):
+    green_refs, refs = refs[:parts], refs[parts:]
+    held_ref, new_ref, out_ref, virtual, half, folded, others = refs
+    copies = green_copies(green_refs, 1, virtual, others)
+    count = held_ref.shape[0]
+    last = others.shape[0] - 2
+    copies.append(pltpu.make_async_copy(held_ref, half.at[pl.ds(0, count)], others.at[last]))
+    copies.append(
+        pltpu.make_async_copy(
+            new_ref, half.at[pl.ds(count, new_ref.shape[0])], others.at[last + 1]
+        )
+    )
+    start_all(copies)
+    wait_all(copies)
+    folded_pairs(
+        kcount, columns, offsets, group_ref[0], half_slot_ref, virtual_tile_ref, virtual, half,
+        folded, out_ref,
+    )
+
+
+def kernel_call(kernel, tables, anywhere, blocks, out_shape, scratch_shapes, name, flops=0):
+    return pl.pallas_call(
+        kernel,
+        in_specs=[pl.BlockSpec(memory_space=pltpu.SMEM)] * len(tables)
+        + [pl.BlockSpec(memory_space=pl.ANY)] * len(anywhere)
+        + [pl.BlockSpec(memory_space=pltpu.VMEM)] * len(blocks),
+        out_specs=jax.tree.map(lambda _: pl.BlockSpec(memory_space=pltpu.VMEM), out_shape),
+        out_shape=out_shape,
+        scratch_shapes=scratch_shapes,
+        compiler_params=pltpu.CompilerParams(vmem_limit_bytes=VMEM_BYTES),
+        cost_estimate=pl.CostEstimate(flops=flops, bytes_accessed=flops // 512, transcendentals=0),
+        name=name,
+    )(*tables, *anywhere, *blocks)
+
+
+def folded_body(
+    integrals,
+    tile_mask,
+    tile_owner,
+    occupied_tiles,
+    occupied_offsets,
+    virtual_tiles,
+    virtual_offsets,
+):
+    aux_local, basis_size, width = integrals.shape
+    tile = basis_size // NT
+    columns = width // tile
+    planes, parts = lax.axis_size("grp"), lax.axis_size("blk")
+    kcount = occupied_offsets.shape[0]
+    group = lax.axis_index("grp")
+
+    part = lax.axis_index("blk")
+    scalars = (
+        jnp.stack([group, part]).astype(jnp.int32),
+        tile_owner,
+        tile_mask.reshape(-1),
+    )
+
+    def swap(values, axis, size, distance):
+        return lax.ppermute(values, axis, [(at, at ^ distance) for at in range(size)])
+
+    greens = jnp.stack(
+        [
+            jnp.swapaxes(occupied_tiles.reshape(-1, tile, tile), 1, 2),
+            virtual_tiles.reshape(-1, tile, tile),
+        ]
+    )
+    held = greens.shape[1]
+    greens = jnp.stack([greens] + [swap(greens, "grp", planes, j) for j in range(1, planes)])
+    pairs = list(pair_tiles(scalars, integrals, parts))
+    for m in (2, 4):
+        pairs[m] = swap(pairs[m], "blk", parts, m)
+    near_off = picked_rows(scalars, integrals, 1, (3, 2))
+    across = picked_rows(scalars, integrals, 2, (0, 1))
+
+    slot = jnp.arange(NT, dtype=jnp.int32)
+    ordered = jnp.zeros((NT,), jnp.int32).at[tile_owner].set(slot)
+    ordered = (ordered // columns ^ group) * columns + ordered % columns
+    nearby = (slot // columns ^ group) * columns + slot % columns
+
+    def table(targets, offsets, order):
+        natural = (targets[:, None] - offsets[None, :]) % NT
+        flat = natural * kcount + jnp.arange(kcount, dtype=jnp.int32)[None, :]
+        device = flat // held
+        plane, other = device // parts ^ group, device % parts ^ part
+        at = ((other * planes + plane) * held) + flat % held
+        return order[natural].reshape(-1), at.reshape(-1)
+
+    plane = ordered // columns
+    halved = (plane % 2 * 2 + plane // 2) * columns + ordered % columns
+    occupied_table = table(tile_owner[nearby], occupied_offsets, ordered)
+    virtual_table = table(tile_owner, virtual_offsets, halved)
+
+    greens, near_off, across, pairs = lax.optimization_barrier((greens, near_off, across, pairs))
+    greens = [greens] + [swap(greens, "blk", parts, m) for m in range(2, parts, 2)]
+    near_off = swap(near_off, "grp", planes, 1)
+    across = swap(across, "grp", planes, 2)
+    near = picked_rows(scalars, integrals, 1, (0,))
+    far = picked_rows(scalars, integrals, 3, (0,))
+    own = picked_rows(scalars, integrals, 0, (0, 1, 2, 3))
+
+    greens, near_off, across, near, far, own, pairs, occupied_table, virtual_table = (
+        lax.optimization_barrier(
+            (greens, near_off, across, near, far, own, pairs, occupied_table, virtual_table)
+        )
+    )
+    near = swap(near, "grp", planes, 1)
+    far = swap(far, "grp", planes, 3)
+    greens = [each for mine in greens for each in (mine, swap(mine, "blk", parts, 1))]
+    for m in (3, 5):
+        pairs[m] = swap(pairs[m], "blk", parts, m)
+
+    where = scalars[0]
+
+    def vmem(*shape, dtype=jnp.bfloat16):
+        return pltpu.VMEM(shape, dtype)
+
+    devices = planes * parts
+    green = vmem(devices * held, tile, tile)
+
+    def full(count):
+        return vmem(basis_size, count * width)
+
+    def half(count):
+        return jax.ShapeDtypeStruct((count * columns, basis_size, tile), jnp.bfloat16)
+
+    def folded(offsets):
+        return (
+            jax.ShapeDtypeStruct(
+                (devices, len(offsets), columns, tile // parts, tile), jnp.bfloat16
+            ),
+            vmem(NT, len(offsets), tile, tile, dtype=jnp.float32),
+        )
+
+    column_blocks = (
+        tuple((0, plane, False) for plane in range(planes)),
+        ((0, 2, True), (1, 0, True), (2, 0, False), (2, 1, False)),
+    )
+    first = kernel_call(
+        functools.partial(early_kernel, kcount, column_blocks, parts),
+        occupied_table,
+        greens,
+        (own, near_off, across),
+        half(2),
+        [green, full(2), pltpu.SemaphoreType.DMA((devices,))],
+        "early_half",
+    )
+    first, near, far, pairs = lax.optimization_barrier((first, near, far, pairs))
+    column_blocks = (
+        ((0, 1, True), (3, 0, False), (1, 0, False), (1, 1, False)),
+        ((0, 3, True), (1, 1, True), (2, 1, True), (4, 0, False)),
+    )
+    out_shape, scratch = folded(CHUNKS[0])
+    sent, second = kernel_call(
+        functools.partial(last_kernel, kcount, columns, column_blocks, CHUNKS[0], parts),
+        (where,) + occupied_table + virtual_table,
+        [*greens, first],
+        (own, near_off, across, near, far),
+        (out_shape, half(2)),
+        [
+            green,
+            green,
+            full(2),
+            vmem(NT, basis_size, tile),
+            scratch,
+            pltpu.SemaphoreType.DMA((devices,)),
+            pltpu.SemaphoreType.DMA((devices + 1,)),
+        ],
+        "last_half_and_pairs",
+    )
+    sent, second, pairs = lax.optimization_barrier((sent, second, pairs))
+    for m in (1, 6, 7):
+        pairs[m] = swap(pairs[m], "blk", parts, m)
+    out_shape, scratch = folded(CHUNKS[1])
+    rest = kernel_call(
+        functools.partial(rest_kernel, kcount, columns, CHUNKS[1], parts),
+        (where,) + virtual_table,
+        [*greens, first, second],
+        (),
+        out_shape,
+        [
+            green,
+            vmem(NT, basis_size, tile),
+            scratch,
+            pltpu.SemaphoreType.DMA((devices + 2,)),
+        ],
+        "other_pairs",
+        flops=2 * 14 * basis_size * kcount * tile * tile * 2,
+    )
+
+    def everyone(values):
+        return lax.all_to_all(values, ("grp", "blk"), split_axis=0, concat_axis=0, tiled=True)
+
+    sent = everyone(sent)
+    sent, rest, pairs = lax.optimization_barrier((sent, rest, pairs))
+    rest = everyone(rest)
+
+    pairs = jnp.stack(pairs)
+    partial_sum = 0.0
+    at = 0
+    for offsets, each in zip(CHUNKS, (sent, rest)):
+        theirs = pairs[:, :, at : at + len(offsets)].reshape(parts * aux_local, -1)
+        at += len(offsets)
+        partial_sum = partial_sum + jnp.einsum(
+            "pe,qe->pq", each.reshape(devices, -1), theirs, preferred_element_type=jnp.float32
+        )
+    partial_sum = partial_sum * (1.0 / basis_size)
+    partial_sum = partial_sum.reshape(planes, parts, parts, aux_local)
+    partial_sum = partial_sum[:, :, jnp.arange(parts, dtype=jnp.int32) ^ part]
+    partial_sum = partial_sum.swapaxes(0, 1).reshape(1, parts, planes, -1)
+    spread = jnp.broadcast_to(partial_sum, (planes,) + partial_sum.shape[1:])
+    spread = everyone(spread.reshape((devices,) + partial_sum.shape[2:]))
+    return jnp.sum(spread, axis=0)
+
+
 def solution(mesh):
+    planes, parts = mesh.shape["grp"], mesh.shape["blk"]
+
+    def body(*args):
+        aux_local, basis_size, width = args[0].shape
+        tile = basis_size // NT
+        fits = aux_local == planes == 4 and parts == 8 and width % tile == 0 and tile % (16 * parts) == 0
+        return (folded_body if fits else general_body)(*args)
+
     in_specs = (
         P("blk", None, "grp"),
         P(),

time: 763 us -> 299 us (0.39)
  local copies, waits for them, and re-layouts: 275 us -> 23.3 us
  matrix products: 256 us -> 6.2 us
  Pallas kernels: 0 us -> 91.3 us
  blocking collectives: 40.2 us -> 10.8 us
  starting transfers between devices: 16.9 us -> 31 us
  waiting for transfers between devices: 143 us -> 129 us
  between operations: 13.9 us -> 0.53 us
    dot_general x17 -> x2, matrix products: 256 us -> 6.2 us  [folded_body(): jnp.einsum('pe,qe->pq', each.reshape(devices, -1), theirs, preferred_elem...]
    gather x25 -> x4, local copies, waits for them, and re-layouts: 161 us -> 4.72 us  [the longest x2 3.46 us: table(): return (order[natural].reshape(-1), at.reshape(-1))]
    pallas_call x0 -> x9, Pallas kernels: none -> 91.3 us  [the longest x3 66.5 us: kernel_call(): pl.pallas_call(kernel, in_specs=[pl.BlockSpec(memory_space=pltpu.SMEM)] *...]
    all_to_all x3 -> x2, waiting for transfers between devices: 142 us -> 59 us  [everyone(): lax.all_to_all(values, ('grp', 'blk'), split_axis=0, concat_axis=0, tiled...]
    ppermute x0 -> x21, waiting for transfers between devices: none -> 70.5 us  [swap(): lax.ppermute(values, axis, [(at, at ^ distance) for at in range(size)])]
    all_to_all x5 -> x1, local copies, waits for them, and re-layouts: 57.1 us -> 0.51 us  [everyone(): lax.all_to_all(values, ('grp', 'blk'), split_axis=0, concat_axis=0, tiled...]
    psum x1 -> x0, blocking collectives: 40.2 us -> none  [body(): total = lax.psum(partial_sum, ('grp', 'blk'))]
    reshape x4 -> x6, local copies, waits for them, and re-layouts: 43.4 us -> 7.22 us  [the longest x2 4.73 us: folded_body(): theirs = pairs[:, :, at:at + len(offsets)].reshape(parts * aux_local, -1)]
  transfers between devices with their start and end apart: 5 -> 23, of which waited for: 2 -> 11; matrix products, arithmetic and copies ran while one was open for 67% -> 7% of each run, Pallas kernels for 0% -> 22%
where the time goes in v2:
time: 299 us; the launch traced here: 298 us
  waiting for transfers between devices  129 us (43%)
  Pallas kernels  91.3 us (31%)
  starting transfers between devices  31 us (10%)
  local copies, waits for them, and re-layouts  23.3 us (8%)
  blocking collectives  10.8 us (4%)
  matrix products  6.2 us (2%)
  other arithmetic  4.97 us (2%)
    ppermute x21, waiting for transfers between devices, swap(): lax.ppermute(values, axis, [(at, at ^ distance) for at in range(size)])  70.5 us
    pallas_call x3, Pallas kernels, kernel_call(): pl.pallas_call(kernel, in_specs=[pl.BlockSpec(memory_space=pltpu.SMEM)] *...  66.5 us
    all_to_all x2, waiting for transfers between devices, everyone(): lax.all_to_all(values, ('grp', 'blk'), split_axis=0, concat_axis=0, tiled...  59 us
    ppermute x21, starting transfers between devices, swap(): lax.ppermute(values, axis, [(at, at ^ distance) for at in range(size)])  23.6 us
    pallas_call x5, Pallas kernels, picked_rows(): pl.pallas_call(functools.partial(picked_kernel, columns, planes_of), grid...  16.2 us
    all_to_all x1, blocking collectives, everyone(): lax.all_to_all(values, ('grp', 'blk'), split_axis=0, concat_axis=0, tiled...  10.8 us
    pallas_call x1, Pallas kernels, pair_tiles(): pl.pallas_call(functools.partial(pair_kernel, columns), grid_spec=pltpu.P...  8.64 us
    all_to_all x2, starting transfers between devices, everyone(): lax.all_to_all(values, ('grp', 'blk'), split_axis=0, concat_axis=0, tiled...  7.38 us
  transfers between devices with their start and end apart: 23, of which 11 were waited for; matrix products, arithmetic and copies ran while one was open for 7% of the time, Pallas kernels for 22%

profile of v2, /device:TPU:0, one launch (start us, length us, event | category | flops | bytes accessed | tf_op | source)
XLA Modules:
  0.0 297.6 jit_solution(4436978008838294401)
XLA Ops:
  0.0 1.0 copy.19
  1.0 0.9 fusion.39
  2.0 3.1 %collective-permute-start = (bf16[2,4,128,128]{3,2,1,0:T(8,128)(2,1)S(1)}, bf16[2,4,128,128]{3,2,1,0:T(8,128)(2,1)S(1)}, u32[]{:S(2)}, u32[]{:S(2)}) collective-permute-start(bf16[2,4,128,128]{3,2,1,0:T(8,128)(2,1)S(1)} %get-tuple-element.154), channel_id=1, source_target_pairs={{0,8},{8,0},{16,24},{24,16},{1,9},{9,1},{17,25},{25,17},{2,10},{10... | collective-permute-start | bytes 786440 | tf_op jit(solution)/shard_map/ppermute | solution.py:373
  5.1 2.6 collective-permute-start.1
  7.7 1.3 reshape.304.mask_ref
  9.6 8.6 %pair_tiles.1 = (bf16[4,9,4,16,128]{4,3,2,1,0:T(8,128)(2,1)}, bf16[4,9,4,16,128]{4,3,2,1,0:T(8,128)(2,1)}, bf16[4,9,4,16,128]{4,3,2,1,0:T(8,128)(2,1)}, bf16[4,9...) custom-call(s32[2]{0:T(128)} %pad_add_fusion.where_ref.group_ref, ...), custom_call_target="tpu_custom_call" | custom-call | tf_op jit(solution)/shard_map/pair_tiles/pallas_call | solution.py:160
  18.3 1.8 collective-permute-start.3
  20.1 1.5 collective-permute-start.4
  22.4 3.0 picked_rows.5
  25.4 2.9 picked_rows.6
  28.3 4.7 %picked_rows.9.refs_8_.refs_9_ = bf16[16,128,512]{2,1,0:T(8,128)(2,1)} custom-call(s32[2]{0:T(128)} %pad_add_fusion.where_ref.group_ref, s32[16]{0:T(128)} %owner_ref.11, s32[256]{0:T(256)} %reshape.304.mask_ref, bf16[4,16,128,512]{3,2,1,0:T(8,128)(2,1)} %bitcast.74, bf16[4,16,128,512]{3,2,1,0:T(8,128)(2,1)} %bitcast.75, bf16[4,16,128,512]{3,2,1,0:T(8,128)(2,1)} %bitcast.76, ...), custom_call_target="tpu_custom_call" | custom-call | tf_op jit(solution)/shard_map/picked_rows/pallas_call | solution.py:117
  33.1 2.7 picked_rows.7
  35.8 2.9 picked_rows.8
  39.8 1.1 pad_maximum_fusion.refs_0_
  41.0 0.9 copy-done.12
  42.9 2.7 collective-permute-start.7
  46.3 3.5 %collective-permute-start.9 = (bf16[8,128,512]{2,1,0:T(8,128)(2,1)}, bf16[8,128,512]{2,1,0:T(8,128)(2,1)}, u32[]{:S(2)}, u32[]{:S(2)}) collective-permute-start(bf16[8,128,512]{2,1,0:T(8,128)(2,1)} %picked_rows.6), channel_id=1, source_target_pairs={{0,16},{8,24},{16,0},{24,8},{1,17},{9,25},{17,1},{25,9},{2,18},{10... | collective-permute-start | bytes 3145736 | tf_op jit(solution)/shard_map/ppermute | solution.py:373
  50.6 1.7 gather_fusion.1
  52.4 1.7 gather_fusion.2
  54.7 13.5 %collective-permute-done.5.refs_2_ = bf16[4,2,4,128,128]{4,3,2,1,0:T(8,128)(2,1)S(1)} collective-permute-done((bf16[4,2,4,128,128]{4,3,2,1,0:T(8,128)(2,1)S(1)}, bf16[4,2,4,128,128]{4,3,2,1,0:T(8,128)(2,1)S(1)}, u32[]{:S(2)}, u32[]{:S(2)}) %collective-permute-start.5) | collective-permute-done | bytes 1048608 | tf_op jit(solution)/shard_map/ppermute | solution.py:373
  68.2 20.2 %collective-permute-done.6.refs_4_ = bf16[4,2,4,128,128]{4,3,2,1,0:T(8,128)(2,1)S(1)} collective-permute-done((bf16[4,2,4,128,128]{4,3,2,1,0:T(8,128)(2,1)S(1)}, bf16[4,2,4,128,128]{4,3,2,1,0:T(8,128)(2,1)S(1)}, u32[]{:S(2)}, u32[]{:S(2)}) %collective-permute-start.6) | collective-permute-done | bytes 1048608 | tf_op jit(solution)/shard_map/ppermute | solution.py:373
  88.4 2.5 collective-permute-done.8.refs_9_.refs_10_
  90.9 2.4 collective-permute-done.9.refs_10_.refs_11_
  94.4 1.5 collective-permute-done.10.refs_1_
  96.1 2.7 collective-permute-done.11.refs_3_
  99.2 1.2 collective-permute-done.12.refs_5_
  100.4 2.4 collective-permute-start.15
  102.8 14.5 %early_half.1.refs_8_ = bf16[8,2048,128]{2,1,0:T(8,128)(2,1)} custom-call(s32[128]{0:T(128)} %gather_fusion.1, s32[128]{0:T(128)} %get-tuple-element.98.tile_ref, bf16[4,2,4,128,128]{4,3,2,1,0:T(8,128)(2,1)} %copy-done.2, bf16[4,2,4,128,128]{4,3,2,1,0:T(8,128)(2,1)} %copy-done.5, bf16[4,2,4,128,128]{4,3,2,1,0:T(8,128)(2,1)} %copy-done.3, ...), custom_call_target="tpu_custom_call" | custom-call | tf_op jit(solution)/shard_map/early_half/pallas_call | solution.py:335
  117.3 7.8 %collective-permute-done.15.refs_13_ = bf16[4,128,512]{2,1,0:T(8,128)(2,1)} collective-permute-done((bf16[4,128,512]{2,1,0:T(8,128)(2,1)}, bf16[4,128,512]{2,1,0:T(8,128)(2,1)}, u32[]{:S(2)}, u32[]{:S(2)}) %collective-permute-start.15) | collective-permute-done | bytes 524320 | tf_op jit(solution)/shard_map/ppermute | solution.py:373
  125.2 26.2 %last_half_and_pairs.1 = (bf16[32,3,4,16,128]{4,3,2,1,0:T(8,128)(2,1)}, bf16[8,2048,128]{2,1,0:T(8,128)(2,1)}) custom-call(s32[2]{0:T(128)} %pad_add_fusion.where_ref.group_ref, s32[128]{0:T(128)} %gather_fusion.1, s32[128]{0:T(128)} %get-tuple-element.98.tile_ref, s32[128]{0:T(128)} %gather_fusion.2, s32[128]{0:T(128)} %get-tuple-element.100.virtual_tile_ref, ...), custom_call_target="tpu_custom_call" | custom-call | tf_op jit(solution)/shard_map/last_half_and_pairs/pallas_call | solution.py:335
  151.4 2.7 all-to-all-start
  154.4 2.6 collective-permute-start.19
  157.0 25.7 %other_pairs.1 = bf16[32,6,4,16,128]{4,3,2,1,0:T(8,128)(2,1)} custom-call(s32[2]{0:T(128)} %pad_add_fusion.where_ref.group_ref, s32[128]{0:T(128)} %gather_fusion.2, s32[128]{0:T(128)} %get-tuple-element.100.virtual_tile_ref, bf16[4,2,4,128,128]{4,3,2,1,0:T(8,128)(2,1)} %copy-done.2, bf16[4,2,4,128,128]{4,3,2,1,0:T(8,128)(2,1)} %copy-done.5, ...), custom_call_target="tpu_custom_call" | custom-call | flops 15032385536 | bytes 29360128 | tf_op jit(solution)/shard_map/other_pairs/pallas_call | solution.py:335
  182.8 6.6 %collective-permute-done.19 = bf16[4,9,4,16,128]{4,3,2,1,0:T(8,128)(2,1)} collective-permute-done((bf16[4,9,4,16,128]{4,3,2,1,0:T(8,128)(2,1)}, bf16[4,9,4,16,128]{4,3,2,1,0:T(8,128)(2,1)}, u32[]{:S(2)}, u32[]{:S(2)}) %collective-permute-start.19) | collective-permute-done | bytes 589856 | tf_op jit(solution)/shard_map/ppermute | solution.py:373
  189.4 12.1 %collective-permute-done.20 = bf16[4,9,4,16,128]{4,3,2,1,0:T(8,128)(2,1)} collective-permute-done((bf16[4,9,4,16,128]{4,3,2,1,0:T(8,128)(2,1)}, bf16[4,9,4,16,128]{4,3,2,1,0:T(8,128)(2,1)}, u32[]{:S(2)}, u32[]{:S(2)}) %collective-permute-start.20) | collective-permute-done | bytes 589856 | tf_op jit(solution)/shard_map/ppermute | solution.py:373
  201.5 4.7 %all-to-all-start.1 = ((bf16[32,6,4,16,128]{4,3,2,1,0:T(8,128)(2,1)}), bf16[32,6,4,16,128]{4,3,2,1,0:T(8,128)(2,1)}, u32[]{:S(2)}, u32[]{:S(2)}) async-start(bf16[32,6,4,16,128]{4,3,2,1,0:T(8,128)(2,1)} %other_pairs.1), calls=%async_computation.1 | async-start | bytes 6291456 | tf_op jit(solution)/shard_map/all_to_all | solution.py:505
  206.3 1.2 bitcast_dynamic-update-slice_fusion.6
  207.6 1.2 bitcast_dynamic-update-slice_fusion.4
  209.0 1.2 bitcast_dynamic-update-slice_fusion.1
  210.1 1.2 bitcast_dynamic-update-slice_fusion
  211.3 0.9 slice.17
  212.2 1.6 slice.16
  213.8 2.8 reshape.311
  216.6 1.9 reshape.309
  218.6 59.0 %all-to-all-done.1 = bf16[32,6,4,16,128]{4,3,2,1,0:T(8,128)(2,1)} async-done(((bf16[32,6,4,16,128]{4,3,2,1,0:T(8,128)(2,1)}), bf16[32,6,4,16,128]{4,3,2,1,0:T(8,128)(2,1)}, u32[]{:S(2)}, u32[]{:S(2)}) %all-to-all-start.1) | async-done | bytes 3145760 | tf_op jit(solution)/shard_map/all_to_all | solution.py:505
  277.5 5.1 %fusion = f32[32,32]{1,0:T(8,128)S(1)} fusion(bf16[32,49152]{1,0:T(8,128)(2,1)} %reshape.311, bf16[4,8,384,128]{3,2,1,0:T(8,128)(2,1)} %bitcast.32), kind=kOutput, calls=%fused_computation.5 | convolution fusion | flops 100663296 | bytes 6295552 | tf_op jit(solution)/shard_map/pe,qe->pq/dot_general | solution.py:517
  282.6 1.1 fusion.9
  284.8 10.8 %all_to_all.15 = f32[32,1,128]{2,1,0:T(1,128)S(1)} all-to-all(f32[32,1,128]{2,1,0:T(1,128)S(1)} %reshape.361), channel_id=1, replica_groups=mesh['grp'=4,'blk'=8] {'grp','blk'}, dimensions={0} | all-to-all | bytes 32768 | tf_op jit(solution)/shard_map/all_to_all | solution.py:505
  (104 shorter events, 11.1 us)
Async XLA Ops:
  2.0 37.1 %collective-permute-start = (bf16[2,4,128,128]{3,2,1,0:T(8,128)(2,1)S(1)}, bf16[2,4,128,128]{3,2,1,0:T(8,128)(2,1)S(1)}, u32[]{:S(2)}, u32[]{:S(2)}) collective-permute-start(bf16[2,4,128,128]{3,2,1,0:T(8,128)(2,1)S(1)} %get-tuple-element.154), channel_id=1, source_target_pairs={{0,8},{8,0},{16,24},{24,16},{1,9},{9,1},{17,25},{25,17},{2,10},{10... | collective-permute-start | bytes 786440 | tf_op jit(solution)/shard_map/ppermute | solution.py:373
  5.1 34.1 %collective-permute-start.1 = (bf16[2,4,128,128]{3,2,1,0:T(8,128)(2,1)S(1)}, bf16[2,4,128,128]{3,2,1,0:T(8,128)(2,1)S(1)}, u32[]{:S(2)}, u32[]{:S(2)}) collective-permute-start(bf16[2,4,128,128]{3,2,1,0:T(8,128)(2,1)S(1)} %get-tuple-element.154), channel_id=1, source_target_pairs={{0,16},{8,24},{16,0},{24,8},{1,17},{9,25},{17,1},{25,9},{2,18},{10... | collective-permute-start | bytes 786440 | tf_op jit(solution)/shard_map/ppermute | solution.py:373
  7.7 31.5 %collective-permute-start.2 = (bf16[2,4,128,128]{3,2,1,0:T(8,128)(2,1)S(1)}, bf16[2,4,128,128]{3,2,1,0:T(8,128)(2,1)S(1)}, u32[]{:S(2)}, u32[]{:S(2)}) collective-permute-start(bf16[2,4,128,128]{3,2,1,0:T(8,128)(2,1)S(1)} %get-tuple-element.154), channel_id=1, source_target_pairs={{0,24},{8,16},{16,8},{24,0},{1,25},{9,17},{17,9},{25,1},{2,26},{10... | collective-permute-start | bytes 786440 | tf_op jit(solution)/shard_map/ppermute | solution.py:373
  9.6 12.0 %copy-start = (s32[16]{0:T(128)S(1)}, s32[16]{0:T(128)}, u32[]{:S(2)}) copy-start(s32[16]{0:T(128)} %owner_ref.11) | copy-start | bytes 196
  9.6 12.0 %copy-start.20 = (s32[8]{0:T(128)S(1)}, s32[8]{0:T(128)}, u32[]{:S(2)}) copy-start(s32[8]{0:T(128)} %param.13) | copy-start | bytes 100
  9.6 12.7 %copy-start.19 = (s32[8]{0:T(128)S(1)}, s32[8]{0:T(128)}, u32[]{:S(2)}) copy-start(s32[8]{0:T(128)} %param.11) | copy-start | bytes 100
  18.3 22.6 %collective-permute-start.3 = (bf16[4,9,4,16,128]{4,3,2,1,0:T(8,128)(2,1)}, bf16[4,9,4,16,128]{4,3,2,1,0:T(8,128)(2,1)S(1)}, u32[]{:S(2)}, u32[]{:S(2)}) collective-permute-start(bf16[4,9,4,16,128]{4,3,2,1,0:T(8,128)(2,1)} %get-tuple-element.80), channel_id=1, source_target_pairs={{0,2},{1,3},{2,0},{3,1},{4,6},{5,7},{6,4},{7,5},{8,10},{9,11},{10,... | collective-permute-start | bytes 1769480 | tf_op jit(solution)/shard_map/ppermute | solution.py:373
  20.1 20.9 %collective-permute-start.4 = (bf16[4,9,4,16,128]{4,3,2,1,0:T(8,128)(2,1)}, bf16[4,9,4,16,128]{4,3,2,1,0:T(8,128)(2,1)S(1)}, u32[]{:S(2)}, u32[]{:S(2)}) collective-permute-start(bf16[4,9,4,16,128]{4,3,2,1,0:T(8,128)(2,1)} %get-tuple-element.82), channel_id=1, source_target_pairs={{0,4},{1,5},{2,6},{3,7},{4,0},{5,1},{6,2},{7,3},{8,12},{9,13},{10,... | collective-permute-start | bytes 1769480 | tf_op jit(solution)/shard_map/ppermute | solution.py:373
  35.8 14.0 %copy-start.1 = (s32[16]{0:T(128)S(1)}, s32[16]{0:T(128)}, u32[]{:S(2)}) copy-start(s32[16]{0:T(128)} %owner_ref.11) | copy-start | bytes 196
  39.1 0.7 copy-start.18
  40.9 52.3 %copy-start.2 = (bf16[4,2,4,128,128]{4,3,2,1,0:T(8,128)(2,1)}, bf16[4,2,4,128,128]{4,3,2,1,0:T(8,128)(2,1)S(1)}, u32[]{:S(2)}) copy-start(bf16[4,2,4,128,128]{4,3,2,1,0:T(8,128)(2,1)S(1)} %pad_maximum_fusion.refs_0_) | copy-start | bytes 3145732
  40.9 1.0 copy-start.12
  41.0 1.1 copy-start.10
  42.1 26.1 %collective-permute-start.5 = (bf16[4,2,4,128,128]{4,3,2,1,0:T(8,128)(2,1)S(1)}, bf16[4,2,4,128,128]{4,3,2,1,0:T(8,128)(2,1)S(1)}, u32[]{:S(2)}, u32[]{:S(2)}) collective-permute-start(bf16[4,2,4,128,128]{4,3,2,1,0:T(8,128)(2,1)S(1)} %pad_maximum_fusion.refs_0_), channel_id=1, source_target_pairs={{0,2},{1,3},{2,0},{3,1},{4,6},{5,7},{6,4},{7,5},{8,10},{9,11},{10,... | collective-permute-start | bytes 3145736 | tf_op jit(solution)/shard_map/ppermute | solution.py:373
  42.6 45.7 %collective-permute-start.6 = (bf16[4,2,4,128,128]{4,3,2,1,0:T(8,128)(2,1)S(1)}, bf16[4,2,4,128,128]{4,3,2,1,0:T(8,128)(2,1)S(1)}, u32[]{:S(2)}, u32[]{:S(2)}) collective-permute-start(bf16[4,2,4,128,128]{4,3,2,1,0:T(8,128)(2,1)S(1)} %pad_maximum_fusion.refs_0_), channel_id=1, source_target_pairs={{0,4},{1,5},{2,6},{3,7},{4,0},{5,1},{6,2},{7,3},{8,12},{9,13},{10,... | collective-permute-start | bytes 3145736 | tf_op jit(solution)/shard_map/ppermute | solution.py:373
  42.9 45.5 %collective-permute-start.7 = (bf16[4,2,4,128,128]{4,3,2,1,0:T(8,128)(2,1)S(1)}, bf16[4,2,4,128,128]{4,3,2,1,0:T(8,128)(2,1)}, u32[]{:S(2)}, u32[]{:S(2)}) collective-permute-start(bf16[4,2,4,128,128]{4,3,2,1,0:T(8,128)(2,1)S(1)} %pad_maximum_fusion.refs_0_), channel_id=1, source_target_pairs={{0,6},{1,7},{2,4},{3,5},{4,2},{5,3},{6,0},{7,1},{8,14},{9,15},{10,... | collective-permute-start | bytes 3145736 | tf_op jit(solution)/shard_map/ppermute | solution.py:373
  45.6 45.3 %collective-permute-start.8 = (bf16[8,128,512]{2,1,0:T(8,128)(2,1)}, bf16[8,128,512]{2,1,0:T(8,128)(2,1)}, u32[]{:S(2)}, u32[]{:S(2)}) collective-permute-start(bf16[8,128,512]{2,1,0:T(8,128)(2,1)} %picked_rows.5), channel_id=1, source_target_pairs={{0,8},{8,0},{16,24},{24,16},{1,9},{9,1},{17,25},{25,17},{2,10},{10... | collective-permute-start | bytes 3145736 | tf_op jit(solution)/shard_map/ppermute | solution.py:373
  46.3 47.0 %collective-permute-start.9 = (bf16[8,128,512]{2,1,0:T(8,128)(2,1)}, bf16[8,128,512]{2,1,0:T(8,128)(2,1)}, u32[]{:S(2)}, u32[]{:S(2)}) collective-permute-start(bf16[8,128,512]{2,1,0:T(8,128)(2,1)} %picked_rows.6), channel_id=1, source_target_pairs={{0,16},{8,24},{16,0},{24,8},{1,17},{9,25},{17,1},{25,9},{2,18},{10... | collective-permute-start | bytes 3145736 | tf_op jit(solution)/shard_map/ppermute | solution.py:373
  68.2 34.6 %copy-start.3 = (bf16[4,2,4,128,128]{4,3,2,1,0:T(8,128)(2,1)}, bf16[4,2,4,128,128]{4,3,2,1,0:T(8,128)(2,1)S(1)}, u32[]{:S(2)}) copy-start(bf16[4,2,4,128,128]{4,3,2,1,0:T(8,128)(2,1)S(1)} %collective-permute-done.5.refs_2_) | copy-start | bytes 3145732
  88.4 14.4 %copy-start.4 = (bf16[4,2,4,128,128]{4,3,2,1,0:T(8,128)(2,1)}, bf16[4,2,4,128,128]{4,3,2,1,0:T(8,128)(2,1)S(1)}, u32[]{:S(2)}) copy-start(bf16[4,2,4,128,128]{4,3,2,1,0:T(8,128)(2,1)S(1)} %collective-permute-done.6.refs_4_) | copy-start | bytes 3145732
  93.2 2.7 collective-permute-start.10
  93.2 5.7 %collective-permute-start.11 = (bf16[4,2,4,128,128]{4,3,2,1,0:T(8,128)(2,1)S(1)}, bf16[4,2,4,128,128]{4,3,2,1,0:T(8,128)(2,1)S(1)}, u32[]{:S(2)}, u32[]{:S(2)}) collective-permute-start(bf16[4,2,4,128,128]{4,3,2,1,0:T(8,128)(2,1)S(1)} %collective-permute-done.5.refs_2_), channel_id=1, source_target_pairs={{0,1},{1,0},{2,3},{3,2},{4,5},{5,4},{6,7},{7,6},{8,9},{9,8},{10,11... | collective-permute-start | bytes 3145736 | tf_op jit(solution)/shard_map/ppermute | solution.py:373
  93.7 6.6 %collective-permute-start.12 = (bf16[4,2,4,128,128]{4,3,2,1,0:T(8,128)(2,1)S(1)}, bf16[4,2,4,128,128]{4,3,2,1,0:T(8,128)(2,1)S(1)}, u32[]{:S(2)}, u32[]{:S(2)}) collective-permute-start(bf16[4,2,4,128,128]{4,3,2,1,0:T(8,128)(2,1)S(1)} %collective-permute-done.6.refs_4_), channel_id=1, source_target_pairs={{0,1},{1,0},{2,3},{3,2},{4,5},{5,4},{6,7},{7,6},{8,9},{9,8},{10,11... | collective-permute-start | bytes 3145736 | tf_op jit(solution)/shard_map/ppermute | solution.py:373
  93.7 9.0 %collective-permute-start.13 = (bf16[4,2,4,128,128]{4,3,2,1,0:T(8,128)(2,1)}, bf16[4,2,4,128,128]{4,3,2,1,0:T(8,128)(2,1)}, u32[]{:S(2)}, u32[]{:S(2)}) collective-permute-start(bf16[4,2,4,128,128]{4,3,2,1,0:T(8,128)(2,1)} %collective-permute-done.7.refs_6_), channel_id=1, source_target_pairs={{0,1},{1,0},{2,3},{3,2},{4,5},{5,4},{6,7},{7,6},{8,9},{9,8},{10,11... | collective-permute-start | bytes 3145736 | tf_op jit(solution)/shard_map/ppermute | solution.py:373
  94.2 30.9 %collective-permute-start.16 = (bf16[4,9,4,16,128]{4,3,2,1,0:T(8,128)(2,1)}, bf16[4,9,4,16,128]{4,3,2,1,0:T(8,128)(2,1)}, u32[]{:S(2)}, u32[]{:S(2)}) collective-permute-start(bf16[4,9,4,16,128]{4,3,2,1,0:T(8,128)(2,1)} %get-tuple-element.113), channel_id=1, source_target_pairs={{0,3},{1,2},{2,1},{3,0},{4,7},{5,6},{6,5},{7,4},{8,11},{9,10},{10,... | collective-permute-start | bytes 1769480 | tf_op jit(solution)/shard_map/ppermute | solution.py:373
  95.9 4.5 %copy-start.5 = (bf16[4,2,4,128,128]{4,3,2,1,0:T(8,128)(2,1)}, bf16[4,2,4,128,128]{4,3,2,1,0:T(8,128)(2,1)S(1)}, u32[]{:S(2)}) copy-start(bf16[4,2,4,128,128]{4,3,2,1,0:T(8,128)(2,1)S(1)} %collective-permute-done.10.refs_1_) | copy-start | bytes 3145732
  95.9 29.2 %collective-permute-start.17 = (bf16[4,9,4,16,128]{4,3,2,1,0:T(8,128)(2,1)}, bf16[4,9,4,16,128]{4,3,2,1,0:T(8,128)(2,1)S(1)}, u32[]{:S(2)}, u32[]{:S(2)}) collective-permute-start(bf16[4,9,4,16,128]{4,3,2,1,0:T(8,128)(2,1)} %get-tuple-element.115), channel_id=1, source_target_pairs={{0,5},{1,4},{2,7},{3,6},{4,1},{5,0},{6,3},{7,2},{8,13},{9,12},{10,... | collective-permute-start | bytes 1769480 | tf_op jit(solution)/shard_map/ppermute | solution.py:373
  98.9 3.9 %copy-start.6 = (bf16[4,2,4,128,128]{4,3,2,1,0:T(8,128)(2,1)}, bf16[4,2,4,128,128]{4,3,2,1,0:T(8,128)(2,1)S(1)}, u32[]{:S(2)}) copy-start(bf16[4,2,4,128,128]{4,3,2,1,0:T(8,128)(2,1)S(1)} %collective-permute-done.11.refs_3_) | copy-start | bytes 3145732
  98.9 18.4 %collective-permute-start.14 = (bf16[4,128,512]{2,1,0:T(8,128)(2,1)}, bf16[4,128,512]{2,1,0:T(8,128)(2,1)S(1)}, u32[]{:S(2)}, u32[]{:S(2)}) collective-permute-start(bf16[4,128,512]{2,1,0:T(8,128)(2,1)} %picked_rows.7), channel_id=1, source_target_pairs={{0,8},{8,0},{16,24},{24,16},{1,9},{9,1},{17,25},{25,17},{2,10},{10... | collective-permute-start | bytes 1572872 | tf_op jit(solution)/shard_map/ppermute | solution.py:373
  100.4 2.4 copy-start.7
  100.4 24.7 %collective-permute-start.15 = (bf16[4,128,512]{2,1,0:T(8,128)(2,1)}, bf16[4,128,512]{2,1,0:T(8,128)(2,1)}, u32[]{:S(2)}, u32[]{:S(2)}) collective-permute-start(bf16[4,128,512]{2,1,0:T(8,128)(2,1)} %picked_rows.8), channel_id=1, source_target_pairs={{0,24},{8,16},{16,8},{24,0},{1,25},{9,17},{17,9},{25,1},{2,26},{10... | collective-permute-start | bytes 1572872 | tf_op jit(solution)/shard_map/ppermute | solution.py:373
  117.3 7.8 %copy-start.17 = (bf16[4,128,512]{2,1,0:T(8,128)(2,1)}, bf16[4,128,512]{2,1,0:T(8,128)(2,1)S(1)}, u32[]{:S(2)}) copy-start(bf16[4,128,512]{2,1,0:T(8,128)(2,1)S(1)} %collective-permute-done.14.refs_12_) | copy-start | bytes 1572868
  125.1 26.2 %copy-start.15 = (bf16[4,9,4,16,128]{4,3,2,1,0:T(8,128)(2,1)}, bf16[4,9,4,16,128]{4,3,2,1,0:T(8,128)(2,1)S(1)}, u32[]{:S(2)}) copy-start(bf16[4,9,4,16,128]{4,3,2,1,0:T(8,128)(2,1)S(1)} %collective-permute-done.17) | copy-start | bytes 1769476
  151.4 50.1 %all-to-all-start = ((bf16[32,3,4,16,128]{4,3,2,1,0:T(8,128)(2,1)}), bf16[32,3,4,16,128]{4,3,2,1,0:T(8,128)(2,1)S(1)}, u32[]{:S(2)}, u32[]{:S(2)}) async-start(bf16[32,3,4,16,128]{4,3,2,1,0:T(8,128)(2,1)} %get-tuple-element.131), calls=%async_computation | async-start | bytes 3145728 | tf_op jit(solution)/shard_map/all_to_all | solution.py:505
  154.1 28.7 %collective-permute-start.18 = (bf16[4,9,4,16,128]{4,3,2,1,0:T(8,128)(2,1)}, bf16[4,9,4,16,128]{4,3,2,1,0:T(8,128)(2,1)}, u32[]{:S(2)}, u32[]{:S(2)}) collective-permute-start(bf16[4,9,4,16,128]{4,3,2,1,0:T(8,128)(2,1)} %get-tuple-element.134), channel_id=1, source_target_pairs={{0,1},{1,0},{2,3},{3,2},{4,5},{5,4},{6,7},{7,6},{8,9},{9,8},{10,11... | collective-permute-start | bytes 1769480 | tf_op jit(solution)/shard_map/ppermute | solution.py:373
  154.4 35.0 %collective-permute-start.19 = (bf16[4,9,4,16,128]{4,3,2,1,0:T(8,128)(2,1)}, bf16[4,9,4,16,128]{4,3,2,1,0:T(8,128)(2,1)}, u32[]{:S(2)}, u32[]{:S(2)}) collective-permute-start(bf16[4,9,4,16,128]{4,3,2,1,0:T(8,128)(2,1)} %get-tuple-element.139), channel_id=1, source_target_pairs={{0,6},{1,7},{2,4},{3,5},{4,2},{5,3},{6,0},{7,1},{8,14},{9,15},{10,... | collective-permute-start | bytes 1769480 | tf_op jit(solution)/shard_map/ppermute | solution.py:373
  157.0 44.5 %collective-permute-start.20 = (bf16[4,9,4,16,128]{4,3,2,1,0:T(8,128)(2,1)}, bf16[4,9,4,16,128]{4,3,2,1,0:T(8,128)(2,1)}, u32[]{:S(2)}, u32[]{:S(2)}) collective-permute-start(bf16[4,9,4,16,128]{4,3,2,1,0:T(8,128)(2,1)} %get-tuple-element.140), channel_id=1, source_target_pairs={{0,7},{1,6},{2,5},{3,4},{4,3},{5,2},{6,1},{7,0},{8,15},{9,14},{10,... | collective-permute-start | bytes 1769480 | tf_op jit(solution)/shard_map/ppermute | solution.py:373
  182.7 23.5 %copy-start.14 = (bf16[4,9,4,16,128]{4,3,2,1,0:T(8,128)(2,1)S(1)}, bf16[4,9,4,16,128]{4,3,2,1,0:T(8,128)(2,1)}, u32[]{:S(2)}) copy-start(bf16[4,9,4,16,128]{4,3,2,1,0:T(8,128)(2,1)} %get-tuple-element.142) | copy-start | bytes 1769476
  182.7 24.8 %copy-start.13 = (bf16[4,9,4,16,128]{4,3,2,1,0:T(8,128)(2,1)S(1)}, bf16[4,9,4,16,128]{4,3,2,1,0:T(8,128)(2,1)}, u32[]{:S(2)}) copy-start(bf16[4,9,4,16,128]{4,3,2,1,0:T(8,128)(2,1)} %copy-done.12) | copy-start | bytes 1769476
  182.7 26.0 %copy-start.11 = (bf16[4,9,4,16,128]{4,3,2,1,0:T(8,128)(2,1)S(1)}, bf16[4,9,4,16,128]{4,3,2,1,0:T(8,128)(2,1)}, u32[]{:S(2)}) copy-start(bf16[4,9,4,16,128]{4,3,2,1,0:T(8,128)(2,1)} %copy-done.10) | copy-start | bytes 1769476
  201.5 6.1 %copy-start.8 = (bf16[32,3,4,16,128]{4,3,2,1,0:T(8,128)(2,1)}, bf16[32,3,4,16,128]{4,3,2,1,0:T(8,128)(2,1)S(1)}, u32[]{:S(2)}) copy-start(bf16[32,3,4,16,128]{4,3,2,1,0:T(8,128)(2,1)S(1)} %all-to-all-done) | copy-start | bytes 4718596
  201.5 76.0 %all-to-all-start.1 = ((bf16[32,6,4,16,128]{4,3,2,1,0:T(8,128)(2,1)}), bf16[32,6,4,16,128]{4,3,2,1,0:T(8,128)(2,1)}, u32[]{:S(2)}, u32[]{:S(2)}) async-start(bf16[32,6,4,16,128]{4,3,2,1,0:T(8,128)(2,1)} %other_pairs.1), calls=%async_computation.1 | async-start | bytes 6291456 | tf_op jit(solution)/shard_map/all_to_all | solution.py:505
  206.2 2.7 copy-start.16
  216.6 66.0 %copy-start.9 = (bf16[32,3,4,16,128]{4,3,2,1,0:T(8,128)(2,1)S(1)}, bf16[32,3,4,16,128]{4,3,2,1,0:T(8,128)(2,1)}, u32[]{:S(2)}) copy-start(bf16[32,3,4,16,128]{4,3,2,1,0:T(8,128)(2,1)} %copy-done.8) | copy-start | bytes 4718596

commit v3 on v2

--- a/solution.py
+++ b/solution.py
@@ -8,8 +8,9 @@
 from jax.sharding import PartitionSpec as P
 
 NT = 16
-CHUNKS = ((0, NT // 2, 1), (2, 3, 4, 5, 6, 7))
+CHUNKS = ((0, NT // 2), (1, 2, 3, 4, 5, 6, 7))
 OFFSETS = CHUNKS[0] + CHUNKS[1]
+PARTS = ((0, 1), (2, 3), (4, 5), (6,), (7,))
 VMEM_BYTES = 60 * 1024 * 1024
 
 
@@ -99,6 +100,46 @@
             out_ref[q, :, lanes] = masked_tile(inputs[q][0, 0, :, lanes], kept)
 
 
+def triangle(columns):
+    return [(q, c) for q in range(columns) for c in range(q + 1)]
+
+
+def picked_square_kernel(columns, where_ref, owner_ref, mask_ref, *refs):
+    inputs, out_ref = refs[:-1], refs[-1]
+    tile = out_ref.shape[1]
+    first = where_ref[0] * columns
+    for at, (q, c) in enumerate(triangle(columns)):
+        kept = place((owner_ref, mask_ref), owner_ref[first + q], first + c)
+        out_ref[at] = masked_tile(inputs[q][0, 0, :, c * tile : (c + 1) * tile], kept)
+
+
+def picked_square(scalars, integrals, away):
+    aux_local, basis_size, width = integrals.shape
+    tile = basis_size // NT
+    columns = width // tile
+    count = len(triangle(columns))
+
+    def row_map(q):
+        def index(i, where, owner, mask):
+            return (where[0] ^ away, owner[where[0] * columns + q], 0, 0)
+
+        return index
+
+    return pl.pallas_call(
+        functools.partial(picked_square_kernel, columns),
+        grid_spec=pltpu.PrefetchScalarGridSpec(
+            num_scalar_prefetch=3,
+            grid=(1,),
+            in_specs=[pl.BlockSpec((1, 1, tile, width), row_map(q)) for q in range(columns)],
+            out_specs=pl.BlockSpec((count, tile, tile), lambda i, *_: (0, 0, 0)),
+        ),
+        out_shape=jax.ShapeDtypeStruct((count, tile, tile), jnp.bfloat16),
+        compiler_params=pltpu.CompilerParams(vmem_limit_bytes=VMEM_BYTES),
+        cost_estimate=pl.CostEstimate(flops=0, bytes_accessed=0, transcendentals=0),
+        name="picked_square",
+    )(*scalars, *([integrals.reshape(aux_local, NT, tile, width)] * columns))
+
+
 def picked_rows(scalars, integrals, away, row_planes):
     aux_local, basis_size, width = integrals.shape
     tile = basis_size // NT
@@ -135,14 +176,15 @@
 
 def pair_kernel(columns, where_ref, owner_ref, mask_ref, *refs):
     inputs, out_refs = refs[:columns], refs[columns:]
-    rows = out_refs[0].shape[3]
+    rows = out_refs[0].shape[4]
     first = where_ref[0] * columns
     for c in range(columns):
         tile_row = owner_ref[lax.rem(first + c + offset_at(pl.program_id(0)), NT)]
         kept = place((owner_ref, mask_ref), tile_row, first + c)
-        for part, out_ref in enumerate(out_refs):
-            start = pl.multiple_of((part ^ where_ref[1]) * rows, rows)
-            out_ref[:, 0, c] = masked_tile(inputs[c][:, 0, pl.ds(start, rows), :], kept)
+        for out_ref, some in zip(out_refs, PARTS):
+            for at, part in enumerate(some):
+                start = pl.multiple_of((part ^ where_ref[1]) * rows, rows)
+                out_ref[at, :, 0, c] = masked_tile(inputs[c][:, 0, pl.ds(start, rows), :], kept)
 
 
 def pair_tiles(scalars, integrals, parts):
@@ -166,14 +208,19 @@
                 pl.BlockSpec((aux_local, 1, tile, tile), row_map(c)) for c in range(columns)
             ],
             out_specs=[
-                pl.BlockSpec((aux_local, 1, columns, rows, tile), lambda d, *_: (0, d, 0, 0, 0))
-            ]
-            * parts,
+                pl.BlockSpec(
+                    (len(some), aux_local, 1, columns, rows, tile),
+                    lambda d, *_: (0, 0, d, 0, 0, 0),
+                )
+                for some in PARTS
+            ],
         ),
         out_shape=[
-            jax.ShapeDtypeStruct((aux_local, len(OFFSETS), columns, rows, tile), jnp.bfloat16)
-        ]
-        * parts,
+            jax.ShapeDtypeStruct(
+                (len(some), aux_local, len(OFFSETS), columns, rows, tile), jnp.bfloat16
+            )
+            for some in PARTS
+        ],
         compiler_params=pltpu.CompilerParams(vmem_limit_bytes=VMEM_BYTES),
         cost_estimate=pl.CostEstimate(flops=0, bytes_accessed=0, transcendentals=0),
         name="pair_tiles",
@@ -191,11 +238,11 @@
 
 
 def green_copies(green_refs, which, green, sems):
-    planes, held = green_refs[0].shape[0], green_refs[0].shape[2]
     copies = []
-    for part, ref in enumerate(green_refs):
-        for plane in range(planes):
-            at = part * planes + plane
+    for ref in green_refs:
+        held = ref.shape[2]
+        for plane in range(ref.shape[0]):
+            at = len(copies)
             copies.append(
                 pltpu.make_async_copy(
                     ref.at[plane, which], green.at[pl.ds(at * held, held)], sems.at[at]
@@ -210,6 +257,15 @@
     columns = width // tile
     for at, blocks in enumerate(column_blocks):
         for plane, (ref, first, turned) in enumerate(blocks):
+            if first is None:
+                for i, (q, c) in enumerate(triangle(columns)):
+                    row, column = plane * width + q * tile, at * width + c * tile
+                    values = block_refs[ref][i]
+                    full[row : row + tile, column : column + tile] = values
+                    if q != c:
+                        row, column = plane * width + c * tile, at * width + q * tile
+                        full[row : row + tile, column : column + tile] = values.T
+                continue
             values = block_refs[ref][first * columns : (first + 1) * columns]
             values = values.reshape(width, width)
             full[plane * width : (plane + 1) * width, at * width : (at + 1) * width] = (
@@ -380,11 +436,8 @@
     )
     held = greens.shape[1]
     greens = jnp.stack([greens] + [swap(greens, "grp", planes, j) for j in range(1, planes)])
-    pairs = list(pair_tiles(scalars, integrals, parts))
-    for m in (2, 4):
-        pairs[m] = swap(pairs[m], "blk", parts, m)
-    near_off = picked_rows(scalars, integrals, 1, (3, 2))
-    across = picked_rows(scalars, integrals, 2, (0, 1))
+    near_two = picked_rows(scalars, integrals, 1, (3,))
+    across_off = picked_rows(scalars, integrals, 2, (1,))
 
     slot = jnp.arange(NT, dtype=jnp.int32)
     ordered = jnp.zeros((NT,), jnp.int32).at[tile_owner].set(slot)
@@ -404,24 +457,44 @@
     occupied_table = table(tile_owner[nearby], occupied_offsets, ordered)
     virtual_table = table(tile_owner, virtual_offsets, halved)
 
-    greens, near_off, across, pairs = lax.optimization_barrier((greens, near_off, across, pairs))
-    greens = [greens] + [swap(greens, "blk", parts, m) for m in range(2, parts, 2)]
-    near_off = swap(near_off, "grp", planes, 1)
+    greens, near_two, across_off, scalars = lax.optimization_barrier(
+        (greens, near_two, across_off, scalars)
+    )
+    greens = [greens, swap(greens, "blk", parts, 1)] + [
+        swap(greens, "blk", parts, m) for m in (2, 4)
+    ]
+    near_two = swap(near_two, "grp", planes, 1)
+    across_off = swap(across_off, "grp", planes, 2)
+    near_three = picked_rows(scalars, integrals, 1, (2,))
+    across = picked_square(scalars, integrals, 2)
+    pairs = list(pair_tiles(scalars, integrals, parts))
+
+    greens, near_two, across_off, near_three, across, pairs, scalars = lax.optimization_barrier(
+        (greens, near_two, across_off, near_three, across, pairs, scalars)
+    )
+    greens = greens[:2] + [
+        greens[2],
+        swap(greens[2], "blk", parts, 1),
+        greens[3],
+        swap(greens[3], "blk", parts, 1),
+        swap(greens[0], "blk", parts, 6),
+    ]
+    near_three = swap(near_three, "grp", planes, 1)
     across = swap(across, "grp", planes, 2)
-    near = picked_rows(scalars, integrals, 1, (0,))
-    far = picked_rows(scalars, integrals, 3, (0,))
+    near = picked_square(scalars, integrals, 1)
+    far = picked_square(scalars, integrals, 3)
     own = picked_rows(scalars, integrals, 0, (0, 1, 2, 3))
 
-    greens, near_off, across, near, far, own, pairs, occupied_table, virtual_table = (
+    greens, near_three, across, near, far, own, pairs, occupied_table, virtual_table = (
         lax.optimization_barrier(
-            (greens, near_off, across, near, far, own, pairs, occupied_table, virtual_table)
+            (greens, near_three, across, near, far, own, pairs, occupied_table, virtual_table)
         )
     )
+    greens = greens + [swap(greens[6], "blk", parts, 1)]
     near = swap(near, "grp", planes, 1)
     far = swap(far, "grp", planes, 3)
-    greens = [each for mine in greens for each in (mine, swap(mine, "blk", parts, 1))]
-    for m in (3, 5):
-        pairs[m] = swap(pairs[m], "blk", parts, m)
+    for m in (1, 2, 3):
+        pairs[m] = swap(pairs[m], "blk", parts, 2 * m)
 
     where = scalars[0]
 
@@ -447,28 +520,29 @@
 
     column_blocks = (
         tuple((0, plane, False) for plane in range(planes)),
-        ((0, 2, True), (1, 0, True), (2, 0, False), (2, 1, False)),
+        ((0, 2, True), (1, 0, True), (3, None, False), (2, 0, False)),
     )
     first = kernel_call(
-        functools.partial(early_kernel, kcount, column_blocks, parts),
+        functools.partial(early_kernel, kcount, column_blocks, len(greens)),
         occupied_table,
         greens,
-        (own, near_off, across),
+        (own, near_two, across_off, across),
         half(2),
         [green, full(2), pltpu.SemaphoreType.DMA((devices,))],
         "early_half",
-    )
-    first, near, far, pairs = lax.optimization_barrier((first, near, far, pairs))
+        flops=2 * basis_size * kcount * tile * 2 * width * 2,
+    )
+    first, near, far = lax.optimization_barrier((first, near, far))
     column_blocks = (
-        ((0, 1, True), (3, 0, False), (1, 0, False), (1, 1, False)),
-        ((0, 3, True), (1, 1, True), (2, 1, True), (4, 0, False)),
+        ((0, 1, True), (4, None, False), (1, 0, False), (2, 0, False)),
+        ((0, 3, True), (2, 0, True), (3, 0, True), (5, None, False)),
     )
     out_shape, scratch = folded(CHUNKS[0])
     sent, second = kernel_call(
-        functools.partial(last_kernel, kcount, columns, column_blocks, CHUNKS[0], parts),
+        functools.partial(last_kernel, kcount, columns, column_blocks, CHUNKS[0], len(greens)),
         (where,) + occupied_table + virtual_table,
         [*greens, first],
-        (own, near_off, across, near, far),
+        (own, near_two, near_three, across_off, near, far),
         (out_shape, half(2)),
         [
             green,
@@ -482,11 +556,10 @@
         "last_half_and_pairs",
     )
     sent, second, pairs = lax.optimization_barrier((sent, second, pairs))
-    for m in (1, 6, 7):
-        pairs[m] = swap(pairs[m], "blk", parts, m)
+    pairs[4] = swap(pairs[4], "blk", parts, 7)
     out_shape, scratch = folded(CHUNKS[1])
     rest = kernel_call(
-        functools.partial(rest_kernel, kcount, columns, CHUNKS[1], parts),
+        functools.partial(rest_kernel, kcount, columns, CHUNKS[1], len(greens)),
         (where,) + virtual_table,
         [*greens, first, second],
         (),
@@ -505,8 +578,13 @@
         return lax.all_to_all(values, ("grp", "blk"), split_axis=0, concat_axis=0, tiled=True)
 
     sent = everyone(sent)
-    sent, rest, pairs = lax.optimization_barrier((sent, rest, pairs))
+    sent, rest = lax.optimization_barrier((sent, rest))
     rest = everyone(rest)
+    pairs = [
+        each
+        for mine in pairs[:3]
+        for each in (mine[0], swap(mine[1], "blk", parts, 1))
+    ] + [pairs[3][0], pairs[4][0]]
 
     pairs = jnp.stack(pairs)
     partial_sum = 0.0

time: 299 us -> 272 us (0.910)
  waiting for transfers between devices: 129 us -> 95.7 us
  starting transfers between devices: 31 us -> 39 us
  local copies, waits for them, and re-layouts: 23.3 us -> 20.1 us
    all_to_all x2, waiting for transfers between devices: 59 us -> 23.5 us  [everyone(): lax.all_to_all(values, ('grp', 'blk'), split_axis=0, concat_axis=0, tiled...]
    pallas_call x0 -> x3, Pallas kernels: none -> 7.88 us  [picked_square(): pl.pallas_call(functools.partial(picked_square_kernel, columns), grid_spe...]
    ppermute x21 -> x23, starting transfers between devices: 23.6 us -> 29.1 us  [swap(): lax.ppermute(values, axis, [(at, at ^ distance) for at in range(size)])]
    unnamed x51 -> x28, local copies, waits for them, and re-layouts: 5.92 us -> 1.69 us
    pallas_call x5 -> x4, Pallas kernels: 16.2 us -> 13.2 us  [picked_rows(): pl.pallas_call(functools.partial(picked_kernel, columns, planes_of), grid...]
    ppermute x21 -> x23, waiting for transfers between devices: 70.5 us -> 72.3 us  [swap(): lax.ppermute(values, axis, [(at, at ^ distance) for at in range(size)])]
  transfers between devices with their start and end apart: 23 -> 25, of which waited for: 11 -> 10; matrix products, arithmetic and copies ran while one was open for 7% -> 7% of each run, Pallas kernels for 22% -> 35%
where the time goes in v3:
time: 272 us; the launch traced here: 271 us
  waiting for transfers between devices  95.7 us (35%)
  Pallas kernels  93.8 us (34%)
  starting transfers between devices  39 us (14%)
  local copies, waits for them, and re-layouts  20.1 us (7%)
  blocking collectives  9.89 us (4%)
  matrix products  7.64 us (3%)
  other arithmetic  3.98 us (1%)
    ppermute x23, waiting for transfers between devices, swap(): lax.ppermute(values, axis, [(at, at ^ distance) for at in range(size)])  72.3 us
    pallas_call x3, Pallas kernels, kernel_call(): pl.pallas_call(kernel, in_specs=[pl.BlockSpec(memory_space=pltpu.SMEM)] *...  64.2 us
    ppermute x23, starting transfers between devices, swap(): lax.ppermute(values, axis, [(at, at ^ distance) for at in range(size)])  29.1 us
    all_to_all x2, waiting for transfers between devices, everyone(): lax.all_to_all(values, ('grp', 'blk'), split_axis=0, concat_axis=0, tiled...  23.5 us
    pallas_call x4, Pallas kernels, picked_rows(): pl.pallas_call(functools.partial(picked_kernel, columns, planes_of), grid...  13.2 us
    all_to_all x1, blocking collectives, everyone(): lax.all_to_all(values, ('grp', 'blk'), split_axis=0, concat_axis=0, tiled...  9.89 us
    all_to_all x2, starting transfers between devices, everyone(): lax.all_to_all(values, ('grp', 'blk'), split_axis=0, concat_axis=0, tiled...  9.87 us
    pallas_call x1, Pallas kernels, pair_tiles(): pl.pallas_call(functools.partial(pair_kernel, columns), grid_spec=pltpu.P...  8.52 us
  transfers between devices with their start and end apart: 25, of which 10 were waited for; matrix products, arithmetic and copies ran while one was open for 7% of the time, Pallas kernels for 35%

profile of v3, /device:TPU:0, one launch (start us, length us, event | category | flops | bytes accessed | tf_op | source)
XLA Modules:
  0.0 270.6 jit_solution(10940280038907234260)
XLA Ops:
  0.0 1.0 copy.19
  1.0 0.9 fusion.33
  2.0 3.1 %collective-permute-start = (bf16[2,4,128,128]{3,2,1,0:T(8,128)(2,1)S(1)}, bf16[2,4,128,128]{3,2,1,0:T(8,128)(2,1)S(1)}, u32[]{:S(2)}, u32[]{:S(2)}) collective-permute-start(bf16[2,4,128,128]{3,2,1,0:T(8,128)(2,1)S(1)} %get-tuple-element.138), channel_id=1, source_target_pairs={{0,8},{8,0},{16,24},{24,16},{1,9},{9,1},{17,25},{25,17},{2,10},{10... | collective-permute-start | bytes 786440 | tf_op jit(solution)/shard_map/ppermute | solution.py:429
  5.1 2.6 collective-permute-start.1
  7.7 1.3 reshape.306.mask_ref
  9.7 2.7 picked_rows.4
  12.3 2.9 %picked_rows.5 = bf16[4,128,512]{2,1,0:T(8,128)(2,1)} custom-call(s32[2]{0:T(128)} %pad_add_fusion.where_ref.group_ref, s32[16]{0:T(128)} %owner_ref.9, s32[256]{0:T(256)} %reshape.306.mask_ref, bf16[4,16,128,512]{3,2,1,0:T(8,128)(2,1)} %bitcast.58, bf16[4,16,128,512]{3,2,1,0:T(8,128)(2,1)} %bitcast.59, bf16[4,16,128,512]{3,2,1,0:T(8,128)(2,1)} %bitcast.60, ...), custom_call_target="tpu_custom_call" | custom-call | tf_op jit(solution)/shard_map/picked_rows/pallas_call | solution.py:158
  15.2 1.0 collective-permute-done
  16.2 10.2 %collective-permute-done.1 = bf16[2,4,128,128]{3,2,1,0:T(8,128)(2,1)S(1)} collective-permute-done((bf16[2,4,128,128]{3,2,1,0:T(8,128)(2,1)S(1)}, bf16[2,4,128,128]{3,2,1,0:T(8,128)(2,1)S(1)}, u32[]{:S(2)}, u32[]{:S(2)}) %collective-permute-start.1) | collective-permute-done | bytes 262176 | tf_op jit(solution)/shard_map/ppermute | solution.py:429
  26.7 1.6 collective-permute-start.4
  28.2 1.5 collective-permute-start.5
  30.4 4.8 %collective-permute-start.6 = (bf16[4,128,512]{2,1,0:T(8,128)(2,1)}, bf16[4,128,512]{2,1,0:T(8,128)(2,1)}, u32[]{:S(2)}, u32[]{:S(2)}) collective-permute-start(bf16[4,128,512]{2,1,0:T(8,128)(2,1)} %picked_rows.4), channel_id=1, source_target_pairs={{0,8},{8,0},{16,24},{24,16},{1,9},{9,1},{17,25},{25,17},{2,10},{10... | collective-permute-start | bytes 1572872 | tf_op jit(solution)/shard_map/ppermute | solution.py:429
  35.3 1.1 collective-permute-start.7
  37.0 8.5 %pair_tiles.1 = (bf16[2,4,9,4,16,128]{5,4,3,2,1,0:T(8,128)(2,1)}, bf16[2,4,9,4,16,128]{5,4,3,2,1,0:T(8,128)(2,1)}, bf16[2,4,9,4,16,128]{5,4,3,2,1,0:T(8,128)(2,1...) custom-call(s32[2]{0:T(128)} %pad_add_fusion.where_ref.group_ref, s32[16]{0:T(128)} %owner_ref.9, ...), custom_call_target="tpu_custom_call" | custom-call | tf_op jit(solution)/shard_map/pair_tiles/pallas_call | solution.py:202
  45.5 2.6 picked_square.3
  48.1 2.8 %picked_rows.6 = bf16[4,128,512]{2,1,0:T(8,128)(2,1)} custom-call(s32[2]{0:T(128)} %pad_add_fusion.where_ref.group_ref, s32[16]{0:T(128)} %owner_ref.9, s32[256]{0:T(256)} %reshape.306.mask_ref, bf16[4,16,128,512]{3,2,1,0:T(8,128)(2,1)} %bitcast.70, bf16[4,16,128,512]{3,2,1,0:T(8,128)(2,1)} %bitcast.71, bf16[4,16,128,512]{3,2,1,0:T(8,128)(2,1)} %bitcast.72, ...), custom_call_target="tpu_custom_call" | custom-call | tf_op jit(solution)/shard_map/picked_rows/pallas_call | solution.py:158
  50.9 7.8 %collective-permute-done.6.refs_9_.refs_10_ = bf16[4,128,512]{2,1,0:T(8,128)(2,1)} collective-permute-done((bf16[4,128,512]{2,1,0:T(8,128)(2,1)}, bf16[4,128,512]{2,1,0:T(8,128)(2,1)}, u32[]{:S(2)}, u32[]{:S(2)}) %collective-permute-start.6) | collective-permute-done | bytes 524320 | tf_op jit(solution)/shard_map/ppermute | solution.py:429
  58.7 2.5 collective-permute-done.7.refs_10_.refs_12_
  63.7 1.8 gather_fusion.1
  65.5 2.6 collective-permute-start.12
  68.1 1.7 gather_fusion.2
  70.3 4.8 %picked_rows.7.refs_8_.refs_9_ = bf16[16,128,512]{2,1,0:T(8,128)(2,1)} custom-call(s32[2]{0:T(128)} %pad_add_fusion.where_ref.group_ref, s32[16]{0:T(128)} %owner_ref.9, s32[256]{0:T(256)} %reshape.306.mask_ref, bf16[4,16,128,512]{3,2,1,0:T(8,128)(2,1)} %bitcast.74, bf16[4,16,128,512]{3,2,1,0:T(8,128)(2,1)} %bitcast.75, bf16[4,16,128,512]{3,2,1,0:T(8,128)(2,1)} %bitcast.76, ...), custom_call_target="tpu_custom_call" | custom-call | tf_op jit(solution)/shard_map/picked_rows/pallas_call | solution.py:158
  75.1 2.6 picked_square.5
  77.7 2.7 picked_square.4
  80.4 2.0 collective-permute-done.12.refs_11_
  82.3 2.0 collective-permute-done.11.refs_11_
  84.5 1.6 collective-permute-start.16
  86.0 1.5 collective-permute-start.17
  87.5 1.3 collective-permute-start.14
  88.8 1.5 collective-permute-start.15
  90.4 1.3 collective-permute-start.18
  91.7 14.3 %early_half.1.refs_8_ = bf16[8,2048,128]{2,1,0:T(8,128)(2,1)} custom-call(s32[128]{0:T(128)} %gather_fusion.1, s32[128]{0:T(128)} %get-tuple-element.93.tile_ref, bf16[4,2,4,128,128]{4,3,2,1,0:T(8,128)(2,1)} %copy-done.2, bf16[4,2,4,128,128]{4,3,2,1,0:T(8,128)(2,1)} %copy-done.4, bf16[4,2,4,128,128]{4,3,2,1,0:T(8,128)(2,1)} %copy-done.5, ...), custom_call_target="tpu_custom_call" | custom-call | flops 8589934592 | bytes 16777216 | tf_op jit(solution)/shard_map/early_half/pallas_call | solution.py:391
  106.1 22.0 %last_half_and_pairs.1 = (bf16[32,2,4,16,128]{4,3,2,1,0:T(8,128)(2,1)}, bf16[8,2048,128]{2,1,0:T(8,128)(2,1)}) custom-call(s32[2]{0:T(128)} %pad_add_fusion.where_ref.group_ref, s32[128]{0:T(128)} %gather_fusion.1, s32[128]{0:T(128)} %get-tuple-element.93.tile_ref, s32[128]{0:T(128)} %gather_fusion.2, s32[128]{0:T(128)} %get-tuple-element.95.virtual_tile_ref, ...), custom_call_target="tpu_custom_call" | custom-call | tf_op jit(solution)/shard_map/last_half_and_pairs/pallas_call | solution.py:391
  128.1 3.8 %all-to-all-start = ((bf16[32,2,4,16,128]{4,3,2,1,0:T(8,128)(2,1)}), bf16[32,2,4,16,128]{4,3,2,1,0:T(8,128)(2,1)}, u32[]{:S(2)}, u32[]{:S(2)}) async-start(bf16[32,2,4,16,128]{4,3,2,1,0:T(8,128)(2,1)} %get-tuple-element.120), calls=%async_computation | async-start | bytes 2097152 | tf_op jit(solution)/shard_map/all_to_all | solution.py:578
  131.9 27.9 %other_pairs.1 = bf16[32,7,4,16,128]{4,3,2,1,0:T(8,128)(2,1)} custom-call(s32[2]{0:T(128)} %pad_add_fusion.where_ref.group_ref, s32[128]{0:T(128)} %gather_fusion.2, s32[128]{0:T(128)} %get-tuple-element.95.virtual_tile_ref, bf16[4,2,4,128,128]{4,3,2,1,0:T(8,128)(2,1)} %copy-done.2, bf16[4,2,4,128,128]{4,3,2,1,0:T(8,128)(2,1)} %copy-done.4, ...), custom_call_target="tpu_custom_call" | custom-call | flops 15032385536 | bytes 29360128 | tf_op jit(solution)/shard_map/other_pairs/pallas_call | solution.py:391
  159.9 6.1 %all-to-all-start.1 = ((bf16[32,7,4,16,128]{4,3,2,1,0:T(8,128)(2,1)}), bf16[32,7,4,16,128]{4,3,2,1,0:T(8,128)(2,1)}, u32[]{:S(2)}, u32[]{:S(2)}) async-start(bf16[32,7,4,16,128]{4,3,2,1,0:T(8,128)(2,1)} %other_pairs.1), calls=%async_computation.1 | async-start | bytes 7340032 | tf_op jit(solution)/shard_map/all_to_all | solution.py:578
  166.3 2.0 collective-permute-done.19
  168.9 1.9 collective-permute-done.20
  171.3 2.4 collective-permute-start.22
  173.9 1.2 constant_dynamic-update-slice_fusion.1
  175.0 42.9 %collective-permute-done.22 = bf16[1,4,9,4,16,128]{5,4,3,2,1,0:T(8,128)(2,1)S(1)} collective-permute-done((bf16[1,4,9,4,16,128]{5,4,3,2,1,0:T(8,128)(2,1)S(1)}, bf16[1,4,9,4,16,128]{5,4,3,2,1,0:T(8,128)(2,1)S(1)}, u32[]{:S(2)}, u32[]{:S(2)}) %collective-permute-start.22) | collective-permute-done | bytes 589856 | tf_op jit(solution)/shard_map/ppermute | solution.py:429
  218.1 2.6 slice.41
  220.9 5.2 %reshape.313 = bf16[32,57344]{1,0:T(8,128)(2,1)} reshape(bf16[8,4,7,4,16,128]{5,4,3,2,1,0:T(8,128)(2,1)} %slice.41) | data formatting | bytes 7340032 | tf_op jit(solution)/shard_map/reshape | solution.py:593
  226.6 23.5 %all-to-all-done.1 = bf16[32,7,4,16,128]{4,3,2,1,0:T(8,128)(2,1)} async-done(((bf16[32,7,4,16,128]{4,3,2,1,0:T(8,128)(2,1)}), bf16[32,7,4,16,128]{4,3,2,1,0:T(8,128)(2,1)}, u32[]{:S(2)}, u32[]{:S(2)}) %all-to-all-start.1) | async-done | bytes 3670048 | tf_op jit(solution)/shard_map/all_to_all | solution.py:578
  250.1 5.6 %fusion = f32[32,32]{1,0:T(8,128)S(1)} fusion(bf16[32,57344]{1,0:T(8,128)(2,1)} %reshape.313, bf16[4,8,448,128]{3,2,1,0:T(8,128)(2,1)} %bitcast.30), kind=kOutput, calls=%fused_computation.5 | convolution fusion | flops 117440512 | bytes 7344128 | tf_op jit(solution)/shard_map/pe,qe->pq/dot_general | solution.py:595
  255.7 2.0 fusion.3
  258.8 9.9 %all_to_all.15 = f32[32,1,128]{2,1,0:T(1,128)S(1)} all-to-all(f32[32,1,128]{2,1,0:T(1,128)S(1)} %reshape.363), channel_id=1, replica_groups=mesh['grp'=4,'blk'=8] {'grp','blk'}, dimensions={0} | all-to-all | bytes 32768 | tf_op jit(solution)/shard_map/all_to_all | solution.py:578
  269.2 0.7 reduce
  (90 shorter events, 9.8 us)
Async XLA Ops:
  2.0 14.2 %collective-permute-start = (bf16[2,4,128,128]{3,2,1,0:T(8,128)(2,1)S(1)}, bf16[2,4,128,128]{3,2,1,0:T(8,128)(2,1)S(1)}, u32[]{:S(2)}, u32[]{:S(2)}) collective-permute-start(bf16[2,4,128,128]{3,2,1,0:T(8,128)(2,1)S(1)} %get-tuple-element.138), channel_id=1, source_target_pairs={{0,8},{8,0},{16,24},{24,16},{1,9},{9,1},{17,25},{25,17},{2,10},{10... | collective-permute-start | bytes 786440 | tf_op jit(solution)/shard_map/ppermute | solution.py:429
  5.1 21.4 %collective-permute-start.1 = (bf16[2,4,128,128]{3,2,1,0:T(8,128)(2,1)S(1)}, bf16[2,4,128,128]{3,2,1,0:T(8,128)(2,1)S(1)}, u32[]{:S(2)}, u32[]{:S(2)}) collective-permute-start(bf16[2,4,128,128]{3,2,1,0:T(8,128)(2,1)S(1)} %get-tuple-element.138), channel_id=1, source_target_pairs={{0,16},{8,24},{16,0},{24,8},{1,17},{9,25},{17,1},{25,9},{2,18},{10... | collective-permute-start | bytes 786440 | tf_op jit(solution)/shard_map/ppermute | solution.py:429
  7.7 18.8 %collective-permute-start.2 = (bf16[2,4,128,128]{3,2,1,0:T(8,128)(2,1)S(1)}, bf16[2,4,128,128]{3,2,1,0:T(8,128)(2,1)S(1)}, u32[]{:S(2)}, u32[]{:S(2)}) collective-permute-start(bf16[2,4,128,128]{3,2,1,0:T(8,128)(2,1)S(1)} %get-tuple-element.138), channel_id=1, source_target_pairs={{0,24},{8,16},{16,8},{24,0},{1,25},{9,17},{17,9},{25,1},{2,26},{10... | collective-permute-start | bytes 786440 | tf_op jit(solution)/shard_map/ppermute | solution.py:429
  12.3 17.4 %copy-start = (s32[16]{0:T(128)S(1)}, s32[16]{0:T(128)}, u32[]{:S(2)}) copy-start(s32[16]{0:T(128)} %owner_ref.9) | copy-start | bytes 196
  12.3 24.0 %copy-start.8 = (s32[8]{0:T(128)S(1)}, s32[8]{0:T(128)}, u32[]{:S(2)}) copy-start(s32[8]{0:T(128)} %param.11) | copy-start | bytes 100
  12.3 24.3 %copy-start.9 = (s32[8]{0:T(128)S(1)}, s32[8]{0:T(128)}, u32[]{:S(2)}) copy-start(s32[8]{0:T(128)} %param.13) | copy-start | bytes 100
  26.6 34.7 %copy-start.2 = (bf16[4,2,4,128,128]{4,3,2,1,0:T(8,128)(2,1)}, bf16[4,2,4,128,128]{4,3,2,1,0:T(8,128)(2,1)S(1)}, u32[]{:S(2)}) copy-start(bf16[4,2,4,128,128]{4,3,2,1,0:T(8,128)(2,1)S(1)} %pad_maximum_fusion.refs_0_) | copy-start | bytes 3145732
  26.6 34.6 %collective-permute-start.3 = (bf16[4,2,4,128,128]{4,3,2,1,0:T(8,128)(2,1)S(1)}, bf16[4,2,4,128,128]{4,3,2,1,0:T(8,128)(2,1)S(1)}, u32[]{:S(2)}, u32[]{:S(2)}) collective-permute-start(bf16[4,2,4,128,128]{4,3,2,1,0:T(8,128)(2,1)S(1)} %pad_maximum_fusion.refs_0_), channel_id=1, source_target_pairs={{0,1},{1,0},{2,3},{3,2},{4,5},{5,4},{6,7},{7,6},{8,9},{9,8},{10,11... | collective-permute-start | bytes 3145736 | tf_op jit(solution)/shard_map/ppermute | solution.py:429
  26.7 34.5 %collective-permute-start.4 = (bf16[4,2,4,128,128]{4,3,2,1,0:T(8,128)(2,1)S(1)}, bf16[4,2,4,128,128]{4,3,2,1,0:T(8,128)(2,1)S(1)}, u32[]{:S(2)}, u32[]{:S(2)}) collective-permute-start(bf16[4,2,4,128,128]{4,3,2,1,0:T(8,128)(2,1)S(1)} %pad_maximum_fusion.refs_0_), channel_id=1, source_target_pairs={{0,2},{1,3},{2,0},{3,1},{4,6},{5,7},{6,4},{7,5},{8,10},{9,11},{10,... | collective-permute-start | bytes 3145736 | tf_op jit(solution)/shard_map/ppermute | solution.py:429
  28.2 33.0 %collective-permute-start.5 = (bf16[4,2,4,128,128]{4,3,2,1,0:T(8,128)(2,1)S(1)}, bf16[4,2,4,128,128]{4,3,2,1,0:T(8,128)(2,1)}, u32[]{:S(2)}, u32[]{:S(2)}) collective-permute-start(bf16[4,2,4,128,128]{4,3,2,1,0:T(8,128)(2,1)S(1)} %pad_maximum_fusion.refs_0_), channel_id=1, source_target_pairs={{0,4},{1,5},{2,6},{3,7},{4,0},{5,1},{6,2},{7,3},{8,12},{9,13},{10,... | collective-permute-start | bytes 3145736 | tf_op jit(solution)/shard_map/ppermute | solution.py:429
  30.4 28.2 %collective-permute-start.6 = (bf16[4,128,512]{2,1,0:T(8,128)(2,1)}, bf16[4,128,512]{2,1,0:T(8,128)(2,1)}, u32[]{:S(2)}, u32[]{:S(2)}) collective-permute-start(bf16[4,128,512]{2,1,0:T(8,128)(2,1)} %picked_rows.4), channel_id=1, source_target_pairs={{0,8},{8,0},{16,24},{24,16},{1,9},{9,1},{17,25},{25,17},{2,10},{10... | collective-permute-start | bytes 1572872 | tf_op jit(solution)/shard_map/ppermute | solution.py:429
  35.3 25.9 %collective-permute-start.7 = (bf16[4,128,512]{2,1,0:T(8,128)(2,1)}, bf16[4,128,512]{2,1,0:T(8,128)(2,1)}, u32[]{:S(2)}, u32[]{:S(2)}) collective-permute-start(bf16[4,128,512]{2,1,0:T(8,128)(2,1)} %picked_rows.5), channel_id=1, source_target_pairs={{0,16},{8,24},{16,0},{24,8},{1,17},{9,25},{17,1},{25,9},{2,18},{10... | collective-permute-start | bytes 1572872 | tf_op jit(solution)/shard_map/ppermute | solution.py:429
  48.1 14.2 %copy-start.1 = (s32[16]{0:T(128)S(1)}, s32[16]{0:T(128)}, u32[]{:S(2)}) copy-start(s32[16]{0:T(128)} %owner_ref.9) | copy-start | bytes 196
  61.2 8.6 %copy-start.4 = (bf16[4,2,4,128,128]{4,3,2,1,0:T(8,128)(2,1)}, bf16[4,2,4,128,128]{4,3,2,1,0:T(8,128)(2,1)S(1)}, u32[]{:S(2)}) copy-start(bf16[4,2,4,128,128]{4,3,2,1,0:T(8,128)(2,1)S(1)} %collective-permute-done.3.refs_1_) | copy-start | bytes 3145732
  61.2 8.5 %copy-start.5 = (bf16[4,2,4,128,128]{4,3,2,1,0:T(8,128)(2,1)}, bf16[4,2,4,128,128]{4,3,2,1,0:T(8,128)(2,1)S(1)}, u32[]{:S(2)}) copy-start(bf16[4,2,4,128,128]{4,3,2,1,0:T(8,128)(2,1)S(1)} %collective-permute-done.4.refs_2_) | copy-start | bytes 3145732
  61.2 23.1 %collective-permute-start.10 = (bf16[4,2,4,128,128]{4,3,2,1,0:T(8,128)(2,1)S(1)}, bf16[4,2,4,128,128]{4,3,2,1,0:T(8,128)(2,1)}, u32[]{:S(2)}, u32[]{:S(2)}) collective-permute-start(bf16[4,2,4,128,128]{4,3,2,1,0:T(8,128)(2,1)S(1)} %pad_maximum_fusion.refs_0_), channel_id=1, source_target_pairs={{0,6},{1,7},{2,4},{3,5},{4,2},{5,3},{6,0},{7,1},{8,14},{9,15},{10,... | collective-permute-start | bytes 3145736 | tf_op jit(solution)/shard_map/ppermute | solution.py:429
  61.8 22.6 %collective-permute-start.8 = (bf16[4,2,4,128,128]{4,3,2,1,0:T(8,128)(2,1)S(1)}, bf16[4,2,4,128,128]{4,3,2,1,0:T(8,128)(2,1)}, u32[]{:S(2)}, u32[]{:S(2)}) collective-permute-start(bf16[4,2,4,128,128]{4,3,2,1,0:T(8,128)(2,1)S(1)} %collective-permute-done.4.refs_2_), channel_id=1, source_target_pairs={{0,1},{1,0},{2,3},{3,2},{4,5},{5,4},{6,7},{7,6},{8,9},{9,8},{10,11... | collective-permute-start | bytes 3145736 | tf_op jit(solution)/shard_map/ppermute | solution.py:429
  61.8 22.6 %collective-permute-start.9 = (bf16[4,2,4,128,128]{4,3,2,1,0:T(8,128)(2,1)}, bf16[4,2,4,128,128]{4,3,2,1,0:T(8,128)(2,1)}, u32[]{:S(2)}, u32[]{:S(2)}) collective-permute-start(bf16[4,2,4,128,128]{4,3,2,1,0:T(8,128)(2,1)} %collective-permute-done.5.refs_4_), channel_id=1, source_target_pairs={{0,1},{1,0},{2,3},{3,2},{4,5},{5,4},{6,7},{7,6},{8,9},{9,8},{10,11... | collective-permute-start | bytes 3145736 | tf_op jit(solution)/shard_map/ppermute | solution.py:429
  63.1 21.2 %collective-permute-start.11 = (bf16[4,128,512]{2,1,0:T(8,128)(2,1)}, bf16[4,128,512]{2,1,0:T(8,128)(2,1)}, u32[]{:S(2)}, u32[]{:S(2)}) collective-permute-start(bf16[4,128,512]{2,1,0:T(8,128)(2,1)} %picked_rows.6), channel_id=1, source_target_pairs={{0,8},{8,0},{16,24},{24,16},{1,9},{9,1},{17,25},{25,17},{2,10},{10... | collective-permute-start | bytes 1572872 | tf_op jit(solution)/shard_map/ppermute | solution.py:429
  65.5 16.9 %collective-permute-start.12 = (bf16[10,128,128]{2,1,0:T(8,128)(2,1)}, bf16[10,128,128]{2,1,0:T(8,128)(2,1)}, u32[]{:S(2)}, u32[]{:S(2)}) collective-permute-start(bf16[10,128,128]{2,1,0:T(8,128)(2,1)} %picked_square.3), channel_id=1, source_target_pairs={{0,16},{8,24},{16,0},{24,8},{1,17},{9,25},{17,1},{25,9},{2,18},{10... | collective-permute-start | bytes 983048 | tf_op jit(solution)/shard_map/ppermute | solution.py:429
  77.7 11.2 %copy-start.7 = (bf16[10,128,128]{2,1,0:T(8,128)(2,1)S(1)}, bf16[10,128,128]{2,1,0:T(8,128)(2,1)}, u32[]{:S(2)}) copy-start(bf16[10,128,128]{2,1,0:T(8,128)(2,1)} %picked_square.5) | copy-start | bytes 983044
  84.4 6.0 %collective-permute-start.13 = (bf16[4,2,4,128,128]{4,3,2,1,0:T(8,128)(2,1)}, bf16[4,2,4,128,128]{4,3,2,1,0:T(8,128)(2,1)S(1)}, u32[]{:S(2)}, u32[]{:S(2)}) collective-permute-start(bf16[4,2,4,128,128]{4,3,2,1,0:T(8,128)(2,1)} %collective-permute-done.10.refs_6_), channel_id=1, source_target_pairs={{0,1},{1,0},{2,3},{3,2},{4,5},{5,4},{6,7},{7,6},{8,9},{9,8},{10,11... | collective-permute-start | bytes 3145736 | tf_op jit(solution)/shard_map/ppermute | solution.py:429
  84.5 43.6 %collective-permute-start.16 = (bf16[2,4,9,4,16,128]{5,4,3,2,1,0:T(8,128)(2,1)}, bf16[2,4,9,4,16,128]{5,4,3,2,1,0:T(8,128)(2,1)S(1)}, u32[]{:S(2)}, u32[]{:S(2)}) collective-permute-start(bf16[2,4,9,4,16,128]{5,4,3,2,1,0:T(8,128)(2,1)} %get-tuple-element.116), channel_id=1, source_target_pairs={{0,2},{1,3},{2,0},{3,1},{4,6},{5,7},{6,4},{7,5},{8,10},{9,11},{10,... | collective-permute-start | bytes 3538952 | tf_op jit(solution)/shard_map/ppermute | solution.py:429
  86.0 42.1 %collective-permute-start.17 = (bf16[2,4,9,4,16,128]{5,4,3,2,1,0:T(8,128)(2,1)}, bf16[2,4,9,4,16,128]{5,4,3,2,1,0:T(8,128)(2,1)S(1)}, u32[]{:S(2)}, u32[]{:S(2)}) collective-permute-start(bf16[2,4,9,4,16,128]{5,4,3,2,1,0:T(8,128)(2,1)} %get-tuple-element.117), channel_id=1, source_target_pairs={{0,4},{1,5},{2,6},{3,7},{4,0},{5,1},{6,2},{7,3},{8,12},{9,13},{10,... | collective-permute-start | bytes 3538952 | tf_op jit(solution)/shard_map/ppermute | solution.py:429
  87.5 18.5 %collective-permute-start.14 = (bf16[10,128,128]{2,1,0:T(8,128)(2,1)}, bf16[10,128,128]{2,1,0:T(8,128)(2,1)}, u32[]{:S(2)}, u32[]{:S(2)}) collective-permute-start(bf16[10,128,128]{2,1,0:T(8,128)(2,1)} %picked_square.4), channel_id=1, source_target_pairs={{0,8},{8,0},{16,24},{24,16},{1,9},{9,1},{17,25},{25,17},{2,10},{10... | collective-permute-start | bytes 983048 | tf_op jit(solution)/shard_map/ppermute | solution.py:429
  88.8 17.2 %collective-permute-start.15 = (bf16[10,128,128]{2,1,0:T(8,128)(2,1)S(1)}, bf16[10,128,128]{2,1,0:T(8,128)(2,1)}, u32[]{:S(2)}, u32[]{:S(2)}) collective-permute-start(bf16[10,128,128]{2,1,0:T(8,128)(2,1)S(1)} %copy-done.7), channel_id=1, source_target_pairs={{0,24},{8,16},{16,8},{24,0},{1,25},{9,17},{17,9},{25,1},{2,26},{10... | collective-permute-start | bytes 983048 | tf_op jit(solution)/shard_map/ppermute | solution.py:429
  90.4 1.4 copy-start.6
  90.4 37.7 %collective-permute-start.18 = (bf16[1,4,9,4,16,128]{5,4,3,2,1,0:T(8,128)(2,1)}, bf16[1,4,9,4,16,128]{5,4,3,2,1,0:T(8,128)(2,1)}, u32[]{:S(2)}, u32[]{:S(2)}) collective-permute-start(bf16[1,4,9,4,16,128]{5,4,3,2,1,0:T(8,128)(2,1)} %get-tuple-element.118), channel_id=1, source_target_pairs={{0,6},{1,7},{2,4},{3,5},{4,2},{5,3},{6,0},{7,1},{8,14},{9,15},{10,... | collective-permute-start | bytes 1769480 | tf_op jit(solution)/shard_map/ppermute | solution.py:429
  128.1 31.7 %all-to-all-start = ((bf16[32,2,4,16,128]{4,3,2,1,0:T(8,128)(2,1)}), bf16[32,2,4,16,128]{4,3,2,1,0:T(8,128)(2,1)}, u32[]{:S(2)}, u32[]{:S(2)}) async-start(bf16[32,2,4,16,128]{4,3,2,1,0:T(8,128)(2,1)} %get-tuple-element.120), calls=%async_computation | async-start | bytes 2097152 | tf_op jit(solution)/shard_map/all_to_all | solution.py:578
  159.9 6.1 %copy-start.3 = (bf16[2,4,9,4,16,128]{5,4,3,2,1,0:T(8,128)(2,1)S(1)}, bf16[2,4,9,4,16,128]{5,4,3,2,1,0:T(8,128)(2,1)}, u32[]{:S(2)}) copy-start(bf16[2,4,9,4,16,128]{5,4,3,2,1,0:T(8,128)(2,1)} %get-tuple-element.123) | copy-start | bytes 3538948
  159.9 90.2 %all-to-all-start.1 = ((bf16[32,7,4,16,128]{4,3,2,1,0:T(8,128)(2,1)}), bf16[32,7,4,16,128]{4,3,2,1,0:T(8,128)(2,1)}, u32[]{:S(2)}, u32[]{:S(2)}) async-start(bf16[32,7,4,16,128]{4,3,2,1,0:T(8,128)(2,1)} %other_pairs.1), calls=%async_computation.1 | async-start | bytes 7340032 | tf_op jit(solution)/shard_map/all_to_all | solution.py:578
  165.9 5.4 %copy-start.10 = (bf16[1,4,9,4,16,128]{5,4,3,2,1,0:T(8,128)(2,1)S(1)}, bf16[1,4,9,4,16,128]{5,4,3,2,1,0:T(8,128)(2,1)}, u32[]{:S(2)}) copy-start(bf16[1,4,9,4,16,128]{5,4,3,2,1,0:T(8,128)(2,1)} %get-tuple-element.127) | copy-start | bytes 1769476
  166.2 2.1 collective-permute-start.19
  168.7 2.1 collective-permute-start.20
  171.1 2.6 collective-permute-start.21
  171.3 46.6 %collective-permute-start.22 = (bf16[1,4,9,4,16,128]{5,4,3,2,1,0:T(8,128)(2,1)S(1)}, bf16[1,4,9,4,16,128]{5,4,3,2,1,0:T(8,128)(2,1)S(1)}, u32[]{:S(2)}, u32[]{:S(2)}) collective-permute-start(bf16[1,4,9,4,16,128]{5,4,3,2,1,0:T(8,128)(2,1)S(1)} %copy-done.10), channel_id=1, source_target_pairs={{0,7},{1,6},{2,5},{3,4},{4,3},{5,2},{6,1},{7,0},{8,15},{9,14},{10,... | collective-permute-start | bytes 1769480 | tf_op jit(solution)/shard_map/ppermute | solution.py:429

commit v4 on v3

--- a/solution.py
+++ b/solution.py
@@ -8,9 +8,10 @@
 from jax.sharding import PartitionSpec as P
 
 NT = 16
-CHUNKS = ((0, NT // 2), (1, 2, 3, 4, 5, 6, 7))
+CHUNKS = ((0, NT // 2, 1), (2, 3, 4, 5, 6, 7))
 OFFSETS = CHUNKS[0] + CHUNKS[1]
 PARTS = ((0, 1), (2, 3), (4, 5), (6,), (7,))
+UNROLL = 4
 VMEM_BYTES = 60 * 1024 * 1024
 
 
@@ -174,17 +175,80 @@
     return sum(jnp.where(i == at, offset, 0) for at, offset in enumerate(OFFSETS))
 
 
+def strips_of(columns, offsets):
+    return sum(
+        columns * 3 // 4 if d == 0 else columns // 2 if d == NT // 2 else columns for d in offsets
+    )
+
+
+def diagonal_strips(tiles, turned):
+    rows, lanes = tiles[0].shape[-2] // 2, tiles[0].shape[-1] // 2
+    shape = tiles[0].shape[:-2] + (rows, 2 * lanes)
+    left = lax.broadcasted_iota(jnp.int32, shape, len(shape) - 1) < lanes
+    kept, rest = [], []
+    for c in range(0, len(tiles), 2):
+        lower, upper = tiles[c][..., rows:, :], tiles[c + 1][..., :rows, :]
+        if turned:
+            lower = lower + jnp.where(left, tiles[c].T[rows:, :], 0)
+            upper = upper + jnp.where(left, 0, tiles[c + 1].T[:rows, :])
+        kept += [lower, upper]
+        rest.append(jnp.where(left, tiles[c][..., :rows, :], tiles[c + 1][..., rows:, :]))
+    halves = kept + rest
+    return [
+        jnp.concatenate(halves[at : at + 2], axis=-2) for at in range(0, len(halves), 2)
+    ]
+
+
 def pair_kernel(columns, where_ref, owner_ref, mask_ref, *refs):
-    inputs, out_refs = refs[:columns], refs[columns:]
-    rows = out_refs[0].shape[4]
+    inputs, out_refs, whole = refs[:columns], refs[columns:-1], refs[-1]
+    rows, tile = out_refs[0].shape[3:]
+    aux_local = out_refs[0].shape[1]
     first = where_ref[0] * columns
-    for c in range(columns):
-        tile_row = owner_ref[lax.rem(first + c + offset_at(pl.program_id(0)), NT)]
-        kept = place((owner_ref, mask_ref), tile_row, first + c)
+    step = pl.program_id(0)
+
+    def tiles():
+        for c in range(columns):
+            tile_row = owner_ref[lax.rem(first + c + offset_at(step), NT)]
+            kept = place((owner_ref, mask_ref), tile_row, first + c)
+            yield masked_tile(inputs[c][:, 0], kept)
+
+    def write(strip, values):
+        whole[...] = values
         for out_ref, some in zip(out_refs, PARTS):
             for at, part in enumerate(some):
                 start = pl.multiple_of((part ^ where_ref[1]) * rows, rows)
-                out_ref[at, :, 0, c] = masked_tile(inputs[c][:, 0, pl.ds(start, rows), :], kept)
+                out_ref[at, :, strip] = whole[:, pl.ds(start, rows), :]
+
+    @pl.when(step == 0)
+    def _():
+        for strip, values in enumerate(diagonal_strips(list(tiles()), False)):
+            write(strip, values)
+
+    @pl.when(step == 1)
+    def _():
+        half = tile // 2
+        late = jnp.full((half, tile), first, jnp.int32) >= NT // 2
+        halves = []
+        for each in tiles():
+            halves.append(
+                jnp.stack(
+                    [
+                        jnp.where(late, each[at].T[half:], each[at][:half])
+                        for at in range(aux_local)
+                    ]
+                )
+            )
+        for at in range(0, columns, 2):
+            write(
+                strips_of(columns, (0,)) + at // 2,
+                jnp.concatenate(halves[at : at + 2], axis=1),
+            )
+
+    @pl.when(step > 1)
+    def _():
+        strip = strips_of(columns, OFFSETS[:2]) + (step - 2) * columns
+        for c, values in enumerate(tiles()):
+            write(strip + c, values)
 
 
 def pair_tiles(scalars, integrals, parts):
@@ -192,6 +256,9 @@
     tile = basis_size // NT
     columns = width // tile
     rows = tile // parts
+    shapes = [
+        (len(some), aux_local, strips_of(columns, OFFSETS), rows, tile) for some in PARTS
+    ]
 
     def row_map(c):
         def index(d, where, owner, mask):
@@ -207,20 +274,10 @@
             in_specs=[
                 pl.BlockSpec((aux_local, 1, tile, tile), row_map(c)) for c in range(columns)
             ],
-            out_specs=[
-                pl.BlockSpec(
-                    (len(some), aux_local, 1, columns, rows, tile),
-                    lambda d, *_: (0, 0, d, 0, 0, 0),
-                )
-                for some in PARTS
-            ],
+            out_specs=[pl.BlockSpec(shape, lambda d, *_: (0, 0, 0, 0, 0)) for shape in shapes],
+            scratch_shapes=[pltpu.VMEM((aux_local, tile, tile), jnp.bfloat16)],
         ),
-        out_shape=[
-            jax.ShapeDtypeStruct(
-                (len(some), aux_local, len(OFFSETS), columns, rows, tile), jnp.bfloat16
-            )
-            for some in PARTS
-        ],
+        out_shape=[jax.ShapeDtypeStruct(shape, jnp.bfloat16) for shape in shapes],
         compiler_params=pltpu.CompilerParams(vmem_limit_bytes=VMEM_BYTES),
         cost_estimate=pl.CostEstimate(flops=0, bytes_accessed=0, transcendentals=0),
         name="pair_tiles",
@@ -251,8 +308,7 @@
     return copies
 
 
-def occupied_columns(kcount, column_blocks, slot_ref, tile_ref, block_refs, green, full, half):
-    tile = green.shape[1]
+def column_planes(column_blocks, block_refs, tile, full):
     width = full.shape[1] // len(column_blocks)
     columns = width // tile
     for at, blocks in enumerate(column_blocks):
@@ -272,30 +328,33 @@
                 values.T if turned else values
             )
 
-    @pl.loop(0, NT)
+
+def occupied_rows(kcount, count, width, slot_ref, tile_ref, green, full, half, first, start, stop):
+    tile = green.shape[1]
+    columns = width // tile
+
+    @pl.loop(start, stop, unroll=UNROLL)
     def _(r):
         left = jnp.concatenate([green[tile_ref[r * kcount + k]] for k in range(kcount)], axis=1)
         starts = [pl.multiple_of(slot_ref[r * kcount + k] * tile, tile) for k in range(kcount)]
         rows = pl.ds(pl.multiple_of(r * tile, tile), tile)
-        for at in range(len(column_blocks)):
+        for at in range(count):
             right = jnp.concatenate(
                 [full[pl.ds(start, tile), at * width : (at + 1) * width] for start in starts],
                 axis=0,
             )
-            values = jnp.dot(left, right, preferred_element_type=jnp.float32)
-            values = values.astype(jnp.bfloat16)
+            values = jnp.dot(left, right, preferred_element_type=jnp.float32).astype(jnp.bfloat16)
             for c in range(columns):
-                half[at * columns + c, rows, :] = values[:, c * tile : (c + 1) * tile]
+                half[first + at * columns + c, rows, :] = values[:, c * tile : (c + 1) * tile]
 
 
 def folded_pairs(kcount, columns, offsets, group, slot_ref, tile_ref, green, half, folded, out_ref):
     tile = green.shape[1]
-    folded[...] = jnp.zeros_like(folded)
     pieces = [(at, d, False) for at, d in enumerate(offsets)]
     pieces += [(at, NT - d, True) for at, d in enumerate(offsets) if 0 < d < NT // 2]
-
-    @pl.loop(0, NT)
-    def _(s):
+    middle = offsets.index(NT // 2) if NT // 2 in offsets else None
+
+    def column(s, late):
         right = jnp.concatenate([green[tile_ref[s * kcount + k]] for k in range(kcount)], axis=0)
         slots = [slot_ref[s * kcount + k] for k in range(kcount)]
         for first in range(0, len(pieces), 4):
@@ -313,31 +372,66 @@
             )
             for place_at, ((at, _, turned), r) in enumerate(zip(some, rows)):
                 piece = values[place_at * tile : (place_at + 1) * tile]
-                if turned:
+                if turned or (at == middle and late):
                     folded[r, at] += piece.T
                 else:
                     folded[s, at] += piece
 
-    rows = out_ref.shape[3]
+    if middle is None:
+        pl.loop(0, NT, unroll=UNROLL)(lambda s: column(s, False))
+    else:
+        pl.loop(0, NT // 2, unroll=UNROLL)(lambda s: column(s, False))
+        pl.loop(NT // 2, NT, unroll=UNROLL)(lambda s: column(s, True))
+
+    rows = out_ref.shape[2]
     parts = tile // rows
 
     @pl.loop(0, NT // columns)
     def _(plane):
-        @pl.loop(0, columns)
-        def _(c):
-            for at in range(len(offsets)):
-                values = folded[plane * columns + c, at].astype(jnp.bfloat16)
-                for part in range(parts):
-                    out_ref[plane * parts + part, at, c] = values[part * rows : (part + 1) * rows]
+        first = plane * columns
+        strips = []
+        for at, d in enumerate(offsets):
+            if d == 0:
+                strips += diagonal_strips([folded[first + c, at] for c in range(columns)], True)
+            elif d == NT // 2:
+                half_rows = pl.ds(
+                    pl.multiple_of(first // (NT // 2) * (tile // 2), tile // 2), tile // 2
+                )
+                halves = [
+                    folded[lax.rem(first + c, NT // 2), at, half_rows] for c in range(columns)
+                ]
+                strips += [
+                    jnp.concatenate(halves[c : c + 2], axis=0) for c in range(0, columns, 2)
+                ]
+            else:
+                strips += [folded[first + c, at] for c in range(columns)]
+        for strip, values in enumerate(strips):
+            values = values.astype(jnp.bfloat16)
+            for part in range(parts):
+                out_ref[plane * parts + part, strip] = values[part * rows : (part + 1) * rows]
 
 
 def early_kernel(kcount, column_blocks, parts, slot_ref, tile_ref, *refs):
     green_refs, refs = refs[:parts], refs[parts:]
-    block_refs, (half_ref, green, full, sems) = refs[:-4], refs[-4:]
+    block_refs, (out_ref, green, full, half, sems, out_sems) = refs[:-6], refs[-6:]
+    width = full.shape[1] // len(column_blocks)
     copies = green_copies(green_refs, 0, green, sems)
     start_all(copies)
+    column_planes(column_blocks, block_refs, green.shape[1], full)
     wait_all(copies)
-    occupied_columns(kcount, column_blocks, slot_ref, tile_ref, block_refs, green, full, half_ref)
+    copies = []
+    rows = half.shape[1] // 2
+    for at in range(2):
+        occupied_rows(
+            kcount, len(column_blocks), width, slot_ref, tile_ref, green, full, half, 0,
+            at * NT // 2, (at + 1) * NT // 2,
+        )
+        some = pl.ds(at * rows, rows)
+        copies.append(
+            pltpu.make_async_copy(half.at[:, some], out_ref.at[:, some], out_sems.at[at])
+        )
+        copies[-1].start()
+    wait_all(copies)
 
 
 def last_kernel(
@@ -345,24 +439,47 @@
     virtual_tile_ref, *refs
 ):
     green_refs, refs = refs[:parts], refs[parts:]
-    held_ref, refs = refs[0], refs[1:]
-    block_refs, refs = refs[:-9], refs[-9:]
-    out_ref, half_ref, green, virtual, full, half, folded, sems, others = refs
+    held_ref, own_ref, refs = refs[0], refs[1], refs[2:]
+    block_refs, refs = refs[:-11], refs[-11:]
+    (
+        out_ref, new_ref, green, virtual, full, half, folded, own, sems, others, own_sems
+    ) = refs
+    count = held_ref.shape[0]
+    width = full.shape[1] // len(column_blocks)
+    own_copies = [
+        pltpu.make_async_copy(
+            own_ref.at[pl.ds((2 * at + 1) * columns, columns)],
+            own.at[pl.ds(at * columns, columns)],
+            own_sems.at[at],
+        )
+        for at in range(len(column_blocks))
+    ]
+    start_all(own_copies)
     copies = green_copies(green_refs, 0, green, sems)
+    start_all(copies)
+    folded[...] = jnp.zeros_like(folded)
+    wait_all(own_copies)
+    column_planes(column_blocks, (own, *block_refs), green.shape[1], full)
+    wait_all(copies)
+    last = others.shape[0] - 1
     later = green_copies(green_refs, 1, virtual, others)
-    count = held_ref.shape[0]
     later.append(
-        pltpu.make_async_copy(held_ref, half.at[pl.ds(0, count)], others.at[others.shape[0] - 1])
-    )
-    start_all(copies + later)
-    wait_all(copies)
-    occupied_columns(kcount, column_blocks, slot_ref, tile_ref, block_refs, green, full, half_ref)
+        pltpu.make_async_copy(held_ref, half.at[pl.ds(0, count)], others.at[last - 1])
+    )
+    start_all(later)
+    occupied_rows(
+        kcount, len(column_blocks), width, slot_ref, tile_ref, green, full, half, count, 0, NT
+    )
+    kept = pltpu.make_async_copy(
+        half.at[pl.ds(count, new_ref.shape[0])], new_ref, others.at[last]
+    )
+    kept.start()
     wait_all(later)
-    half[count:] = half_ref[...]
     folded_pairs(
         kcount, columns, offsets, group_ref[0], half_slot_ref, virtual_tile_ref, virtual, half,
         folded, out_ref,
     )
+    kept.wait()
 
 
 def rest_kernel(
@@ -372,14 +489,13 @@
     held_ref, new_ref, out_ref, virtual, half, folded, others = refs
     copies = green_copies(green_refs, 1, virtual, others)
     count = held_ref.shape[0]
-    last = others.shape[0] - 2
-    copies.append(pltpu.make_async_copy(held_ref, half.at[pl.ds(0, count)], others.at[last]))
+    last = others.shape[0] - 1
+    copies.append(pltpu.make_async_copy(held_ref, half.at[pl.ds(0, count)], others.at[last - 1]))
     copies.append(
-        pltpu.make_async_copy(
-            new_ref, half.at[pl.ds(count, new_ref.shape[0])], others.at[last + 1]
-        )
+        pltpu.make_async_copy(new_ref, half.at[pl.ds(count, new_ref.shape[0])], others.at[last])
     )
     start_all(copies)
+    folded[...] = jnp.zeros_like(folded)
     wait_all(copies)
     folded_pairs(
         kcount, columns, offsets, group_ref[0], half_slot_ref, virtual_tile_ref, virtual, half,
@@ -387,13 +503,15 @@
     )
 
 
-def kernel_call(kernel, tables, anywhere, blocks, out_shape, scratch_shapes, name, flops=0):
+def kernel_call(
+    kernel, tables, anywhere, blocks, out_shape, out_spaces, scratch_shapes, name, flops=0
+):
     return pl.pallas_call(
         kernel,
         in_specs=[pl.BlockSpec(memory_space=pltpu.SMEM)] * len(tables)
         + [pl.BlockSpec(memory_space=pl.ANY)] * len(anywhere)
         + [pl.BlockSpec(memory_space=pltpu.VMEM)] * len(blocks),
-        out_specs=jax.tree.map(lambda _: pl.BlockSpec(memory_space=pltpu.VMEM), out_shape),
+        out_specs=[pl.BlockSpec(memory_space=space) for space in out_spaces],
         out_shape=out_shape,
         scratch_shapes=scratch_shapes,
         compiler_params=pltpu.CompilerParams(vmem_limit_bytes=VMEM_BYTES),
@@ -513,7 +631,7 @@
     def folded(offsets):
         return (
             jax.ShapeDtypeStruct(
-                (devices, len(offsets), columns, tile // parts, tile), jnp.bfloat16
+                (devices, strips_of(columns, offsets), tile // parts, tile), jnp.bfloat16
             ),
             vmem(NT, len(offsets), tile, tile, dtype=jnp.float32),
         )
@@ -522,48 +640,61 @@
         tuple((0, plane, False) for plane in range(planes)),
         ((0, 2, True), (1, 0, True), (3, None, False), (2, 0, False)),
     )
-    first = kernel_call(
+    (first,) = kernel_call(
         functools.partial(early_kernel, kcount, column_blocks, len(greens)),
         occupied_table,
         greens,
         (own, near_two, across_off, across),
-        half(2),
-        [green, full(2), pltpu.SemaphoreType.DMA((devices,))],
+        [half(2)],
+        [pl.ANY],
+        [
+            green,
+            full(2),
+            vmem(2 * columns, basis_size, tile),
+            pltpu.SemaphoreType.DMA((devices,)),
+            pltpu.SemaphoreType.DMA((2,)),
+        ],
         "early_half",
         flops=2 * basis_size * kcount * tile * 2 * width * 2,
     )
     first, near, far = lax.optimization_barrier((first, near, far))
     column_blocks = (
-        ((0, 1, True), (4, None, False), (1, 0, False), (2, 0, False)),
-        ((0, 3, True), (2, 0, True), (3, 0, True), (5, None, False)),
+        ((0, 0, True), (4, None, False), (1, 0, False), (2, 0, False)),
+        ((0, 1, True), (2, 0, True), (3, 0, True), (5, None, False)),
     )
     out_shape, scratch = folded(CHUNKS[0])
     sent, second = kernel_call(
         functools.partial(last_kernel, kcount, columns, column_blocks, CHUNKS[0], len(greens)),
         (where,) + occupied_table + virtual_table,
-        [*greens, first],
-        (own, near_two, near_three, across_off, near, far),
-        (out_shape, half(2)),
+        [*greens, first, own],
+        (near_two, near_three, across_off, near, far),
+        [out_shape, half(2)],
+        [pltpu.VMEM, pl.ANY],
         [
             green,
             green,
             full(2),
             vmem(NT, basis_size, tile),
             scratch,
+            vmem(2 * columns, tile, width),
             pltpu.SemaphoreType.DMA((devices,)),
-            pltpu.SemaphoreType.DMA((devices + 1,)),
+            pltpu.SemaphoreType.DMA((devices + 2,)),
+            pltpu.SemaphoreType.DMA((2,)),
         ],
         "last_half_and_pairs",
     )
-    sent, second, pairs = lax.optimization_barrier((sent, second, pairs))
+    sent, second, pairs[:3], pairs[4] = lax.optimization_barrier(
+        (sent, second, pairs[:3], pairs[4])
+    )
     pairs[4] = swap(pairs[4], "blk", parts, 7)
     out_shape, scratch = folded(CHUNKS[1])
-    rest = kernel_call(
+    (rest,) = kernel_call(
         functools.partial(rest_kernel, kcount, columns, CHUNKS[1], len(greens)),
         (where,) + virtual_table,
         [*greens, first, second],
         (),
-        out_shape,
+        [out_shape],
+        [pltpu.VMEM],
         [
             green,
             vmem(NT, basis_size, tile),
@@ -571,14 +702,14 @@
             pltpu.SemaphoreType.DMA((devices + 2,)),
         ],
         "other_pairs",
-        flops=2 * 14 * basis_size * kcount * tile * tile * 2,
+        flops=2 * 12 * basis_size * kcount * tile * tile * 2,
     )
 
     def everyone(values):
         return lax.all_to_all(values, ("grp", "blk"), split_axis=0, concat_axis=0, tiled=True)
 
     sent = everyone(sent)
-    sent, rest = lax.optimization_barrier((sent, rest))
+    sent, rest, pairs[3] = lax.optimization_barrier((sent, rest, pairs[3]))
     rest = everyone(rest)
     pairs = [
         each
@@ -590,8 +721,9 @@
     partial_sum = 0.0
     at = 0
     for offsets, each in zip(CHUNKS, (sent, rest)):
-        theirs = pairs[:, :, at : at + len(offsets)].reshape(parts * aux_local, -1)
-        at += len(offsets)
+        count = strips_of(columns, offsets)
+        theirs = pairs[:, :, at : at + count].reshape(parts * aux_local, -1)
+        at += count
         partial_sum = partial_sum + jnp.einsum(
             "pe,qe->pq", each.reshape(devices, -1), theirs, preferred_element_type=jnp.float32
         )
@@ -610,7 +742,7 @@
     def body(*args):
         aux_local, basis_size, width = args[0].shape
         tile = basis_size // NT
-        fits = aux_local == planes == 4 and parts == 8 and width % tile == 0 and tile % (16 * parts) == 0
+        fits = aux_local == planes == 4 and parts == 8 and width % tile == 0 and tile % (16 * parts) == 0 and width == 4 * tile
         return (folded_body if fits else general_body)(*args)
 
     in_specs = (

time: 272 us -> 255 us (0.938)
  Pallas kernels: 93.8 us -> 81.3 us
  waiting for transfers between devices: 95.7 us -> 92.7 us
    pallas_call x3, Pallas kernels: 64.2 us -> 50.8 us  [kernel_call(): pl.pallas_call(kernel, in_specs=[pl.BlockSpec(memory_space=pltpu.SMEM)] *...]
    unnamed x28 -> x38, local copies, waits for them, and re-layouts: 1.69 us -> 5.33 us
    all_to_all x2, waiting for transfers between devices: 23.5 us -> 19.9 us  [everyone(): lax.all_to_all(values, ('grp', 'blk'), split_axis=0, concat_axis=0, tiled...]
  transfers between devices with their start and end apart: 25 -> 25, of which waited for: 10 -> 12; matrix products, arithmetic and copies ran while one was open for 7% -> 7% of each run, Pallas kernels for 35% -> 32%
where the time goes in v4:
time: 255 us; the launch traced here: 254 us
  waiting for transfers between devices  92.7 us (36%)
  Pallas kernels  81.3 us (32%)
  starting transfers between devices  38.3 us (15%)
  local copies, waits for them, and re-layouts  21.6 us (8%)
  blocking collectives  9.95 us (4%)
  matrix products  5.61 us (2%)
  other arithmetic  3.99 us (2%)
    ppermute x23, waiting for transfers between devices, swap(): lax.ppermute(values, axis, [(at, at ^ distance) for at in range(size)])  72.7 us
    pallas_call x3, Pallas kernels, kernel_call(): pl.pallas_call(kernel, in_specs=[pl.BlockSpec(memory_space=pltpu.SMEM)] *...  50.8 us
    ppermute x23, starting transfers between devices, swap(): lax.ppermute(values, axis, [(at, at ^ distance) for at in range(size)])  30.7 us
    all_to_all x2, waiting for transfers between devices, everyone(): lax.all_to_all(values, ('grp', 'blk'), split_axis=0, concat_axis=0, tiled...  19.9 us
    pallas_call x4, Pallas kernels, picked_rows(): pl.pallas_call(functools.partial(picked_kernel, columns, planes_of), grid...  13.1 us
    all_to_all x1, blocking collectives, everyone(): lax.all_to_all(values, ('grp', 'blk'), split_axis=0, concat_axis=0, tiled...  9.95 us
    pallas_call x1, Pallas kernels, pair_tiles(): pl.pallas_call(functools.partial(pair_kernel, columns), grid_spec=pltpu.P...  9.63 us
    pallas_call x3, Pallas kernels, picked_square(): pl.pallas_call(functools.partial(picked_square_kernel, columns), grid_spe...  7.8 us
  transfers between devices with their start and end apart: 25, of which 12 were waited for; matrix products, arithmetic and copies ran while one was open for 7% of the time, Pallas kernels for 32%

profile of v4, /device:TPU:0, one launch (start us, length us, event | category | flops | bytes accessed | tf_op | source)
XLA Modules:
  0.0 253.9 jit_solution(17222762766283046480)
XLA Ops:
  0.0 1.0 copy.19
  2.0 3.1 %collective-permute-start = (bf16[2,4,128,128]{3,2,1,0:T(8,128)(2,1)S(1)}, bf16[2,4,128,128]{3,2,1,0:T(8,128)(2,1)S(1)}, u32[]{:S(2)}, u32[]{:S(2)}) collective-permute-start(bf16[2,4,128,128]{3,2,1,0:T(8,128)(2,1)S(1)} %get-tuple-element.138), channel_id=1, source_target_pairs={{0,8},{8,0},{16,24},{24,16},{1,9},{9,1},{17,25},{25,17},{2,10},{10... | collective-permute-start | bytes 786440 | tf_op jit(solution)/shard_map/ppermute | solution.py:547
  5.1 2.6 %collective-permute-start.1 = (bf16[2,4,128,128]{3,2,1,0:T(8,128)(2,1)S(1)}, bf16[2,4,128,128]{3,2,1,0:T(8,128)(2,1)S(1)}, u32[]{:S(2)}, u32[]{:S(2)}) collective-permute-start(bf16[2,4,128,128]{3,2,1,0:T(8,128)(2,1)S(1)} %get-tuple-element.138), channel_id=1, source_target_pairs={{0,16},{8,24},{16,0},{24,8},{1,17},{9,25},{17,1},{25,9},{2,18},{10... | collective-permute-start | bytes 786440 | tf_op jit(solution)/shard_map/ppermute | solution.py:547
  7.7 1.3 reshape.306.mask_ref
  9.6 2.7 %picked_rows.4 = bf16[4,128,512]{2,1,0:T(8,128)(2,1)} custom-call(s32[2]{0:T(128)} %pad_add_fusion.where_ref.group_ref, s32[16]{0:T(128)} %owner_ref.9, s32[256]{0:T(256)} %reshape.306.mask_ref, bf16[4,16,128,512]{3,2,1,0:T(8,128)(2,1)} %bitcast.58, bf16[4,16,128,512]{3,2,1,0:T(8,128)(2,1)} %bitcast.59, bf16[4,16,128,512]{3,2,1,0:T(8,128)(2,1)} %bitcast.60, ...), custom_call_target="tpu_custom_call" | custom-call | tf_op jit(solution)/shard_map/picked_rows/pallas_call | solution.py:159
  12.3 2.8 %picked_rows.5 = bf16[4,128,512]{2,1,0:T(8,128)(2,1)} custom-call(s32[2]{0:T(128)} %pad_add_fusion.where_ref.group_ref, s32[16]{0:T(128)} %owner_ref.9, s32[256]{0:T(256)} %reshape.306.mask_ref, bf16[4,16,128,512]{3,2,1,0:T(8,128)(2,1)} %bitcast.62, bf16[4,16,128,512]{3,2,1,0:T(8,128)(2,1)} %bitcast.63, bf16[4,16,128,512]{3,2,1,0:T(8,128)(2,1)} %bitcast.64, ...), custom_call_target="tpu_custom_call" | custom-call | tf_op jit(solution)/shard_map/picked_rows/pallas_call | solution.py:159
  15.1 1.1 collective-permute-done
  16.2 10.2 %collective-permute-done.1 = bf16[2,4,128,128]{3,2,1,0:T(8,128)(2,1)S(1)} collective-permute-done((bf16[2,4,128,128]{3,2,1,0:T(8,128)(2,1)S(1)}, bf16[2,4,128,128]{3,2,1,0:T(8,128)(2,1)S(1)}, u32[]{:S(2)}, u32[]{:S(2)}) %collective-permute-start.1) | collective-permute-done | bytes 262176 | tf_op jit(solution)/shard_map/ppermute | solution.py:547
  26.7 1.6 collective-permute-start.4
  28.2 1.5 collective-permute-start.5
  30.4 4.8 %collective-permute-start.6 = (bf16[4,128,512]{2,1,0:T(8,128)(2,1)}, bf16[4,128,512]{2,1,0:T(8,128)(2,1)}, u32[]{:S(2)}, u32[]{:S(2)}) collective-permute-start(bf16[4,128,512]{2,1,0:T(8,128)(2,1)} %picked_rows.4), channel_id=1, source_target_pairs={{0,8},{8,0},{16,24},{24,16},{1,9},{9,1},{17,25},{25,17},{2,10},{10... | collective-permute-start | bytes 1572872 | tf_op jit(solution)/shard_map/ppermute | solution.py:547
  35.3 1.1 collective-permute-start.7
  37.0 9.6 %pair_tiles.1 = (bf16[2,4,33,16,128]{4,3,2,1,0:T(8,128)(2,1)}, bf16[2,4,33,16,128]{4,3,2,1,0:T(8,128)(2,1)}, bf16[2,4,33,16,128]{4,3,2,1,0:T(8,128)(2,1)}, bf16[...) custom-call(s32[2]{0:T(128)} %pad_add_fusion.where_ref.group_ref, s32[16]{0:T(128)} %owner_ref.9, ...), custom_call_target="tpu_custom_call" | custom-call | tf_op jit(solution)/shard_map/pair_tiles/pallas_call | solution.py:269
  46.6 2.6 %picked_square.3 = bf16[10,128,128]{2,1,0:T(8,128)(2,1)} custom-call(s32[2]{0:T(128)} %pad_add_fusion.where_ref.group_ref, s32[16]{0:T(128)} %owner_ref.9, s32[256]{0:T(256)} %reshape.306.mask_ref, bf16[4,16,128,512]{3,2,1,0:T(8,128)(2,1)} %bitcast.73, bf16[4,16,128,512]{3,2,1,0:T(8,128)(2,1)} %bitcast.71, bf16[4,16,128,512]{3,2,1,0:T(8,128)(2,1)} %bitcast.72, ...), custom_call_target="tpu_custom_call" | custom-call | tf_op jit(solution)/shard_map/picked_square/pallas_call | solution.py:129
  49.2 2.8 %picked_rows.6 = bf16[4,128,512]{2,1,0:T(8,128)(2,1)} custom-call(s32[2]{0:T(128)} %pad_add_fusion.where_ref.group_ref, s32[16]{0:T(128)} %owner_ref.9, s32[256]{0:T(256)} %reshape.306.mask_ref, bf16[4,16,128,512]{3,2,1,0:T(8,128)(2,1)} %bitcast.74, bf16[4,16,128,512]{3,2,1,0:T(8,128)(2,1)} %bitcast.75, bf16[4,16,128,512]{3,2,1,0:T(8,128)(2,1)} %bitcast.76, ...), custom_call_target="tpu_custom_call" | custom-call | tf_op jit(solution)/shard_map/picked_rows/pallas_call | solution.py:159
  52.0 6.6 %collective-permute-done.6.refs_9_.refs_10_ = bf16[4,128,512]{2,1,0:T(8,128)(2,1)} collective-permute-done((bf16[4,128,512]{2,1,0:T(8,128)(2,1)}, bf16[4,128,512]{2,1,0:T(8,128)(2,1)}, u32[]{:S(2)}, u32[]{:S(2)}) %collective-permute-start.6) | collective-permute-done | bytes 524320 | tf_op jit(solution)/shard_map/ppermute | solution.py:547
  58.7 2.5 collective-permute-done.7.refs_10_.refs_12_
  63.9 1.7 gather_fusion.1
  65.6 2.6 %collective-permute-start.12 = (bf16[10,128,128]{2,1,0:T(8,128)(2,1)}, bf16[10,128,128]{2,1,0:T(8,128)(2,1)}, u32[]{:S(2)}, u32[]{:S(2)}) collective-permute-start(bf16[10,128,128]{2,1,0:T(8,128)(2,1)} %picked_square.3), channel_id=1, source_target_pairs={{0,16},{8,24},{16,0},{24,8},{1,17},{9,25},{17,1},{25,9},{2,18},{10... | collective-permute-start | bytes 983048 | tf_op jit(solution)/shard_map/ppermute | solution.py:547
  68.2 1.7 gather_fusion.2
  70.5 4.7 %picked_rows.7.refs_8_.refs_9_ = bf16[16,128,512]{2,1,0:T(8,128)(2,1)} custom-call(s32[2]{0:T(128)} %pad_add_fusion.where_ref.group_ref, s32[16]{0:T(128)} %owner_ref.9, s32[256]{0:T(256)} %reshape.306.mask_ref, bf16[4,16,128,512]{3,2,1,0:T(8,128)(2,1)} %bitcast.78, bf16[4,16,128,512]{3,2,1,0:T(8,128)(2,1)} %bitcast.79, bf16[4,16,128,512]{3,2,1,0:T(8,128)(2,1)} %bitcast.80, ...), custom_call_target="tpu_custom_call" | custom-call | tf_op jit(solution)/shard_map/picked_rows/pallas_call | solution.py:159
  75.3 2.6 %picked_square.5 = bf16[10,128,128]{2,1,0:T(8,128)(2,1)} custom-call(s32[2]{0:T(128)} %pad_add_fusion.where_ref.group_ref, s32[16]{0:T(128)} %owner_ref.9, s32[256]{0:T(256)} %reshape.306.mask_ref, bf16[4,16,128,512]{3,2,1,0:T(8,128)(2,1)} %bitcast.82, bf16[4,16,128,512]{3,2,1,0:T(8,128)(2,1)} %bitcast.83, bf16[4,16,128,512]{3,2,1,0:T(8,128)(2,1)} %bitcast.84, ...), custom_call_target="tpu_custom_call" | custom-call | tf_op jit(solution)/shard_map/picked_square/pallas_call | solution.py:129
  77.9 2.6 %picked_square.4 = bf16[10,128,128]{2,1,0:T(8,128)(2,1)} custom-call(s32[2]{0:T(128)} %pad_add_fusion.where_ref.group_ref, s32[16]{0:T(128)} %owner_ref.9, s32[256]{0:T(256)} %reshape.306.mask_ref, bf16[4,16,128,512]{3,2,1,0:T(8,128)(2,1)} %bitcast.86, bf16[4,16,128,512]{3,2,1,0:T(8,128)(2,1)} %bitcast.87, bf16[4,16,128,512]{3,2,1,0:T(8,128)(2,1)} %bitcast.88, ...), custom_call_target="tpu_custom_call" | custom-call | tf_op jit(solution)/shard_map/picked_square/pallas_call | solution.py:129
  80.5 2.0 collective-permute-done.12.refs_11_
  82.5 2.0 collective-permute-done.11.refs_11_
  84.6 1.6 collective-permute-start.16
  86.2 1.5 collective-permute-start.17
  87.7 1.3 collective-permute-start.14
  89.0 1.5 collective-permute-start.15
  91.5 10.9 %early_half.1.refs_8_ = bf16[8,2048,128]{2,1,0:T(8,128)(2,1)} custom-call(s32[128]{0:T(128)} %gather_fusion.1, s32[128]{0:T(128)} %get-tuple-element.93.tile_ref, bf16[4,2,4,128,128]{4,3,2,1,0:T(8,128)(2,1)} %copy-done.2, bf16[4,2,4,128,128]{4,3,2,1,0:T(8,128)(2,1)} %copy-done.8, bf16[4,2,4,128,128]{4,3,2,1,0:T(8,128)(2,1)} %copy-done.9, ...), custom_call_target="tpu_custom_call" | custom-call | flops 8589934592 | bytes 16777216 | tf_op jit(solution)/shard_map/early_half/pallas_call | solution.py:509
  102.5 2.9 %collective-permute-done.15.refs_14_ = bf16[10,128,128]{2,1,0:T(8,128)(2,1)S(1)} collective-permute-done((bf16[10,128,128]{2,1,0:T(8,128)(2,1)}, bf16[10,128,128]{2,1,0:T(8,128)(2,1)S(1)}, u32[]{:S(2)}, u32[]{:S(2)}) %collective-permute-start.15) | collective-permute-done | bytes 327712 | tf_op jit(solution)/shard_map/ppermute | solution.py:547
  106.1 17.9 %last_half_and_pairs.1 = (bf16[32,9,16,128]{3,2,1,0:T(8,128)(2,1)}, bf16[8,2048,128]{2,1,0:T(8,128)(2,1)}) custom-call(s32[2]{0:T(128)} %pad_add_fusion.where_ref.group_ref, s32[128]{0:T(128)} %gather_fusion.1, s32[128]{0:T(128)} %get-tuple-element.93.tile_ref, s32[128]{0:T(128)} %gather_fusion.2, s32[128]{0:T(128)} %get-tuple-element.95.virtual_tile_ref, ...), custom_call_target="tpu_custom_call" | custom-call | tf_op jit(solution)/shard_map/last_half_and_pairs/pallas_call | solution.py:509
  125.0 3.6 %all-to-all-start = ((bf16[32,9,16,128]{3,2,1,0:T(8,128)(2,1)}), bf16[32,9,16,128]{3,2,1,0:T(8,128)(2,1)S(1)}, u32[]{:S(2)}, u32[]{:S(2)}) async-start(bf16[32,9,16,128]{3,2,1,0:T(8,128)(2,1)} %get-tuple-element.119), calls=%async_computation | async-start | bytes 2359296 | tf_op jit(solution)/shard_map/all_to_all | solution.py:709
  128.6 2.5 collective-permute-start.18
  131.1 22.0 %other_pairs.1 = bf16[32,24,16,128]{3,2,1,0:T(8,128)(2,1)} custom-call(s32[2]{0:T(128)} %pad_add_fusion.where_ref.group_ref, s32[128]{0:T(128)} %gather_fusion.2, s32[128]{0:T(128)} %get-tuple-element.95.virtual_tile_ref, bf16[4,2,4,128,128]{4,3,2,1,0:T(8,128)(2,1)} %copy-done.2, bf16[4,2,4,128,128]{4,3,2,1,0:T(8,128)(2,1)} %copy-done.8, ...), custom_call_target="tpu_custom_call" | custom-call | flops 12884901888 | bytes 25165824 | tf_op jit(solution)/shard_map/other_pairs/pallas_call | solution.py:509
  153.1 4.6 %collective-permute-done.18 = bf16[1,4,33,16,128]{4,3,2,1,0:T(8,128)(2,1)} collective-permute-done((bf16[1,4,33,16,128]{4,3,2,1,0:T(8,128)(2,1)}, bf16[1,4,33,16,128]{4,3,2,1,0:T(8,128)(2,1)}, u32[]{:S(2)}, u32[]{:S(2)}) %collective-permute-start.18) | collective-permute-done | bytes 540704 | tf_op jit(solution)/shard_map/ppermute | solution.py:547
  158.7 4.1 %all-to-all-start.1 = ((bf16[32,24,16,128]{3,2,1,0:T(8,128)(2,1)}), bf16[32,24,16,128]{3,2,1,0:T(8,128)(2,1)}, u32[]{:S(2)}, u32[]{:S(2)}) async-start(bf16[32,24,16,128]{3,2,1,0:T(8,128)(2,1)} %other_pairs.1), calls=%async_computation.1 | async-start | bytes 6291456 | tf_op jit(solution)/shard_map/all_to_all | solution.py:709
  163.3 1.7 collective-permute-done.19
  165.6 1.7 collective-permute-done.20
  167.9 2.5 collective-permute-start.22
  170.5 1.1 constant_dynamic-update-slice_fusion.1
  171.7 37.2 %collective-permute-done.22 = bf16[1,4,33,16,128]{4,3,2,1,0:T(8,128)(2,1)S(1)} collective-permute-done((bf16[1,4,33,16,128]{4,3,2,1,0:T(8,128)(2,1)S(1)}, bf16[1,4,33,16,128]{4,3,2,1,0:T(8,128)(2,1)S(1)}, u32[]{:S(2)}, u32[]{:S(2)}) %collective-permute-start.22) | collective-permute-done | bytes 540704 | tf_op jit(solution)/shard_map/ppermute | solution.py:547
  209.8 1.3 slice.40
  211.0 2.8 %reshape.313 = bf16[32,49152]{1,0:T(8,128)(2,1)} reshape(bf16[8,4,24,16,128]{4,3,2,1,0:T(8,128)(2,1)S(1)} %slice.41) | data formatting | bytes 6291456 | tf_op jit(solution)/shard_map/reshape | solution.py:725
  213.8 1.6 reshape.311
  215.4 19.9 %all-to-all-done.1 = bf16[32,24,16,128]{3,2,1,0:T(8,128)(2,1)} async-done(((bf16[32,24,16,128]{3,2,1,0:T(8,128)(2,1)}), bf16[32,24,16,128]{3,2,1,0:T(8,128)(2,1)}, u32[]{:S(2)}, u32[]{:S(2)}) %all-to-all-start.1) | async-done | bytes 3145760 | tf_op jit(solution)/shard_map/all_to_all | solution.py:709
  235.3 5.2 %fusion = f32[32,32]{1,0:T(8,128)S(1)} fusion(bf16[32,49152]{1,0:T(8,128)(2,1)} %reshape.313, bf16[4,8,384,128]{3,2,1,0:T(8,128)(2,1)} %bitcast.30), kind=kOutput, calls=%fused_computation.5 | convolution fusion | flops 100663296 | bytes 6295552 | tf_op jit(solution)/shard_map/pe,qe->pq/dot_general | solution.py:727
  242.0 10.0 %all_to_all.15 = f32[32,1,128]{2,1,0:T(1,128)S(1)} all-to-all(f32[32,1,128]{2,1,0:T(1,128)S(1)} %reshape.363), channel_id=1, replica_groups=mesh['grp'=4,'blk'=8] {'grp','blk'}, dimensions={0} | all-to-all | bytes 32768 | tf_op jit(solution)/shard_map/all_to_all | solution.py:709
  (100 shorter events, 16.0 us)
Async XLA Ops:
  2.0 14.2 %collective-permute-start = (bf16[2,4,128,128]{3,2,1,0:T(8,128)(2,1)S(1)}, bf16[2,4,128,128]{3,2,1,0:T(8,128)(2,1)S(1)}, u32[]{:S(2)}, u32[]{:S(2)}) collective-permute-start(bf16[2,4,128,128]{3,2,1,0:T(8,128)(2,1)S(1)} %get-tuple-element.138), channel_id=1, source_target_pairs={{0,8},{8,0},{16,24},{24,16},{1,9},{9,1},{17,25},{25,17},{2,10},{10... | collective-permute-start | bytes 786440 | tf_op jit(solution)/shard_map/ppermute | solution.py:547
  5.1 21.4 %collective-permute-start.1 = (bf16[2,4,128,128]{3,2,1,0:T(8,128)(2,1)S(1)}, bf16[2,4,128,128]{3,2,1,0:T(8,128)(2,1)S(1)}, u32[]{:S(2)}, u32[]{:S(2)}) collective-permute-start(bf16[2,4,128,128]{3,2,1,0:T(8,128)(2,1)S(1)} %get-tuple-element.138), channel_id=1, source_target_pairs={{0,16},{8,24},{16,0},{24,8},{1,17},{9,25},{17,1},{25,9},{2,18},{10... | collective-permute-start | bytes 786440 | tf_op jit(solution)/shard_map/ppermute | solution.py:547
  7.7 18.8 %collective-permute-start.2 = (bf16[2,4,128,128]{3,2,1,0:T(8,128)(2,1)S(1)}, bf16[2,4,128,128]{3,2,1,0:T(8,128)(2,1)S(1)}, u32[]{:S(2)}, u32[]{:S(2)}) collective-permute-start(bf16[2,4,128,128]{3,2,1,0:T(8,128)(2,1)S(1)} %get-tuple-element.138), channel_id=1, source_target_pairs={{0,24},{8,16},{16,8},{24,0},{1,25},{9,17},{17,9},{25,1},{2,26},{10... | collective-permute-start | bytes 786440 | tf_op jit(solution)/shard_map/ppermute | solution.py:547
  12.3 17.5 %copy-start = (s32[16]{0:T(128)S(1)}, s32[16]{0:T(128)}, u32[]{:S(2)}) copy-start(s32[16]{0:T(128)} %owner_ref.9) | copy-start | bytes 196
  12.3 24.1 %copy-start.13 = (s32[8]{0:T(128)S(1)}, s32[8]{0:T(128)}, u32[]{:S(2)}) copy-start(s32[8]{0:T(128)} %param.11) | copy-start | bytes 100
  12.3 24.3 %copy-start.14 = (s32[8]{0:T(128)S(1)}, s32[8]{0:T(128)}, u32[]{:S(2)}) copy-start(s32[8]{0:T(128)} %param.13) | copy-start | bytes 100
  26.6 34.7 %copy-start.2 = (bf16[4,2,4,128,128]{4,3,2,1,0:T(8,128)(2,1)}, bf16[4,2,4,128,128]{4,3,2,1,0:T(8,128)(2,1)S(1)}, u32[]{:S(2)}) copy-start(bf16[4,2,4,128,128]{4,3,2,1,0:T(8,128)(2,1)S(1)} %pad_maximum_fusion.refs_0_) | copy-start | bytes 3145732
  26.6 34.6 %collective-permute-start.3 = (bf16[4,2,4,128,128]{4,3,2,1,0:T(8,128)(2,1)S(1)}, bf16[4,2,4,128,128]{4,3,2,1,0:T(8,128)(2,1)S(1)}, u32[]{:S(2)}, u32[]{:S(2)}) collective-permute-start(bf16[4,2,4,128,128]{4,3,2,1,0:T(8,128)(2,1)S(1)} %pad_maximum_fusion.refs_0_), channel_id=1, source_target_pairs={{0,1},{1,0},{2,3},{3,2},{4,5},{5,4},{6,7},{7,6},{8,9},{9,8},{10,11... | collective-permute-start | bytes 3145736 | tf_op jit(solution)/shard_map/ppermute | solution.py:547
  26.7 34.5 %collective-permute-start.4 = (bf16[4,2,4,128,128]{4,3,2,1,0:T(8,128)(2,1)S(1)}, bf16[4,2,4,128,128]{4,3,2,1,0:T(8,128)(2,1)S(1)}, u32[]{:S(2)}, u32[]{:S(2)}) collective-permute-start(bf16[4,2,4,128,128]{4,3,2,1,0:T(8,128)(2,1)S(1)} %pad_maximum_fusion.refs_0_), channel_id=1, source_target_pairs={{0,2},{1,3},{2,0},{3,1},{4,6},{5,7},{6,4},{7,5},{8,10},{9,11},{10,... | collective-permute-start | bytes 3145736 | tf_op jit(solution)/shard_map/ppermute | solution.py:547
  28.2 33.0 %collective-permute-start.5 = (bf16[4,2,4,128,128]{4,3,2,1,0:T(8,128)(2,1)S(1)}, bf16[4,2,4,128,128]{4,3,2,1,0:T(8,128)(2,1)}, u32[]{:S(2)}, u32[]{:S(2)}) collective-permute-start(bf16[4,2,4,128,128]{4,3,2,1,0:T(8,128)(2,1)S(1)} %pad_maximum_fusion.refs_0_), channel_id=1, source_target_pairs={{0,4},{1,5},{2,6},{3,7},{4,0},{5,1},{6,2},{7,3},{8,12},{9,13},{10,... | collective-permute-start | bytes 3145736 | tf_op jit(solution)/shard_map/ppermute | solution.py:547
  30.4 28.2 %collective-permute-start.6 = (bf16[4,128,512]{2,1,0:T(8,128)(2,1)}, bf16[4,128,512]{2,1,0:T(8,128)(2,1)}, u32[]{:S(2)}, u32[]{:S(2)}) collective-permute-start(bf16[4,128,512]{2,1,0:T(8,128)(2,1)} %picked_rows.4), channel_id=1, source_target_pairs={{0,8},{8,0},{16,24},{24,16},{1,9},{9,1},{17,25},{25,17},{2,10},{10... | collective-permute-start | bytes 1572872 | tf_op jit(solution)/shard_map/ppermute | solution.py:547
  35.3 25.9 %collective-permute-start.7 = (bf16[4,128,512]{2,1,0:T(8,128)(2,1)}, bf16[4,128,512]{2,1,0:T(8,128)(2,1)}, u32[]{:S(2)}, u32[]{:S(2)}) collective-permute-start(bf16[4,128,512]{2,1,0:T(8,128)(2,1)} %picked_rows.5), channel_id=1, source_target_pairs={{0,16},{8,24},{16,0},{24,8},{1,17},{9,25},{17,1},{25,9},{2,18},{10... | collective-permute-start | bytes 1572872 | tf_op jit(solution)/shard_map/ppermute | solution.py:547
  49.2 13.1 %copy-start.1 = (s32[16]{0:T(128)S(1)}, s32[16]{0:T(128)}, u32[]{:S(2)}) copy-start(s32[16]{0:T(128)} %owner_ref.9) | copy-start | bytes 196
  61.2 4.4 %copy-start.8 = (bf16[4,2,4,128,128]{4,3,2,1,0:T(8,128)(2,1)}, bf16[4,2,4,128,128]{4,3,2,1,0:T(8,128)(2,1)S(1)}, u32[]{:S(2)}) copy-start(bf16[4,2,4,128,128]{4,3,2,1,0:T(8,128)(2,1)S(1)} %collective-permute-done.3.refs_1_) | copy-start | bytes 3145732
  61.2 4.4 %copy-start.9 = (bf16[4,2,4,128,128]{4,3,2,1,0:T(8,128)(2,1)}, bf16[4,2,4,128,128]{4,3,2,1,0:T(8,128)(2,1)S(1)}, u32[]{:S(2)}) copy-start(bf16[4,2,4,128,128]{4,3,2,1,0:T(8,128)(2,1)S(1)} %collective-permute-done.4.refs_2_) | copy-start | bytes 3145732
  61.2 23.3 %collective-permute-start.10 = (bf16[4,2,4,128,128]{4,3,2,1,0:T(8,128)(2,1)S(1)}, bf16[4,2,4,128,128]{4,3,2,1,0:T(8,128)(2,1)}, u32[]{:S(2)}, u32[]{:S(2)}) collective-permute-start(bf16[4,2,4,128,128]{4,3,2,1,0:T(8,128)(2,1)S(1)} %pad_maximum_fusion.refs_0_), channel_id=1, source_target_pairs={{0,6},{1,7},{2,4},{3,5},{4,2},{5,3},{6,0},{7,1},{8,14},{9,15},{10,... | collective-permute-start | bytes 3145736 | tf_op jit(solution)/shard_map/ppermute | solution.py:547
  61.8 22.8 %collective-permute-start.8 = (bf16[4,2,4,128,128]{4,3,2,1,0:T(8,128)(2,1)S(1)}, bf16[4,2,4,128,128]{4,3,2,1,0:T(8,128)(2,1)}, u32[]{:S(2)}, u32[]{:S(2)}) collective-permute-start(bf16[4,2,4,128,128]{4,3,2,1,0:T(8,128)(2,1)S(1)} %collective-permute-done.4.refs_2_), channel_id=1, source_target_pairs={{0,1},{1,0},{2,3},{3,2},{4,5},{5,4},{6,7},{7,6},{8,9},{9,8},{10,11... | collective-permute-start | bytes 3145736 | tf_op jit(solution)/shard_map/ppermute | solution.py:547
  61.8 22.8 %collective-permute-start.9 = (bf16[4,2,4,128,128]{4,3,2,1,0:T(8,128)(2,1)}, bf16[4,2,4,128,128]{4,3,2,1,0:T(8,128)(2,1)}, u32[]{:S(2)}, u32[]{:S(2)}) collective-permute-start(bf16[4,2,4,128,128]{4,3,2,1,0:T(8,128)(2,1)} %collective-permute-done.5.refs_4_), channel_id=1, source_target_pairs={{0,1},{1,0},{2,3},{3,2},{4,5},{5,4},{6,7},{7,6},{8,9},{9,8},{10,11... | collective-permute-start | bytes 3145736 | tf_op jit(solution)/shard_map/ppermute | solution.py:547
  63.3 21.2 %collective-permute-start.11 = (bf16[4,128,512]{2,1,0:T(8,128)(2,1)}, bf16[4,128,512]{2,1,0:T(8,128)(2,1)}, u32[]{:S(2)}, u32[]{:S(2)}) collective-permute-start(bf16[4,128,512]{2,1,0:T(8,128)(2,1)} %picked_rows.6), channel_id=1, source_target_pairs={{0,8},{8,0},{16,24},{24,16},{1,9},{9,1},{17,25},{25,17},{2,10},{10... | collective-permute-start | bytes 1572872 | tf_op jit(solution)/shard_map/ppermute | solution.py:547
  65.6 16.9 %collective-permute-start.12 = (bf16[10,128,128]{2,1,0:T(8,128)(2,1)}, bf16[10,128,128]{2,1,0:T(8,128)(2,1)}, u32[]{:S(2)}, u32[]{:S(2)}) collective-permute-start(bf16[10,128,128]{2,1,0:T(8,128)(2,1)} %picked_square.3), channel_id=1, source_target_pairs={{0,16},{8,24},{16,0},{24,8},{1,17},{9,25},{17,1},{25,9},{2,18},{10... | collective-permute-start | bytes 983048 | tf_op jit(solution)/shard_map/ppermute | solution.py:547
  84.6 6.0 %collective-permute-start.13 = (bf16[4,2,4,128,128]{4,3,2,1,0:T(8,128)(2,1)}, bf16[4,2,4,128,128]{4,3,2,1,0:T(8,128)(2,1)S(1)}, u32[]{:S(2)}, u32[]{:S(2)}) collective-permute-start(bf16[4,2,4,128,128]{4,3,2,1,0:T(8,128)(2,1)} %collective-permute-done.10.refs_6_), channel_id=1, source_target_pairs={{0,1},{1,0},{2,3},{3,2},{4,5},{5,4},{6,7},{7,6},{8,9},{9,8},{10,11... | collective-permute-start | bytes 3145736 | tf_op jit(solution)/shard_map/ppermute | solution.py:547
  84.6 39.3 %collective-permute-start.16 = (bf16[2,4,33,16,128]{4,3,2,1,0:T(8,128)(2,1)}, bf16[2,4,33,16,128]{4,3,2,1,0:T(8,128)(2,1)S(1)}, u32[]{:S(2)}, u32[]{:S(2)}) collective-permute-start(bf16[2,4,33,16,128]{4,3,2,1,0:T(8,128)(2,1)} %get-tuple-element.116), channel_id=1, source_target_pairs={{0,2},{1,3},{2,0},{3,1},{4,6},{5,7},{6,4},{7,5},{8,10},{9,11},{10,... | collective-permute-start | bytes 3244040 | tf_op jit(solution)/shard_map/ppermute | solution.py:547
  86.2 37.8 %collective-permute-start.17 = (bf16[2,4,33,16,128]{4,3,2,1,0:T(8,128)(2,1)}, bf16[2,4,33,16,128]{4,3,2,1,0:T(8,128)(2,1)S(1)}, u32[]{:S(2)}, u32[]{:S(2)}) collective-permute-start(bf16[2,4,33,16,128]{4,3,2,1,0:T(8,128)(2,1)} %get-tuple-element.117), channel_id=1, source_target_pairs={{0,4},{1,5},{2,6},{3,7},{4,0},{5,1},{6,2},{7,3},{8,12},{9,13},{10,... | collective-permute-start | bytes 3244040 | tf_op jit(solution)/shard_map/ppermute | solution.py:547
  87.7 14.7 %collective-permute-start.14 = (bf16[10,128,128]{2,1,0:T(8,128)(2,1)}, bf16[10,128,128]{2,1,0:T(8,128)(2,1)S(1)}, u32[]{:S(2)}, u32[]{:S(2)}) collective-permute-start(bf16[10,128,128]{2,1,0:T(8,128)(2,1)} %picked_square.4), channel_id=1, source_target_pairs={{0,8},{8,0},{16,24},{24,16},{1,9},{9,1},{17,25},{25,17},{2,10},{10... | collective-permute-start | bytes 983048 | tf_op jit(solution)/shard_map/ppermute | solution.py:547
  89.0 16.3 %collective-permute-start.15 = (bf16[10,128,128]{2,1,0:T(8,128)(2,1)}, bf16[10,128,128]{2,1,0:T(8,128)(2,1)S(1)}, u32[]{:S(2)}, u32[]{:S(2)}) collective-permute-start(bf16[10,128,128]{2,1,0:T(8,128)(2,1)} %picked_square.5), channel_id=1, source_target_pairs={{0,24},{8,16},{16,8},{24,0},{1,25},{9,17},{17,9},{25,1},{2,26},{10... | collective-permute-start | bytes 983048 | tf_op jit(solution)/shard_map/ppermute | solution.py:547
  90.5 1.0 copy-start.10
  102.5 2.9 %copy-start.11 = (bf16[10,128,128]{2,1,0:T(8,128)(2,1)}, bf16[10,128,128]{2,1,0:T(8,128)(2,1)S(1)}, u32[]{:S(2)}) copy-start(bf16[10,128,128]{2,1,0:T(8,128)(2,1)S(1)} %collective-permute-done.14.refs_13_) | copy-start | bytes 983044
  105.4 0.7 copy-start.12
  124.0 1.0 copy-start.6
  125.0 32.7 %all-to-all-start = ((bf16[32,9,16,128]{3,2,1,0:T(8,128)(2,1)}), bf16[32,9,16,128]{3,2,1,0:T(8,128)(2,1)S(1)}, u32[]{:S(2)}, u32[]{:S(2)}) async-start(bf16[32,9,16,128]{3,2,1,0:T(8,128)(2,1)} %get-tuple-element.119), calls=%async_computation | async-start | bytes 2359296 | tf_op jit(solution)/shard_map/all_to_all | solution.py:709
  128.6 29.1 %collective-permute-start.18 = (bf16[1,4,33,16,128]{4,3,2,1,0:T(8,128)(2,1)}, bf16[1,4,33,16,128]{4,3,2,1,0:T(8,128)(2,1)}, u32[]{:S(2)}, u32[]{:S(2)}) collective-permute-start(bf16[1,4,33,16,128]{4,3,2,1,0:T(8,128)(2,1)} %get-tuple-element.121), channel_id=1, source_target_pairs={{0,6},{1,7},{2,4},{3,5},{4,2},{5,3},{6,0},{7,1},{8,14},{9,15},{10,... | collective-permute-start | bytes 1622024 | tf_op jit(solution)/shard_map/ppermute | solution.py:547
  153.1 9.8 %copy-start.5 = (bf16[2,4,33,16,128]{4,3,2,1,0:T(8,128)(2,1)S(1)}, bf16[2,4,33,16,128]{4,3,2,1,0:T(8,128)(2,1)}, u32[]{:S(2)}) copy-start(bf16[2,4,33,16,128]{4,3,2,1,0:T(8,128)(2,1)} %get-tuple-element.123) | copy-start | bytes 3244036
  157.7 1.0 copy-start.3
  158.7 76.6 %all-to-all-start.1 = ((bf16[32,24,16,128]{3,2,1,0:T(8,128)(2,1)}), bf16[32,24,16,128]{3,2,1,0:T(8,128)(2,1)}, u32[]{:S(2)}, u32[]{:S(2)}) async-start(bf16[32,24,16,128]{3,2,1,0:T(8,128)(2,1)} %other_pairs.1), calls=%async_computation.1 | async-start | bytes 6291456 | tf_op jit(solution)/shard_map/all_to_all | solution.py:709
  162.8 2.3 copy-start.7
  163.1 2.0 collective-permute-start.19
  165.1 2.9 %copy-start.15 = (bf16[1,4,33,16,128]{4,3,2,1,0:T(8,128)(2,1)S(1)}, bf16[1,4,33,16,128]{4,3,2,1,0:T(8,128)(2,1)}, u32[]{:S(2)}) copy-start(bf16[1,4,33,16,128]{4,3,2,1,0:T(8,128)(2,1)} %get-tuple-element.127) | copy-start | bytes 1622020
  165.4 2.0 collective-permute-start.20
  167.7 2.8 %collective-permute-start.21 = (bf16[4,33,16,128]{3,2,1,0:T(8,128)(2,1)S(1)}, bf16[4,33,16,128]{3,2,1,0:T(8,128)(2,1)S(1)}, u32[]{:S(2)}, u32[]{:S(2)}) collective-permute-start(bf16[4,33,16,128]{3,2,1,0:T(8,128)(2,1)S(1)} %get-tuple-element.131), channel_id=1, source_target_pairs={{0,1},{1,0},{2,3},{3,2},{4,5},{5,4},{6,7},{7,6},{8,9},{9,8},{10,11... | collective-permute-start | bytes 1622024 | tf_op jit(solution)/shard_map/ppermute | solution.py:547
  167.9 40.9 %collective-permute-start.22 = (bf16[1,4,33,16,128]{4,3,2,1,0:T(8,128)(2,1)S(1)}, bf16[1,4,33,16,128]{4,3,2,1,0:T(8,128)(2,1)S(1)}, u32[]{:S(2)}, u32[]{:S(2)}) collective-permute-start(bf16[1,4,33,16,128]{4,3,2,1,0:T(8,128)(2,1)S(1)} %copy-done.15), channel_id=1, source_target_pairs={{0,7},{1,6},{2,5},{3,4},{4,3},{5,2},{6,1},{7,0},{8,15},{9,14},{10,... | collective-permute-start | bytes 1622024 | tf_op jit(solution)/shard_map/ppermute | solution.py:547
  235.3 5.2 %copy-start.4 = (bf16[32,9,16,128]{3,2,1,0:T(8,128)(2,1)S(1)}, bf16[32,9,16,128]{3,2,1,0:T(8,128)(2,1)}, u32[]{:S(2)}) copy-start(bf16[32,9,16,128]{3,2,1,0:T(8,128)(2,1)} %copy-done.3) | copy-start | bytes 3538948

commit v5 on v2

v5 whole, which is shorter than its diff:
```python
import functools

import jax
import jax.numpy as jnp
from jax import lax
from jax.experimental import pallas as pl
from jax.experimental.pallas import tpu as pltpu
from jax.sharding import PartitionSpec as P

NT = 16
UNROLL = 4
VMEM_BYTES = 60 * 1024 * 1024
PARTS = (
    ((0, 0), (0, 1), (1, 0), (1, 1)),
    ((2, 0), (2, 1), (3, 0), (3, 1)),
    ((4, 0), (4, 1), (5, 0), (5, 1)),
    ((7, 0), (7, 1), (6, 0)),
    ((6, 1),),
)


def general_body(
    integrals,
    tile_mask,
    tile_owner,
    occupied_tiles,
    occupied_offsets,
    virtual_tiles,
    virtual_offsets,
):
    aux_local, basis_size, local_width = integrals.shape
    tile_width = basis_size // NT
    kcount = occupied_offsets.shape[0]
    local_tiles = local_width // tile_width
    group_index = lax.axis_index("grp")
    local_owner = lax.dynamic_slice_in_dim(tile_owner, group_index * local_tiles, local_tiles)
    matches = (local_owner[None, :, None] == jnp.arange(NT, dtype=jnp.int32)[None, None, :]).astype(
        jnp.int32
    )
    column_mask = jnp.sum(tile_mask[:, None, :] * matches, axis=2)
    blocked = integrals.reshape(aux_local, NT, tile_width, local_tiles, tile_width)
    masked = blocked * column_mask.astype(jnp.bfloat16)[None, :, None, :, None]
    masked = masked.reshape(aux_local, NT, tile_width, local_width)
    occupied_all, virtual_all = (
        lax.all_gather(occupied_tiles, ("grp", "blk"), axis=0, tiled=True),
        lax.all_gather(virtual_tiles, ("grp", "blk"), axis=0, tiled=True),
    )
    occupied_all = occupied_all.reshape(NT, kcount, tile_width, tile_width)
    virtual_all = virtual_all.reshape(NT, kcount, tile_width, tile_width)
    source_rows = (tile_owner[:, None] - occupied_offsets[None, :]) % NT
    partner_rows = (tile_owner[:, None] + virtual_offsets[None, :]) % NT
    virtual_pick = virtual_all[tile_owner]
    occupied_sum = jnp.zeros((aux_local, NT, tile_width, local_width), jnp.float32)
    virtual_sum = jnp.zeros((aux_local, local_width, NT, tile_width), jnp.float32)
    for slot in range(kcount):
        occupied_pick = occupied_all[source_rows[:, slot], slot]
        occupied_inputs = masked[:, source_rows[:, slot]]
        occupied_sum = occupied_sum + jnp.einsum(
            "tmn,ptml->ptnl", occupied_pick, occupied_inputs, preferred_element_type=jnp.float32
        )
        virtual_inputs = masked[:, partner_rows[:, slot]]
        virtual_sum = virtual_sum + jnp.einsum(
            "tnm,ptml->pltn",
            virtual_pick[:, slot],
            virtual_inputs,
            preferred_element_type=jnp.float32,
        )
    occupied_part = occupied_sum.astype(jnp.bfloat16)
    virtual_part = virtual_sum.astype(jnp.bfloat16).reshape(
        aux_local, local_tiles, tile_width, basis_size
    )
    occupied_moved = lax.all_to_all(occupied_part, "grp", split_axis=1, concat_axis=3, tiled=True)
    occupied_full, virtual_full = (
        lax.all_to_all(occupied_moved, "blk", split_axis=2, concat_axis=0, tiled=True),
        lax.all_to_all(virtual_part, "blk", split_axis=2, concat_axis=0, tiled=True),
    )
    left_side = occupied_full.reshape(occupied_full.shape[0], -1)
    right_side = virtual_full.reshape(virtual_full.shape[0], -1)
    partial_sum = jnp.einsum(
        "pe,qe->pq", left_side, right_side, preferred_element_type=jnp.float32
    ) * (1.0 / basis_size)
    total = lax.psum(partial_sum, ("grp", "blk"))
    return lax.dynamic_slice_in_dim(total, lax.axis_index("blk") * aux_local, aux_local, 0)


def place(refs, tile_row, column):
    owner_ref, mask_ref = refs
    return mask_ref[tile_row * NT + owner_ref[column]]


def masked_tile(values, kept):
    return values * jnp.full(values.shape, kept, jnp.int32).astype(values.dtype)


def picked_kernel(columns, planes_of, where_ref, owner_ref, mask_ref, *refs):
    inputs, out_ref = refs[:-1], refs[-1]
    tile = out_ref.shape[1]
    group = where_ref[0]
    row_plane = planes_of(pl.program_id(0)) ^ group
    for q in range(columns):
        tile_row = owner_ref[row_plane * columns + q]
        for c in range(columns):
            lanes = slice(c * tile, (c + 1) * tile)
            kept = place((owner_ref, mask_ref), tile_row, group * columns + c)
            out_ref[q, :, lanes] = masked_tile(inputs[q][0, 0, :, lanes], kept)


def triangle(columns):
    return [(q, c) for q in range(columns) for c in range(q + 1)]


def picked_square_kernel(columns, planes, where_ref, owner_ref, mask_ref, *refs):
    inputs, out_ref = refs[:-1], refs[-1]
    tile = out_ref.shape[1]
    first = where_ref[0] * columns
    wanted = [(0, q, c) for q, c in triangle(columns)]
    wanted += [(i, q, c) for i in range(1, len(planes)) for q in range(columns) for c in range(columns)]
    for at, (i, q, c) in enumerate(wanted):
        row = owner_ref[(where_ref[0] ^ planes[i]) * columns + q]
        kept = place((owner_ref, mask_ref), row, first + c)
        out_ref[at] = masked_tile(inputs[i * columns + q][0, 0, :, c * tile : (c + 1) * tile], kept)


def picked_square(scalars, integrals, away, planes=(0,)):
    aux_local, basis_size, width = integrals.shape
    tile = basis_size // NT
    columns = width // tile
    count = len(triangle(columns)) + (len(planes) - 1) * columns * columns

    def row_map(plane, q):
        def index(i, where, owner, mask):
            return (where[0] ^ away, owner[(where[0] ^ plane) * columns + q], 0, 0)

        return index

    return pl.pallas_call(
        functools.partial(picked_square_kernel, columns, planes),
        grid_spec=pltpu.PrefetchScalarGridSpec(
            num_scalar_prefetch=3,
            grid=(1,),
            in_specs=[
                pl.BlockSpec((1, 1, tile, width), row_map(plane, q))
                for plane in planes
                for q in range(columns)
            ],
            out_specs=pl.BlockSpec((count, tile, tile), lambda i, *_: (0, 0, 0)),
        ),
        out_shape=jax.ShapeDtypeStruct((count, tile, tile), jnp.bfloat16),
        compiler_params=pltpu.CompilerParams(vmem_limit_bytes=VMEM_BYTES),
        cost_estimate=pl.CostEstimate(flops=0, bytes_accessed=0, transcendentals=0),
        name="picked_square",
    )(*scalars, *([integrals.reshape(aux_local, NT, tile, width)] * (columns * len(planes))))


def picked_rows(scalars, integrals, away, row_planes):
    aux_local, basis_size, width = integrals.shape
    tile = basis_size // NT
    columns = width // tile

    def planes_of(i):
        return sum(jnp.where(i == at, plane, 0) for at, plane in enumerate(row_planes))

    def row_map(q):
        def index(i, where, owner, mask):
            plane = planes_of(i) ^ where[0]
            return (where[0] ^ away, owner[plane * columns + q], 0, 0)

        return index

    return pl.pallas_call(
        functools.partial(picked_kernel, columns, planes_of),
        grid_spec=pltpu.PrefetchScalarGridSpec(
            num_scalar_prefetch=3,
            grid=(len(row_planes),),
            in_specs=[pl.BlockSpec((1, 1, tile, width), row_map(q)) for q in range(columns)],
            out_specs=pl.BlockSpec((columns, tile, width), lambda i, *_: (i, 0, 0)),
        ),
        out_shape=jax.ShapeDtypeStruct((len(row_planes) * columns, tile, width), jnp.bfloat16),
        compiler_params=pltpu.CompilerParams(vmem_limit_bytes=VMEM_BYTES),
        cost_estimate=pl.CostEstimate(flops=0, bytes_accessed=0, transcendentals=0),
        name="picked_rows",
    )(*scalars, *([integrals.reshape(aux_local, NT, tile, width)] * columns))


def strips_of(columns):
    square = columns * columns
    return 2 * square, columns * 3 // 4 + (square - columns) // 2 + square // 2


def diagonal_strips(tiles, turned):
    rows, lanes = tiles[0].shape[-2] // 2, tiles[0].shape[-1] // 2
    shape = tiles[0].shape[:-2] + (rows, 2 * lanes)
    left = lax.broadcasted_iota(jnp.int32, shape, len(shape) - 1) < lanes
    kept, rest = [], []
    for c in range(0, len(tiles), 2):
        lower, upper = tiles[c][..., rows:, :], tiles[c + 1][..., :rows, :]
        if turned:
            lower = lower + jnp.where(left, tiles[c].T[rows:, :], 0)
            upper = upper + jnp.where(left, 0, tiles[c + 1].T[:rows, :])
        kept += [lower, upper]
        rest.append(jnp.where(left, tiles[c][..., :rows, :], tiles[c + 1][..., rows:, :]))
    halves = kept + rest
    return [
        jnp.concatenate(halves[at : at + 2], axis=-2) for at in range(0, len(halves), 2)
    ]


def pair_kernel(columns, where_ref, owner_ref, mask_ref, *refs):
    inputs, out_refs, (whole,) = refs[:columns], refs[columns:-1], refs[-1:]
    rows, tile = out_refs[0].shape[3:]
    first = where_ref[0] * columns
    step = pl.program_id(0)
    plane = where_ref[0] ^ pair_plane(step)
    cross, _ = strips_of(columns)
    within = cross + columns * 3 // 4
    sibling = within + (columns * columns - columns) // 2
    starts = [
        [(pl.multiple_of((part ^ where_ref[1]) * rows, rows), at) for part, at in some]
        for some in PARTS
    ]

    def masked(q, c):
        kept = place((owner_ref, mask_ref), owner_ref[plane * columns + q], first + c)
        return masked_tile(inputs[q][:, 0, :, c * tile : (c + 1) * tile], kept)

    def write(strip, strips):
        for at, values in enumerate(strips):
            whole[at] = values
        for out_ref, some in zip(out_refs, starts):
            count = out_ref.shape[1]
            for piece, (start, aux) in enumerate(some):
                for at in range(len(strips)):
                    out_ref[piece, :, strip + at] = whole[
                        at, aux * count : (aux + 1) * count, pl.ds(start, rows), :
                    ]

    @pl.when(step < 2)
    def _():
        for q in range(columns):
            write((step * columns + q) * columns, [masked(q, c) for c in range(columns)])

    @pl.when(step == 2)
    def _():
        write(cross, diagonal_strips([masked(c, c) for c in range(columns)], False))
        write(within, [masked(q, c) for q in range(columns) for c in range(q)])

    @pl.when((step == 3) & (where_ref[0] % 2 == 0))
    def _():
        write(sibling, [masked(q, c) for q in range(columns // 2) for c in range(columns)])

    @pl.when((step == 3) & (where_ref[0] % 2 == 1))
    def _():
        write(
            sibling, [masked(q, c) for q in range(columns) for c in range(columns // 2, columns)]
        )


def pair_plane(k):
    return jnp.where(k < 2, k + 2, k - 2)


def pair_tiles(scalars, integrals, parts):
    aux_local, basis_size, width = integrals.shape
    tile = basis_size // NT
    columns = width // tile
    rows = tile // parts
    shapes = [
        (len(some), aux_local // 2, sum(strips_of(columns)), rows, tile) for some in PARTS
    ]

    def row_map(q):
        def index(i, where, owner, mask):
            return (0, owner[(where[0] ^ pair_plane(i)) * columns + q], 0, 0)

        return index

    return pl.pallas_call(
        functools.partial(pair_kernel, columns),
        grid_spec=pltpu.PrefetchScalarGridSpec(
            num_scalar_prefetch=3,
            grid=(NT // columns,),
            in_specs=[
                pl.BlockSpec((aux_local, 1, tile, width), row_map(q)) for q in range(columns)
            ],
            out_specs=[pl.BlockSpec(shape, lambda i, *_: (0, 0, 0, 0, 0)) for shape in shapes],
            scratch_shapes=[
                pltpu.VMEM((columns * columns // 2, aux_local, tile, tile), jnp.bfloat16)
            ],
        ),
        out_shape=[jax.ShapeDtypeStruct(shape, jnp.bfloat16) for shape in shapes],
        compiler_params=pltpu.CompilerParams(vmem_limit_bytes=VMEM_BYTES),
        cost_estimate=pl.CostEstimate(flops=0, bytes_accessed=0, transcendentals=0),
        name="pair_tiles",
    )(*scalars, *([integrals.reshape(aux_local, NT, tile, width)] * columns))


def start_all(copies):
    for copy in copies:
        copy.start()


def wait_all(copies):
    for copy in copies:
        copy.wait()


def green_copies(green_refs, which, green, sems):
    copies = []
    for ref in green_refs:
        held = ref.shape[2]
        for plane in range(ref.shape[0]):
            at = len(copies)
            copies.append(
                pltpu.make_async_copy(
                    ref.at[plane, which], green.at[pl.ds(at * held, held)], sems.at[at]
                )
            )
    return copies


def column_planes(column_blocks, block_refs, tile, full):
    width = full.shape[1] // len(column_blocks)
    columns = width // tile
    for at, blocks in enumerate(column_blocks):
        for plane, (ref, first, turned) in enumerate(blocks):
            if first is None:
                for i, (q, c) in enumerate(triangle(columns)):
                    row, column = plane * width + q * tile, at * width + c * tile
                    values = block_refs[ref][i]
                    full[row : row + tile, column : column + tile] = values
                    if q != c:
                        row, column = plane * width + c * tile, at * width + q * tile
                        full[row : row + tile, column : column + tile] = values.T
                continue
            if block_refs[ref].shape[2] == tile:
                count = len(triangle(columns)) + (first - 1) * columns * columns
                for i in range(columns * columns):
                    q, c = i // columns, i % columns
                    if turned:
                        q, c = c, q
                    row, column = plane * width + q * tile, at * width + c * tile
                    values = block_refs[ref][count + i]
                    full[row : row + tile, column : column + tile] = values.T if turned else values
                continue
            values = block_refs[ref][first * columns : (first + 1) * columns]
            values = values.reshape(width, width)
            full[plane * width : (plane + 1) * width, at * width : (at + 1) * width] = (
                values.T if turned else values
            )


def occupied_rows(kcount, count, width, slot_ref, tile_ref, green, full, half, first, start, stop):
    tile = green.shape[1]
    columns = width // tile

    @pl.loop(start, stop, unroll=UNROLL)
    def _(r):
        left = jnp.concatenate([green[tile_ref[r * kcount + k]] for k in range(kcount)], axis=1)
        starts = [pl.multiple_of(slot_ref[r * kcount + k] * tile, tile) for k in range(kcount)]
        rows = pl.ds(pl.multiple_of(r * tile, tile), tile)
        for at in range(count):
            right = jnp.concatenate(
                [full[pl.ds(start, tile), at * width : (at + 1) * width] for start in starts],
                axis=0,
            )
            values = jnp.dot(left, right, preferred_element_type=jnp.float32).astype(jnp.bfloat16)
            for c in range(columns):
                half[first + at * columns + c, rows, :] = values[:, c * tile : (c + 1) * tile]


def half_products(kcount, other, slot_ref, tile_ref, green, half, product):
    tile = green.shape[1]
    count = NT // 2

    def column(t, rows):
        right = jnp.concatenate([green[tile_ref[t * kcount + k]] for k in range(kcount)], axis=0)
        slots = [slot_ref[t * kcount + k] for k in range(kcount)]
        for first in range(0, count, 4):
            start = (rows + first) * tile
            left = jnp.concatenate(
                [half[slot, start : start + 4 * tile, :] for slot in slots], axis=1
            )
            values = jnp.dot(left, right, preferred_element_type=jnp.float32)
            product[t, first : first + 4] = values.reshape(4, tile, tile)

    pl.loop(0, count, unroll=UNROLL)(lambda t: column(t, count if other else 0))
    pl.loop(count, NT, unroll=UNROLL)(lambda t: column(t, 0 if other else count))


def write_strip(out_ref, device, strip, values):
    rows = out_ref.shape[2]
    values = values.astype(jnp.bfloat16)
    for part in range(values.shape[0] // rows):
        out_ref[device + part, strip] = values[part * rows : (part + 1) * rows]


def cross_strips(columns, group, product, out_ref):
    count = NT // 2
    parts = out_ref.shape[0] // 2

    @pl.loop(0, 2)
    def _(plane):
        away = plane ^ lax.rem(group, 2)

        @pl.loop(0, 2)
        def _(k):
            first = (k ^ away) * columns
            for q in range(columns):
                for c in range(columns):
                    s = away * columns + c
                    values = product[s, first + q] + product[count + first + q, s].T
                    write_strip(out_ref, plane * parts, (k * columns + q) * columns + c, values)


def within_strips(columns, group, product, out_ref):
    planes = NT // columns
    parts = out_ref.shape[0] // planes

    for plane in range(planes):
        away = plane ^ group
        own, near = lax.rem(away, 2) * columns, (1 - lax.rem(away, 2)) * columns
        first, sibling = away * columns, (away ^ 1) * columns
        tiles = [product[first + c, own + c] for c in range(columns)]
        strips = diagonal_strips(tiles, True)
        for q in range(columns):
            for c in range(q):
                strips.append(product[first + c, own + q] + product[first + q, own + c].T)
        for at in range(columns * columns // 2):
            if plane % 2:
                q, c = at // (columns // 2), columns // 2 + at % (columns // 2)
            else:
                q, c = at // columns, at % columns
            strips.append(product[first + c, near + q] + product[sibling + q, own + c].T)
        for strip, values in enumerate(strips):
            write_strip(out_ref, plane * parts, strip, values)


def first_kernel(
    kcount, columns, column_blocks, parts, group_ref, slot_ref, tile_ref, half_slot_ref,
    virtual_tile_ref, *refs
):
    green_refs, refs = refs[:parts], refs[parts:]
    block_refs, refs = refs[:-9], refs[-9:]
    out_ref, half_ref, green, virtual, full, half, product, sems, others = refs
    width = full.shape[1] // len(column_blocks)
    copies = green_copies(green_refs, 0, green, sems)
    start_all(copies)
    column_planes(column_blocks, block_refs, green.shape[1], full)
    wait_all(copies)
    later = green_copies(green_refs, 1, virtual, others)
    start_all(later)
    occupied_rows(
        kcount, len(column_blocks), width, slot_ref, tile_ref, green, full, half, 0, 0, NT
    )
    kept = pltpu.make_async_copy(half, half_ref, others.at[others.shape[0] - 1])
    kept.start()
    wait_all(later)
    half_products(kcount, False, half_slot_ref, virtual_tile_ref, virtual, half, product)
    within_strips(columns, group_ref[0], product, out_ref)
    kept.wait()


def rest_kernel(
    kcount, columns, parts, group_ref, half_slot_ref, virtual_tile_ref, *refs
):
    green_refs, refs = refs[:parts], refs[parts:]
    half_ref, out_ref, virtual, half, product, others = refs
    copies = green_copies(green_refs, 1, virtual, others)
    copies.append(pltpu.make_async_copy(half_ref, half, others.at[others.shape[0] - 1]))
    start_all(copies)
    wait_all(copies)
    half_products(kcount, True, half_slot_ref, virtual_tile_ref, virtual, half, product)
    cross_strips(columns, group_ref[0], product, out_ref)


def kernel_call(
    kernel, tables, anywhere, blocks, out_shape, out_spaces, scratch_shapes, name, flops=0
):
    return pl.pallas_call(
        kernel,
        in_specs=[pl.BlockSpec(memory_space=pltpu.SMEM)] * len(tables)
        + [pl.BlockSpec(memory_space=pl.ANY)] * len(anywhere)
        + [pl.BlockSpec(memory_space=pltpu.VMEM)] * len(blocks),
        out_specs=[pl.BlockSpec(memory_space=space) for space in out_spaces],
        out_shape=out_shape,
        scratch_shapes=scratch_shapes,
        compiler_params=pltpu.CompilerParams(vmem_limit_bytes=VMEM_BYTES),
        cost_estimate=pl.CostEstimate(flops=flops, bytes_accessed=flops // 512, transcendentals=0),
        name=name,
    )(*tables, *anywhere, *blocks)


def paired_kernel(first, parts, left_ref, *refs):
    right_refs, (out_ref, right, sems) = refs[:parts], refs[parts:]
    sources, count, rows, tile = left_ref.shape
    copies = []
    others = 0
    for at, ref in enumerate(right_refs):
        copies.append(
            pltpu.make_async_copy(
                ref.at[:, pl.ds(first, count)],
                right.at[pl.ds(others, ref.shape[0])],
                sems.at[at],
            )
        )
        others += ref.shape[0]
    start_all(copies)
    wait_all(copies)
    left = jnp.concatenate(
        [left_ref[:, at].reshape(sources * rows, tile) for at in range(count)], axis=1
    )
    right = jnp.concatenate(
        [right[:, at].reshape(others * rows, tile) for at in range(count)], axis=1
    )
    total = lax.dot_general(
        left, right, (((1,), (1,)), ((), ())), preferred_element_type=jnp.float32
    )
    down = lax.broadcasted_iota(jnp.int32, total.shape, 0)
    along = lax.broadcasted_iota(jnp.int32, total.shape, 1)
    total = jnp.where((down ^ along) % rows == 0, total, 0.0)
    total = jnp.sum(total.reshape(sources, rows, others * rows), axis=1)
    out_ref[...] = jnp.sum(total.T.reshape(others, rows, sources), axis=1)


def paired(left, rights, first, count):
    parts = len(rights)
    others = sum(each.shape[0] for each in rights)
    return pl.pallas_call(
        functools.partial(paired_kernel, first, parts),
        in_specs=[pl.BlockSpec(memory_space=pltpu.VMEM)]
        + [pl.BlockSpec(memory_space=pl.ANY)] * parts,
        out_specs=pl.BlockSpec(memory_space=pltpu.VMEM),
        out_shape=jax.ShapeDtypeStruct((others, left.shape[0]), jnp.float32),
        scratch_shapes=[
            pltpu.VMEM((others, count) + left.shape[2:], jnp.bfloat16),
            pltpu.SemaphoreType.DMA((parts,)),
        ],
        compiler_params=pltpu.CompilerParams(vmem_limit_bytes=VMEM_BYTES),
        name="paired",
    )(left, *rights)


def folded_body(
    integrals,
    tile_mask,
    tile_owner,
    occupied_tiles,
    occupied_offsets,
    virtual_tiles,
    virtual_offsets,
):
    aux_local, basis_size, width = integrals.shape
    tile = basis_size // NT
    columns = width // tile
    planes, parts = lax.axis_size("grp"), lax.axis_size("blk")
    kcount = occupied_offsets.shape[0]
    group = lax.axis_index("grp")

    part = lax.axis_index("blk")
    scalars = (
        jnp.stack([group, part]).astype(jnp.int32),
        tile_owner,
        tile_mask.reshape(-1),
    )

    def swap(values, axis, size, distance):
        return lax.ppermute(values, axis, [(at, at ^ distance) for at in range(size)])

    greens = jnp.stack(
        [
            jnp.swapaxes(occupied_tiles.reshape(-1, tile, tile), 1, 2),
            virtual_tiles.reshape(-1, tile, tile),
        ]
    )
    held = greens.shape[1]
    greens = jnp.stack([greens] + [swap(greens, "grp", planes, j) for j in range(1, planes)])
    pairs = list(pair_tiles(scalars, integrals, parts))
    pairs[3] = swap(pairs[3], "blk", parts, 6)
    near_off = picked_rows(scalars, integrals, 1, (3, 2))
    across = picked_square(scalars, integrals, 2, (0, 1))

    slot = jnp.arange(NT, dtype=jnp.int32)
    ordered = jnp.zeros((NT,), jnp.int32).at[tile_owner].set(slot)
    ordered = (ordered // columns ^ group) * columns + ordered % columns
    nearby = (slot // columns ^ group) * columns + slot % columns

    def table(targets, offsets):
        natural = (targets[:, None] - offsets[None, :]) % NT
        flat = natural * kcount + jnp.arange(kcount, dtype=jnp.int32)[None, :]
        device = flat // held
        plane, other = device // parts ^ group, device % parts ^ part
        at = ((other * planes + plane) * held) + flat % held
        return ordered[natural].reshape(-1), at.reshape(-1)

    occupied_table = table(tile_owner[nearby], occupied_offsets)
    virtual_table = table(tile_owner[nearby], virtual_offsets)

    greens, near_off, across, scalars = lax.optimization_barrier(
        (greens, near_off, across, scalars)
    )
    greens = [greens] + [swap(greens, "blk", parts, m) for m in (2, 4)]
    near_off = swap(near_off, "grp", planes, 1)
    across = swap(across, "grp", planes, 2)
    near = picked_square(scalars, integrals, 1)
    far = picked_square(scalars, integrals, 3)

    greens, near_off, across, near, far, pairs, scalars = lax.optimization_barrier(
        (greens, near_off, across, near, far, pairs, scalars)
    )
    greens = [
        greens[0],
        greens[1],
        swap(greens[1], "blk", parts, 1),
        greens[2],
        swap(greens[1][: planes // 2], "blk", parts, 4),
        swap(greens[2][planes // 2 :], "blk", parts, 2),
    ]
    near = swap(near, "grp", planes, 1)
    far = swap(far, "grp", planes, 3)
    own = picked_rows(scalars, integrals, 0, (0, 1, 2, 3))

    greens, near, far, own, pairs, occupied_table, virtual_table = lax.optimization_barrier(
        (greens, near, far, own, pairs, occupied_table, virtual_table)
    )
    greens = [
        greens[0],
        swap(greens[0], "blk", parts, 1),
        *greens[1:4],
        swap(greens[3], "blk", parts, 1),
        *greens[4:],
        swap(greens[4], "blk", parts, 1),
        swap(greens[5], "blk", parts, 1),
    ]
    for m in (1, 2):
        pairs[m] = swap(pairs[m], "blk", parts, 2 * m)

    where = scalars[0]

    def vmem(*shape, dtype=jnp.bfloat16):
        return pltpu.VMEM(shape, dtype)

    devices = planes * parts
    green = vmem(devices * held, tile, tile)

    cross, within = strips_of(columns)

    def strips(count, strips):
        return jax.ShapeDtypeStruct((count, strips, tile // parts, tile), jnp.bfloat16)

    product = vmem(NT, NT // 2, tile, tile, dtype=jnp.float32)

    column_blocks = (
        ((0, 0, False), (0, 1, False), (0, 2, False), (0, 3, False)),
        ((0, 1, True), (1, None, False), (2, 0, False), (2, 1, False)),
        ((0, 2, True), (2, 0, True), (3, None, False), (3, 1, False)),
        ((0, 3, True), (2, 1, True), (3, 1, True), (4, None, False)),
    )
    half = vmem(NT, basis_size, tile)
    sent, halves = kernel_call(
        functools.partial(first_kernel, kcount, columns, column_blocks, len(greens)),
        (where,) + occupied_table + virtual_table,
        greens,
        (own, near, near_off, across, far),
        [strips(devices, within), jax.ShapeDtypeStruct((NT, basis_size, tile), jnp.bfloat16)],
        [pltpu.VMEM, pl.ANY],
        [
            green,
            green,
            vmem(basis_size, basis_size),
            half,
            product,
            pltpu.SemaphoreType.DMA((devices,)),
            pltpu.SemaphoreType.DMA((devices + 1,)),
        ],
        "half_and_pairs",
    )
    sent, halves, pairs = lax.optimization_barrier((sent, halves, pairs))
    pairs[4] = swap(pairs[4], "blk", parts, 6)
    pairs[3:] = [pairs[3][2:], pairs[4], swap(pairs[3][:2], "blk", parts, 1)]
    pairs = [
        each
        for mine in pairs[:3]
        for each in (mine[:2], swap(mine[2:], "blk", parts, 1))
    ] + pairs[3:]
    (rest,) = kernel_call(
        functools.partial(rest_kernel, kcount, columns, len(greens)),
        (where,) + virtual_table,
        [*greens, halves],
        (),
        [strips(2 * parts, cross)],
        [pltpu.VMEM],
        [
            green,
            half,
            product,
            pltpu.SemaphoreType.DMA((devices + 1,)),
        ],
        "other_pairs",
        flops=2 * 8 * basis_size * kcount * tile * tile * 2,
    )

    def everyone(values, groups=None):
        return lax.all_to_all(
            values, ("grp", "blk"), split_axis=0, concat_axis=0, tiled=True,
            axis_index_groups=groups,
        )

    sent = everyone(sent)
    sent, rest, pairs = lax.optimization_barrier((sent, rest, pairs))
    rest = everyone(rest, [list(range(2 * parts)), list(range(2 * parts, devices))])
    pairs = [each.reshape((-1,) + each.shape[2:]) for each in pairs]

    partial_sum = paired(sent, pairs, cross, within).reshape(-1, 2, 2, parts)
    here = (jnp.arange(2, dtype=jnp.int32) == group // 2)[:, None, None]
    crossing = paired(rest, pairs, 0, cross).reshape(-1, 1, 2, parts)
    partial_sum = (partial_sum + jnp.where(here, crossing, 0.0)) * (1.0 / basis_size)
    partial_sum = partial_sum.reshape(parts, aux_local, planes, parts)
    partial_sum = partial_sum[jnp.arange(parts, dtype=jnp.int32) ^ part]
    partial_sum = partial_sum.transpose(3, 2, 0, 1).reshape(1, parts, planes, -1)
    spread = jnp.broadcast_to(partial_sum, (planes,) + partial_sum.shape[1:])
    spread = everyone(spread.reshape((devices,) + partial_sum.shape[2:]))
    return jnp.sum(spread, axis=0)


def solution(mesh):
    planes, parts = mesh.shape["grp"], mesh.shape["blk"]

    def body(*args):
        aux_local, basis_size, width = args[0].shape
        tile = basis_size // NT
        fits = aux_local == planes == 4 and parts == 8 and width % tile == 0 and tile % (16 * parts) == 0 and width == 4 * tile
        return (folded_body if fits else general_body)(*args)

    in_specs = (
        P("blk", None, "grp"),
        P(),
        P(),
        P(("grp", "blk"), None),
        P(),
        P(("grp", "blk"), None),
        P(),
    )
    out_specs = P("blk", None)
    return jax.shard_map(body, mesh=mesh, in_specs=in_specs, out_specs=out_specs, check_vma=False)
```

time: 299 us -> 250 us (0.84)
  waiting for transfers between devices: 129 us -> 86.5 us
  Pallas kernels: 91.3 us -> 80.6 us
  starting transfers between devices: 31 us -> 37.6 us
  matrix products: 6.2 us -> 0 us
  local copies, waits for them, and re-layouts: 23.3 us -> 28.3 us
    ppermute x21 -> x24, waiting for transfers between devices: 70.5 us -> 46.6 us  [swap(): lax.ppermute(values, axis, [(at, at ^ distance) for at in range(size)])]
    pallas_call x3 -> x2, Pallas kernels: 66.5 us -> 44.6 us  [kernel_call(): pl.pallas_call(kernel, in_specs=[pl.BlockSpec(memory_space=pltpu.SMEM)] *...]
    pallas_call x0 -> x5, Pallas kernels: none -> 19.7 us  [the longest x2 11.4 us: paired(): pl.pallas_call(functools.partial(paired_kernel, first, parts), in_specs=[...]
    all_to_all x2, waiting for transfers between devices: 59 us -> 39.9 us  [everyone(): lax.all_to_all(values, ('grp', 'blk'), split_axis=0, concat_axis=0, tiled...]
    slice x2 -> x7, local copies, waits for them, and re-layouts: 2.5 us -> 14.1 us  [the longest x3 8.45 us: folded_body(): mine[2:]]
    pallas_call x5 -> x2, Pallas kernels: 16.2 us -> 7.67 us  [picked_rows(): pl.pallas_call(functools.partial(picked_kernel, columns, planes_of), grid...]
    dot_general x2 -> x0, matrix products: 6.2 us -> none  [folded_body(): jnp.einsum('pe,qe->pq', each.reshape(devices, -1), theirs, preferred_elem...]
    ppermute x21 -> x24, starting transfers between devices: 23.6 us -> 29.2 us  [swap(): lax.ppermute(values, axis, [(at, at ^ distance) for at in range(size)])]
  transfers between devices with their start and end apart: 23 -> 26, of which waited for: 11 -> 9; matrix products, arithmetic and copies ran while one was open for 7% -> 9% of each run, Pallas kernels for 22% -> 30%
where the time goes in v5:
time: 250 us; the launch traced here: 249 us
  waiting for transfers between devices  86.5 us (35%)
  Pallas kernels  80.6 us (32%)
  starting transfers between devices  37.6 us (15%)
  local copies, waits for them, and re-layouts  28.3 us (11%)
  blocking collectives  11.3 us (5%)
  other arithmetic  3.97 us (2%)
    ppermute x24, waiting for transfers between devices, swap(): lax.ppermute(values, axis, [(at, at ^ distance) for at in range(size)])  46.6 us
    pallas_call x2, Pallas kernels, kernel_call(): pl.pallas_call(kernel, in_specs=[pl.BlockSpec(memory_space=pltpu.SMEM)] *...  44.6 us
    all_to_all x2, waiting for transfers between devices, everyone(): lax.all_to_all(values, ('grp', 'blk'), split_axis=0, concat_axis=0, tiled...  39.9 us
    ppermute x24, starting transfers between devices, swap(): lax.ppermute(values, axis, [(at, at ^ distance) for at in range(size)])  29.2 us
    pallas_call x2, Pallas kernels, paired(): pl.pallas_call(functools.partial(paired_kernel, first, parts), in_specs=[...  11.4 us
    all_to_all x1, blocking collectives, everyone(): lax.all_to_all(values, ('grp', 'blk'), split_axis=0, concat_axis=0, tiled...  11.3 us
    pallas_call x1, Pallas kernels, pair_tiles(): pl.pallas_call(functools.partial(pair_kernel, columns), grid_spec=pltpu.P...  8.64 us
    slice x3, local copies, waits for them, and re-layouts, folded_body(): mine[2:]  8.45 us
  transfers between devices with their start and end apart: 26, of which 9 were waited for; matrix products, arithmetic and copies ran while one was open for 9% of the time, Pallas kernels for 30%

profile of v5, /device:TPU:0, one launch (start us, length us, event | category | flops | bytes accessed | tf_op | source)
XLA Modules:
  0.0 248.7 jit_solution(8627551902340641291)
XLA Ops:
  0.0 1.0 copy.17
  1.0 0.9 fusion.24
  2.0 3.1 %collective-permute-start = (bf16[2,4,128,128]{3,2,1,0:T(8,128)(2,1)S(1)}, bf16[2,4,128,128]{3,2,1,0:T(8,128)(2,1)S(1)}, u32[]{:S(2)}, u32[]{:S(2)}) collective-permute-start(bf16[2,4,128,128]{3,2,1,0:T(8,128)(2,1)S(1)} %get-tuple-element.140), channel_id=1, source_target_pairs={{0,8},{8,0},{16,24},{24,16},{1,9},{9,1},{17,25},{25,17},{2,10},{10... | collective-permute-start | bytes 786440 | tf_op jit(solution)/shard_map/ppermute | solution.py:567
  5.1 2.6 %collective-permute-start.1 = (bf16[2,4,128,128]{3,2,1,0:T(8,128)(2,1)S(1)}, bf16[2,4,128,128]{3,2,1,0:T(8,128)(2,1)S(1)}, u32[]{:S(2)}, u32[]{:S(2)}) collective-permute-start(bf16[2,4,128,128]{3,2,1,0:T(8,128)(2,1)S(1)} %get-tuple-element.140), channel_id=1, source_target_pairs={{0,16},{8,24},{16,0},{24,8},{1,17},{9,25},{17,1},{25,9},{2,18},{10... | collective-permute-start | bytes 786440 | tf_op jit(solution)/shard_map/ppermute | solution.py:567
  7.7 1.3 reshape.323.mask_ref
  9.7 8.6 %pair_tiles.1 = (bf16[4,2,49,16,128]{4,3,2,1,0:T(8,128)(2,1)}, bf16[4,2,49,16,128]{4,3,2,1,0:T(8,128)(2,1)}, bf16[4,2,49,16,128]{4,3,2,1,0:T(8,128)(2,1)}, bf16[...) custom-call(s32[2]{0:T(128)} %pad_add_fusion.where_ref.group_ref, s32[16]{0:T(128)} %owner_ref.8, ...), custom_call_target="tpu_custom_call" | custom-call | tf_op jit(solution)/shard_map/pair_tiles/pallas_call | solution.py:277
  18.3 2.7 %collective-permute-start.7 = (bf16[3,2,49,16,128]{4,3,2,1,0:T(8,128)(2,1)}, bf16[3,2,49,16,128]{4,3,2,1,0:T(8,128)(2,1)}, u32[]{:S(2)}, u32[]{:S(2)}) collective-permute-start(bf16[3,2,49,16,128]{4,3,2,1,0:T(8,128)(2,1)} %get-tuple-element.78), channel_id=1, source_target_pairs={{0,6},{1,7},{2,4},{3,5},{4,2},{5,3},{6,0},{7,1},{8,14},{9,15},{10,... | collective-permute-start | bytes 3612680 | tf_op jit(solution)/shard_map/ppermute | solution.py:567
  21.0 2.9 %picked_rows.2 = bf16[8,128,512]{2,1,0:T(8,128)(2,1)} custom-call(s32[2]{0:T(128)} %pad_add_fusion.where_ref.group_ref, s32[16]{0:T(128)} %owner_ref.8, s32[256]{0:T(256)} %reshape.323.mask_ref, bf16[4,16,128,512]{3,2,1,0:T(8,128)(2,1)} %bitcast.40, bf16[4,16,128,512]{3,2,1,0:T(8,128)(2,1)} %bitcast.41, bf16[4,16,128,512]{3,2,1,0:T(8,128)(2,1)} %bitcast.42, ...), custom_call_target="tpu_custom_call" | custom-call | tf_op jit(solution)/shard_map/picked_rows/pallas_call | solution.py:170
  23.9 3.0 %picked_square.3 = bf16[26,128,128]{2,1,0:T(8,128)(2,1)} custom-call(s32[2]{0:T(128)} %pad_add_fusion.where_ref.group_ref, s32[16]{0:T(128)} %owner_ref.8, s32[256]{0:T(256)} %reshape.323.mask_ref, bf16[4,16,128,512]{3,2,1,0:T(8,128)(2,1)} %bitcast.49, bf16[4,16,128,512]{3,2,1,0:T(8,128)(2,1)} %bitcast.45, bf16[4,16,128,512]{3,2,1,0:T(8,128)(2,1)} %bitcast.46, ...), custom_call_target="tpu_custom_call" | custom-call | tf_op jit(solution)/shard_map/picked_square/pallas_call | solution.py:136
  27.1 1.0 collective-permute-start.3
  28.1 1.5 collective-permute-start.4
  29.7 4.8 %collective-permute-start.5 = (bf16[8,128,512]{2,1,0:T(8,128)(2,1)}, bf16[8,128,512]{2,1,0:T(8,128)(2,1)}, u32[]{:S(2)}, u32[]{:S(2)}) collective-permute-start(bf16[8,128,512]{2,1,0:T(8,128)(2,1)} %picked_rows.2), channel_id=1, source_target_pairs={{0,8},{8,0},{16,24},{24,16},{1,9},{9,1},{17,25},{25,17},{2,10},{10... | collective-permute-start | bytes 3145736 | tf_op jit(solution)/shard_map/ppermute | solution.py:567
  34.4 1.0 collective-permute-start.6
  36.5 2.6 %picked_square.5 = bf16[10,128,128]{2,1,0:T(8,128)(2,1)} custom-call(s32[2]{0:T(128)} %pad_add_fusion.where_ref.group_ref, s32[16]{0:T(128)} %owner_ref.8, s32[256]{0:T(256)} %reshape.323.mask_ref, bf16[4,16,128,512]{3,2,1,0:T(8,128)(2,1)} %bitcast.52, bf16[4,16,128,512]{3,2,1,0:T(8,128)(2,1)} %bitcast.53, bf16[4,16,128,512]{3,2,1,0:T(8,128)(2,1)} %bitcast.54, ...), custom_call_target="tpu_custom_call" | custom-call | tf_op jit(solution)/shard_map/picked_square/pallas_call | solution.py:136
  39.1 2.7 %picked_square.4 = bf16[10,128,128]{2,1,0:T(8,128)(2,1)} custom-call(s32[2]{0:T(128)} %pad_add_fusion.where_ref.group_ref, s32[16]{0:T(128)} %owner_ref.8, s32[256]{0:T(256)} %reshape.323.mask_ref, bf16[4,16,128,512]{3,2,1,0:T(8,128)(2,1)} %bitcast.56, bf16[4,16,128,512]{3,2,1,0:T(8,128)(2,1)} %bitcast.57, bf16[4,16,128,512]{3,2,1,0:T(8,128)(2,1)} %bitcast.58, ...), custom_call_target="tpu_custom_call" | custom-call | tf_op jit(solution)/shard_map/picked_square/pallas_call | solution.py:136
  41.8 32.0 %collective-permute-done.6.refs_13_ = bf16[26,128,128]{2,1,0:T(8,128)(2,1)} collective-permute-done((bf16[26,128,128]{2,1,0:T(8,128)(2,1)}, bf16[26,128,128]{2,1,0:T(8,128)(2,1)}, u32[]{:S(2)}, u32[]{:S(2)}) %collective-permute-start.6) | collective-permute-done | bytes 852000 | tf_op jit(solution)/shard_map/ppermute | solution.py:567
  74.8 0.8 scatter_custom_fusion
  75.7 0.8 slice.30
  76.5 0.9 slice.31
  78.4 1.8 gather_fusion.1
  80.2 2.9 %collective-permute-start.11 = (bf16[10,128,128]{2,1,0:T(8,128)(2,1)}, bf16[10,128,128]{2,1,0:T(8,128)(2,1)}, u32[]{:S(2)}, u32[]{:S(2)}) collective-permute-start(bf16[10,128,128]{2,1,0:T(8,128)(2,1)} %picked_square.4), channel_id=1, source_target_pairs={{0,8},{8,0},{16,24},{24,16},{1,9},{9,1},{17,25},{25,17},{2,10},{10... | collective-permute-start | bytes 983048 | tf_op jit(solution)/shard_map/ppermute | solution.py:567
  83.1 1.4 collective-permute-start.12
  84.4 1.7 gather_fusion.2
  86.8 4.7 %picked_rows.3.refs_10_ = bf16[16,128,512]{2,1,0:T(8,128)(2,1)} custom-call(s32[2]{0:T(128)} %pad_add_fusion.where_ref.group_ref, s32[16]{0:T(128)} %owner_ref.8, s32[256]{0:T(256)} %reshape.323.mask_ref, bf16[4,16,128,512]{3,2,1,0:T(8,128)(2,1)} %bitcast.60, bf16[4,16,128,512]{3,2,1,0:T(8,128)(2,1)} %bitcast.61, bf16[4,16,128,512]{3,2,1,0:T(8,128)(2,1)} %bitcast.62, ...), custom_call_target="tpu_custom_call" | custom-call | tf_op jit(solution)/shard_map/picked_rows/pallas_call | solution.py:170
  91.5 7.8 %collective-permute-done.12.refs_14_ = bf16[10,128,128]{2,1,0:T(8,128)(2,1)} collective-permute-done((bf16[10,128,128]{2,1,0:T(8,128)(2,1)S(1)}, bf16[10,128,128]{2,1,0:T(8,128)(2,1)}, u32[]{:S(2)}, u32[]{:S(2)}) %collective-permute-start.12) | collective-permute-done | bytes 327712 | tf_op jit(solution)/shard_map/ppermute | solution.py:567
  99.3 1.6 collective-permute-start.17
  100.8 1.5 collective-permute-start.18
  102.9 2.2 collective-permute-done.15.refs_8_
  105.3 2.9 %collective-permute-done.16.refs_9_ = bf16[2,2,4,128,128]{4,3,2,1,0:T(8,128)(2,1)S(1)} collective-permute-done((bf16[2,2,4,128,128]{4,3,2,1,0:T(8,128)(2,1)}, bf16[2,2,4,128,128]{4,3,2,1,0:T(8,128)(2,1)S(1)}, u32[]{:S(2)}, u32[]{:S(2)}) %collective-permute-start.16) | collective-permute-done | bytes 524320 | tf_op jit(solution)/shard_map/ppermute | solution.py:567
  108.2 0.8 copy-done.10
  109.0 1.0 copy-done.8
  110.0 26.8 %half_and_pairs.1 = (bf16[32,17,16,128]{3,2,1,0:T(8,128)(2,1)}, bf16[16,2048,128]{2,1,0:T(8,128)(2,1)}) custom-call(s32[2]{0:T(128)} %pad_add_fusion.where_ref.group_ref, s32[128]{0:T(128)} %gather_fusion.1, s32[128]{0:T(128)} %get-tuple-element.94.tile_ref, s32[128]{0:T(128)} %gather_fusion.2, s32[128]{0:T(128)} %get-tuple-element.96.virtual_tile_ref, ...), custom_call_target="tpu_custom_call" | custom-call | tf_op jit(solution)/shard_map/half_and_pairs/pallas_call | solution.py:479
  136.9 4.0 %all-to-all-start = ((bf16[32,17,16,128]{3,2,1,0:T(8,128)(2,1)}), bf16[32,17,16,128]{3,2,1,0:T(8,128)(2,1)S(1)}, u32[]{:S(2)}, u32[]{:S(2)}) async-start(bf16[32,17,16,128]{3,2,1,0:T(8,128)(2,1)} %get-tuple-element.115), calls=%async_computation | async-start | bytes 4456448 | tf_op jit(solution)/shard_map/all_to_all | solution.py:703
  141.0 2.8 %fusion.27 = (bf16[2,2,49,16,128]{4,3,2,1,0:T(8,128)(2,1)}, bf16[2,2,49,16,128]{4,3,2,1,0:T(8,128)(2,1)}) fusion(bf16[4,2,49,16,128]{4,3,2,1,0:T(8,128)(2,1)} %get-tuple-element.117), kind=kLoop, calls=%fused_computation.94 | loop fusion | bytes 3211264 | tf_op jit(solution)/shard_map/slice | solution.py:683
  143.8 2.8 %fusion.26 = (bf16[2,2,49,16,128]{4,3,2,1,0:T(8,128)(2,1)}, bf16[2,2,49,16,128]{4,3,2,1,0:T(8,128)(2,1)}) fusion(bf16[4,2,49,16,128]{4,3,2,1,0:T(8,128)(2,1)} %collective-permute-done.17), kind=kLoop, calls=%fused_computation.93 | loop fusion | bytes 3211264 | tf_op jit(solution)/shard_map/slice | solution.py:683
  147.1 2.8 %fusion.25 = (bf16[2,2,49,16,128]{4,3,2,1,0:T(8,128)(2,1)}, bf16[2,2,49,16,128]{4,3,2,1,0:T(8,128)(2,1)}) fusion(bf16[4,2,49,16,128]{4,3,2,1,0:T(8,128)(2,1)} %collective-permute-done.18), kind=kLoop, calls=%fused_computation.92 | loop fusion | bytes 3211264 | tf_op jit(solution)/shard_map/slice | solution.py:683
  150.0 2.2 slice.39
  152.6 2.5 collective-permute-start.22
  155.1 17.8 %other_pairs.1 = bf16[16,32,16,128]{3,2,1,0:T(8,128)(2,1)} custom-call(s32[2]{0:T(128)} %pad_add_fusion.where_ref.group_ref, s32[128]{0:T(128)} %gather_fusion.2, s32[128]{0:T(128)} %get-tuple-element.96.virtual_tile_ref, bf16[4,2,4,128,128]{4,3,2,1,0:T(8,128)(2,1)} %copy-done.3, bf16[4,2,4,128,128]{4,3,2,1,0:T(8,128)(2,1)} %copy-done.8, ...), custom_call_target="tpu_custom_call" | custom-call | flops 8589934592 | bytes 16777216 | tf_op jit(solution)/shard_map/other_pairs/pallas_call | solution.py:479
  172.9 1.8 slice.38
  175.5 17.2 %all-to-all-done.left_ref = bf16[32,17,16,128]{3,2,1,0:T(8,128)(2,1)S(1)} async-done(((bf16[32,17,16,128]{3,2,1,0:T(8,128)(2,1)}), bf16[32,17,16,128]{3,2,1,0:T(8,128)(2,1)S(1)}, u32[]{:S(2)}, u32[]{:S(2)}) %all-to-all-start) | async-done | bytes 2228256 | tf_op jit(solution)/shard_map/all_to_all | solution.py:703
  192.7 1.4 copy-done.2
  194.1 4.4 %all-to-all-start.1 = ((bf16[16,32,16,128]{3,2,1,0:T(8,128)(2,1)}), bf16[16,32,16,128]{3,2,1,0:T(8,128)(2,1)}, u32[]{:S(2)}, u32[]{:S(2)}) async-start(bf16[16,32,16,128]{3,2,1,0:T(8,128)(2,1)} %other_pairs.1), calls=%async_computation.1 | async-start | bytes 4194304 | tf_op jit(solution)/shard_map/all_to_all | solution.py:703
  198.7 5.5 %paired.2 = f32[32,32]{1,0:T(8,128)} custom-call(bf16[32,17,16,128]{3,2,1,0:T(8,128)(2,1)} %copy-done.2, bf16[4,49,16,128]{3,2,1,0:T(8,128)(2,1)} %bitcast.64, bf16[4,49,16,128]{3,2,1,0:T(8,128)(2,1)} %bitcast.72, bf16[4,49,16,128]{3,2,1,0:T(8,128)(2,1)} %bitcast.66, bf16[4,49,16,128]{3,2,1,0:T(8,128)(2,1)} %bitcast.15.refs_3_, ...), custom_call_target="tpu_custom_call" | custom-call | tf_op jit(solution)/shard_map/paired/pallas_call | solution.py:528
  204.3 0.8 reshape.336
  205.1 22.7 %all-to-all-done.1.left_ref = bf16[16,32,16,128]{3,2,1,0:T(8,128)(2,1)} async-done(((bf16[16,32,16,128]{3,2,1,0:T(8,128)(2,1)}), bf16[16,32,16,128]{3,2,1,0:T(8,128)(2,1)}, u32[]{:S(2)}, u32[]{:S(2)}) %all-to-all-start.1) | async-done | bytes 2097184 | tf_op jit(solution)/shard_map/all_to_all | solution.py:703
  227.8 5.9 %paired.3 = f32[32,16]{1,0:T(8,128)} custom-call(bf16[16,32,16,128]{3,2,1,0:T(8,128)(2,1)} %all-to-all-done.1.left_ref, bf16[4,49,16,128]{3,2,1,0:T(8,128)(2,1)} %bitcast.65, bf16[4,49,16,128]{3,2,1,0:T(8,128)(2,1)} %bitcast.73, bf16[4,49,16,128]{3,2,1,0:T(8,128)(2,1)} %bitcast.67, bf16[4,49,16,128]{3,2,1,0:T(8,128)(2,1)} %bitcast.15.refs_3_, ...), custom_call_target="tpu_custom_call" | custom-call | tf_op jit(solution)/shard_map/paired/pallas_call | solution.py:528
  235.5 11.3 %all_to_all.15 = f32[32,1,128]{2,1,0:T(1,128)S(1)} all-to-all(f32[32,1,128]{2,1,0:T(1,128)S(1)} %reshape.385), channel_id=1, replica_groups=mesh['grp'=4,'blk'=8] {'grp','blk'}, dimensions={0} | all-to-all | bytes 32768 | tf_op jit(solution)/shard_map/all_to_all | solution.py:703
  (95 shorter events, 11.0 us)
Async XLA Ops:
  2.0 24.9 %collective-permute-start = (bf16[2,4,128,128]{3,2,1,0:T(8,128)(2,1)S(1)}, bf16[2,4,128,128]{3,2,1,0:T(8,128)(2,1)S(1)}, u32[]{:S(2)}, u32[]{:S(2)}) collective-permute-start(bf16[2,4,128,128]{3,2,1,0:T(8,128)(2,1)S(1)} %get-tuple-element.140), channel_id=1, source_target_pairs={{0,8},{8,0},{16,24},{24,16},{1,9},{9,1},{17,25},{25,17},{2,10},{10... | collective-permute-start | bytes 786440 | tf_op jit(solution)/shard_map/ppermute | solution.py:567
  5.1 21.9 %collective-permute-start.1 = (bf16[2,4,128,128]{3,2,1,0:T(8,128)(2,1)S(1)}, bf16[2,4,128,128]{3,2,1,0:T(8,128)(2,1)S(1)}, u32[]{:S(2)}, u32[]{:S(2)}) collective-permute-start(bf16[2,4,128,128]{3,2,1,0:T(8,128)(2,1)S(1)} %get-tuple-element.140), channel_id=1, source_target_pairs={{0,16},{8,24},{16,0},{24,8},{1,17},{9,25},{17,1},{25,9},{2,18},{10... | collective-permute-start | bytes 786440 | tf_op jit(solution)/shard_map/ppermute | solution.py:567
  7.7 19.3 %collective-permute-start.2 = (bf16[2,4,128,128]{3,2,1,0:T(8,128)(2,1)S(1)}, bf16[2,4,128,128]{3,2,1,0:T(8,128)(2,1)S(1)}, u32[]{:S(2)}, u32[]{:S(2)}) collective-permute-start(bf16[2,4,128,128]{3,2,1,0:T(8,128)(2,1)S(1)} %get-tuple-element.140), channel_id=1, source_target_pairs={{0,24},{8,16},{16,8},{24,0},{1,25},{9,17},{17,9},{25,1},{2,26},{10... | collective-permute-start | bytes 786440 | tf_op jit(solution)/shard_map/ppermute | solution.py:567
  18.3 55.5 %collective-permute-start.7 = (bf16[3,2,49,16,128]{4,3,2,1,0:T(8,128)(2,1)}, bf16[3,2,49,16,128]{4,3,2,1,0:T(8,128)(2,1)}, u32[]{:S(2)}, u32[]{:S(2)}) collective-permute-start(bf16[3,2,49,16,128]{4,3,2,1,0:T(8,128)(2,1)} %get-tuple-element.78), channel_id=1, source_target_pairs={{0,6},{1,7},{2,4},{3,5},{4,2},{5,3},{6,0},{7,1},{8,14},{9,15},{10,... | collective-permute-start | bytes 3612680 | tf_op jit(solution)/shard_map/ppermute | solution.py:567
  26.9 8.5 %copy-start = (s32[16]{0:T(128)S(1)}, s32[16]{0:T(128)}, u32[]{:S(2)}) copy-start(s32[16]{0:T(128)} %owner_ref.8) | copy-start | bytes 196
  26.9 9.2 %copy-start.12 = (s32[8]{0:T(128)S(1)}, s32[8]{0:T(128)}, u32[]{:S(2)}) copy-start(s32[8]{0:T(128)} %param.13) | copy-start | bytes 100
  26.9 9.2 %copy-start.13 = (s32[8]{0:T(128)S(1)}, s32[8]{0:T(128)}, u32[]{:S(2)}) copy-start(s32[8]{0:T(128)} %param.11) | copy-start | bytes 100
  27.1 75.3 %copy-start.3 = (bf16[4,2,4,128,128]{4,3,2,1,0:T(8,128)(2,1)}, bf16[4,2,4,128,128]{4,3,2,1,0:T(8,128)(2,1)S(1)}, u32[]{:S(2)}) copy-start(bf16[4,2,4,128,128]{4,3,2,1,0:T(8,128)(2,1)S(1)} %pad_maximum_fusion.refs_0_) | copy-start | bytes 3145732
  27.1 46.7 %collective-permute-start.3 = (bf16[4,2,4,128,128]{4,3,2,1,0:T(8,128)(2,1)S(1)}, bf16[4,2,4,128,128]{4,3,2,1,0:T(8,128)(2,1)S(1)}, u32[]{:S(2)}, u32[]{:S(2)}) collective-permute-start(bf16[4,2,4,128,128]{4,3,2,1,0:T(8,128)(2,1)S(1)} %pad_maximum_fusion.refs_0_), channel_id=1, source_target_pairs={{0,2},{1,3},{2,0},{3,1},{4,6},{5,7},{6,4},{7,5},{8,10},{9,11},{10,... | collective-permute-start | bytes 3145736 | tf_op jit(solution)/shard_map/ppermute | solution.py:567
  28.1 45.7 %collective-permute-start.4 = (bf16[4,2,4,128,128]{4,3,2,1,0:T(8,128)(2,1)S(1)}, bf16[4,2,4,128,128]{4,3,2,1,0:T(8,128)(2,1)S(1)}, u32[]{:S(2)}, u32[]{:S(2)}) collective-permute-start(bf16[4,2,4,128,128]{4,3,2,1,0:T(8,128)(2,1)S(1)} %pad_maximum_fusion.refs_0_), channel_id=1, source_target_pairs={{0,4},{1,5},{2,6},{3,7},{4,0},{5,1},{6,2},{7,3},{8,12},{9,13},{10,... | collective-permute-start | bytes 3145736 | tf_op jit(solution)/shard_map/ppermute | solution.py:567
  29.7 44.9 %collective-permute-start.5 = (bf16[8,128,512]{2,1,0:T(8,128)(2,1)}, bf16[8,128,512]{2,1,0:T(8,128)(2,1)}, u32[]{:S(2)}, u32[]{:S(2)}) collective-permute-start(bf16[8,128,512]{2,1,0:T(8,128)(2,1)} %picked_rows.2), channel_id=1, source_target_pairs={{0,8},{8,0},{16,24},{24,16},{1,9},{9,1},{17,25},{25,17},{2,10},{10... | collective-permute-start | bytes 3145736 | tf_op jit(solution)/shard_map/ppermute | solution.py:567
  34.4 39.4 %collective-permute-start.6 = (bf16[26,128,128]{2,1,0:T(8,128)(2,1)}, bf16[26,128,128]{2,1,0:T(8,128)(2,1)}, u32[]{:S(2)}, u32[]{:S(2)}) collective-permute-start(bf16[26,128,128]{2,1,0:T(8,128)(2,1)} %picked_square.3), channel_id=1, source_target_pairs={{0,16},{8,24},{16,0},{24,8},{1,17},{9,25},{17,1},{25,9},{2,18},{10... | collective-permute-start | bytes 2555912 | tf_op jit(solution)/shard_map/ppermute | solution.py:567
  39.1 35.7 %copy-start.1 = (s32[16]{0:T(128)S(1)}, s32[16]{0:T(128)}, u32[]{:S(2)}) copy-start(s32[16]{0:T(128)} %owner_ref.8) | copy-start | bytes 196
  73.8 6.4 %copy-start.5 = (bf16[4,2,4,128,128]{4,3,2,1,0:T(8,128)(2,1)}, bf16[4,2,4,128,128]{4,3,2,1,0:T(8,128)(2,1)S(1)}, u32[]{:S(2)}) copy-start(bf16[4,2,4,128,128]{4,3,2,1,0:T(8,128)(2,1)S(1)} %collective-permute-done.3.refs_2_) | copy-start | bytes 3145732
  73.8 29.0 %copy-start.6 = (bf16[4,2,4,128,128]{4,3,2,1,0:T(8,128)(2,1)}, bf16[4,2,4,128,128]{4,3,2,1,0:T(8,128)(2,1)S(1)}, u32[]{:S(2)}) copy-start(bf16[4,2,4,128,128]{4,3,2,1,0:T(8,128)(2,1)S(1)} %collective-permute-done.4.refs_4_) | copy-start | bytes 3145732
  74.5 24.7 %collective-permute-start.8 = (bf16[4,2,4,128,128]{4,3,2,1,0:T(8,128)(2,1)S(1)}, bf16[4,2,4,128,128]{4,3,2,1,0:T(8,128)(2,1)}, u32[]{:S(2)}, u32[]{:S(2)}) collective-permute-start(bf16[4,2,4,128,128]{4,3,2,1,0:T(8,128)(2,1)S(1)} %collective-permute-done.3.refs_2_), channel_id=1, source_target_pairs={{0,1},{1,0},{2,3},{3,2},{4,5},{5,4},{6,7},{7,6},{8,9},{9,8},{10,11... | collective-permute-start | bytes 3145736 | tf_op jit(solution)/shard_map/ppermute | solution.py:567
  77.4 21.9 %collective-permute-start.10 = (bf16[2,2,4,128,128]{4,3,2,1,0:T(8,128)(2,1)}, bf16[2,2,4,128,128]{4,3,2,1,0:T(8,128)(2,1)}, u32[]{:S(2)}, u32[]{:S(2)}) collective-permute-start(bf16[2,2,4,128,128]{4,3,2,1,0:T(8,128)(2,1)} %slice.31), channel_id=1, source_target_pairs={{0,2},{1,3},{2,0},{3,1},{4,6},{5,7},{6,4},{7,5},{8,10},{9,11},{10,... | collective-permute-start | bytes 1572872 | tf_op jit(solution)/shard_map/ppermute | solution.py:567
  77.9 21.4 %collective-permute-start.9 = (bf16[2,2,4,128,128]{4,3,2,1,0:T(8,128)(2,1)}, bf16[2,2,4,128,128]{4,3,2,1,0:T(8,128)(2,1)}, u32[]{:S(2)}, u32[]{:S(2)}) collective-permute-start(bf16[2,2,4,128,128]{4,3,2,1,0:T(8,128)(2,1)} %slice.30), channel_id=1, source_target_pairs={{0,4},{1,5},{2,6},{3,7},{4,0},{5,1},{6,2},{7,3},{8,12},{9,13},{10,... | collective-permute-start | bytes 1572872 | tf_op jit(solution)/shard_map/ppermute | solution.py:567
  78.4 4.6 %copy-start.11 = (bf16[10,128,128]{2,1,0:T(8,128)(2,1)S(1)}, bf16[10,128,128]{2,1,0:T(8,128)(2,1)}, u32[]{:S(2)}) copy-start(bf16[10,128,128]{2,1,0:T(8,128)(2,1)} %picked_square.5) | copy-start | bytes 983044
  80.2 11.3 %collective-permute-start.11 = (bf16[10,128,128]{2,1,0:T(8,128)(2,1)}, bf16[10,128,128]{2,1,0:T(8,128)(2,1)}, u32[]{:S(2)}, u32[]{:S(2)}) collective-permute-start(bf16[10,128,128]{2,1,0:T(8,128)(2,1)} %picked_square.4), channel_id=1, source_target_pairs={{0,8},{8,0},{16,24},{24,16},{1,9},{9,1},{17,25},{25,17},{2,10},{10... | collective-permute-start | bytes 983048 | tf_op jit(solution)/shard_map/ppermute | solution.py:567
  83.1 16.2 %collective-permute-start.12 = (bf16[10,128,128]{2,1,0:T(8,128)(2,1)S(1)}, bf16[10,128,128]{2,1,0:T(8,128)(2,1)}, u32[]{:S(2)}, u32[]{:S(2)}) collective-permute-start(bf16[10,128,128]{2,1,0:T(8,128)(2,1)S(1)} %copy-done.11), channel_id=1, source_target_pairs={{0,24},{8,16},{16,8},{24,0},{1,25},{9,17},{17,9},{25,1},{2,26},{10... | collective-permute-start | bytes 983048 | tf_op jit(solution)/shard_map/ppermute | solution.py:567
  99.3 37.5 %collective-permute-start.17 = (bf16[4,2,49,16,128]{4,3,2,1,0:T(8,128)(2,1)}, bf16[4,2,49,16,128]{4,3,2,1,0:T(8,128)(2,1)}, u32[]{:S(2)}, u32[]{:S(2)}) collective-permute-start(bf16[4,2,49,16,128]{4,3,2,1,0:T(8,128)(2,1)} %get-tuple-element.111), channel_id=1, source_target_pairs={{0,2},{1,3},{2,0},{3,1},{4,6},{5,7},{6,4},{7,5},{8,10},{9,11},{10,... | collective-permute-start | bytes 4816904 | tf_op jit(solution)/shard_map/ppermute | solution.py:567
  100.8 36.1 %collective-permute-start.18 = (bf16[4,2,49,16,128]{4,3,2,1,0:T(8,128)(2,1)}, bf16[4,2,49,16,128]{4,3,2,1,0:T(8,128)(2,1)}, u32[]{:S(2)}, u32[]{:S(2)}) collective-permute-start(bf16[4,2,49,16,128]{4,3,2,1,0:T(8,128)(2,1)} %get-tuple-element.112), channel_id=1, source_target_pairs={{0,4},{1,5},{2,6},{3,7},{4,0},{5,1},{6,2},{7,3},{8,12},{9,13},{10,... | collective-permute-start | bytes 4816904 | tf_op jit(solution)/shard_map/ppermute | solution.py:567
  102.4 2.8 %collective-permute-start.15 = (bf16[2,2,4,128,128]{4,3,2,1,0:T(8,128)(2,1)}, bf16[2,2,4,128,128]{4,3,2,1,0:T(8,128)(2,1)S(1)}, u32[]{:S(2)}, u32[]{:S(2)}) collective-permute-start(bf16[2,2,4,128,128]{4,3,2,1,0:T(8,128)(2,1)} %collective-permute-done.9.refs_6_), channel_id=1, source_target_pairs={{0,1},{1,0},{2,3},{3,2},{4,5},{5,4},{6,7},{7,6},{8,9},{9,8},{10,11... | collective-permute-start | bytes 1572872 | tf_op jit(solution)/shard_map/ppermute | solution.py:567
  102.4 5.9 %collective-permute-start.13 = (bf16[4,2,4,128,128]{4,3,2,1,0:T(8,128)(2,1)S(1)}, bf16[4,2,4,128,128]{4,3,2,1,0:T(8,128)(2,1)S(1)}, u32[]{:S(2)}, u32[]{:S(2)}) collective-permute-start(bf16[4,2,4,128,128]{4,3,2,1,0:T(8,128)(2,1)S(1)} %pad_maximum_fusion.refs_0_), channel_id=1, source_target_pairs={{0,1},{1,0},{2,3},{3,2},{4,5},{5,4},{6,7},{7,6},{8,9},{9,8},{10,11... | collective-permute-start | bytes 3145736 | tf_op jit(solution)/shard_map/ppermute | solution.py:567
  102.9 6.2 %collective-permute-start.14 = (bf16[4,2,4,128,128]{4,3,2,1,0:T(8,128)(2,1)S(1)}, bf16[4,2,4,128,128]{4,3,2,1,0:T(8,128)(2,1)}, u32[]{:S(2)}, u32[]{:S(2)}) collective-permute-start(bf16[4,2,4,128,128]{4,3,2,1,0:T(8,128)(2,1)S(1)} %collective-permute-done.4.refs_4_), channel_id=1, source_target_pairs={{0,1},{1,0},{2,3},{3,2},{4,5},{5,4},{6,7},{7,6},{8,9},{9,8},{10,11... | collective-permute-start | bytes 3145736 | tf_op jit(solution)/shard_map/ppermute | solution.py:567
  105.2 3.9 %copy-start.9 = (bf16[2,2,4,128,128]{4,3,2,1,0:T(8,128)(2,1)}, bf16[2,2,4,128,128]{4,3,2,1,0:T(8,128)(2,1)S(1)}, u32[]{:S(2)}) copy-start(bf16[2,2,4,128,128]{4,3,2,1,0:T(8,128)(2,1)S(1)} %collective-permute-done.15.refs_8_) | copy-start | bytes 1572868
  105.2 3.1 %collective-permute-start.16 = (bf16[2,2,4,128,128]{4,3,2,1,0:T(8,128)(2,1)}, bf16[2,2,4,128,128]{4,3,2,1,0:T(8,128)(2,1)S(1)}, u32[]{:S(2)}, u32[]{:S(2)}) collective-permute-start(bf16[2,2,4,128,128]{4,3,2,1,0:T(8,128)(2,1)} %collective-permute-done.10.refs_7_), channel_id=1, source_target_pairs={{0,1},{1,0},{2,3},{3,2},{4,5},{5,4},{6,7},{7,6},{8,9},{9,8},{10,11... | collective-permute-start | bytes 1572872 | tf_op jit(solution)/shard_map/ppermute | solution.py:567
  108.2 0.8 copy-start.10
  109.0 1.0 copy-start.8
  136.9 55.8 %all-to-all-start = ((bf16[32,17,16,128]{3,2,1,0:T(8,128)(2,1)}), bf16[32,17,16,128]{3,2,1,0:T(8,128)(2,1)S(1)}, u32[]{:S(2)}, u32[]{:S(2)}) async-start(bf16[32,17,16,128]{3,2,1,0:T(8,128)(2,1)} %get-tuple-element.115), calls=%async_computation | async-start | bytes 4456448 | tf_op jit(solution)/shard_map/all_to_all | solution.py:703
  143.8 31.7 %collective-permute-start.19 = (bf16[2,2,49,16,128]{4,3,2,1,0:T(8,128)(2,1)}, bf16[2,2,49,16,128]{4,3,2,1,0:T(8,128)(2,1)S(1)}, u32[]{:S(2)}, u32[]{:S(2)}) collective-permute-start(bf16[2,2,49,16,128]{4,3,2,1,0:T(8,128)(2,1)} %get-tuple-element.137), channel_id=1, source_target_pairs={{0,1},{1,0},{2,3},{3,2},{4,5},{5,4},{6,7},{7,6},{8,9},{9,8},{10,11... | collective-permute-start | bytes 2408456 | tf_op jit(solution)/shard_map/ppermute | solution.py:567
  146.6 28.8 %collective-permute-start.20 = (bf16[2,2,49,16,128]{4,3,2,1,0:T(8,128)(2,1)}, bf16[2,2,49,16,128]{4,3,2,1,0:T(8,128)(2,1)}, u32[]{:S(2)}, u32[]{:S(2)}) collective-permute-start(bf16[2,2,49,16,128]{4,3,2,1,0:T(8,128)(2,1)} %get-tuple-element.135), channel_id=1, source_target_pairs={{0,1},{1,0},{2,3},{3,2},{4,5},{5,4},{6,7},{7,6},{8,9},{9,8},{10,11... | collective-permute-start | bytes 2408456 | tf_op jit(solution)/shard_map/ppermute | solution.py:567
  149.9 2.7 %copy-start.14 = (bf16[1,2,49,16,128]{4,3,2,1,0:T(8,128)(2,1)S(1)}, bf16[1,2,49,16,128]{4,3,2,1,0:T(8,128)(2,1)}, u32[]{:S(2)}) copy-start(bf16[1,2,49,16,128]{4,3,2,1,0:T(8,128)(2,1)} %get-tuple-element.121) | copy-start | bytes 1204228
  149.9 25.5 %collective-permute-start.21 = (bf16[2,2,49,16,128]{4,3,2,1,0:T(8,128)(2,1)}, bf16[2,2,49,16,128]{4,3,2,1,0:T(8,128)(2,1)}, u32[]{:S(2)}, u32[]{:S(2)}) collective-permute-start(bf16[2,2,49,16,128]{4,3,2,1,0:T(8,128)(2,1)} %get-tuple-element.133), channel_id=1, source_target_pairs={{0,1},{1,0},{2,3},{3,2},{4,5},{5,4},{6,7},{7,6},{8,9},{9,8},{10,11... | collective-permute-start | bytes 2408456 | tf_op jit(solution)/shard_map/ppermute | solution.py:567
  152.2 23.3 %collective-permute-start.23 = (bf16[2,2,49,16,128]{4,3,2,1,0:T(8,128)(2,1)}, bf16[2,2,49,16,128]{4,3,2,1,0:T(8,128)(2,1)}, u32[]{:S(2)}, u32[]{:S(2)}) collective-permute-start(bf16[2,2,49,16,128]{4,3,2,1,0:T(8,128)(2,1)} %slice.39), channel_id=1, source_target_pairs={{0,1},{1,0},{2,3},{3,2},{4,5},{5,4},{6,7},{7,6},{8,9},{9,8},{10,11... | collective-permute-start | bytes 2408456 | tf_op jit(solution)/shard_map/ppermute | solution.py:567
  152.6 22.8 %collective-permute-start.22 = (bf16[1,2,49,16,128]{4,3,2,1,0:T(8,128)(2,1)S(1)}, bf16[1,2,49,16,128]{4,3,2,1,0:T(8,128)(2,1)S(1)}, u32[]{:S(2)}, u32[]{:S(2)}) collective-permute-start(bf16[1,2,49,16,128]{4,3,2,1,0:T(8,128)(2,1)S(1)} %copy-done.14), channel_id=1, source_target_pairs={{0,6},{1,7},{2,4},{3,5},{4,2},{5,3},{6,0},{7,1},{8,14},{9,15},{10,... | collective-permute-start | bytes 1204232 | tf_op jit(solution)/shard_map/ppermute | solution.py:567
  175.4 17.3 %copy-start.7 = (bf16[1,2,49,16,128]{4,3,2,1,0:T(8,128)(2,1)}, bf16[1,2,49,16,128]{4,3,2,1,0:T(8,128)(2,1)S(1)}, u32[]{:S(2)}) copy-start(bf16[1,2,49,16,128]{4,3,2,1,0:T(8,128)(2,1)S(1)} %collective-permute-done.22) | copy-start | bytes 1204228
  175.5 17.3 %copy-start.4 = (bf16[2,2,49,16,128]{4,3,2,1,0:T(8,128)(2,1)}, bf16[2,2,49,16,128]{4,3,2,1,0:T(8,128)(2,1)S(1)}, u32[]{:S(2)}) copy-start(bf16[2,2,49,16,128]{4,3,2,1,0:T(8,128)(2,1)S(1)} %collective-permute-done.19) | copy-start | bytes 2408452
  192.7 1.4 copy-start.2
  194.1 33.7 %all-to-all-start.1 = ((bf16[16,32,16,128]{3,2,1,0:T(8,128)(2,1)}), bf16[16,32,16,128]{3,2,1,0:T(8,128)(2,1)}, u32[]{:S(2)}, u32[]{:S(2)}) async-start(bf16[16,32,16,128]{3,2,1,0:T(8,128)(2,1)} %other_pairs.1), calls=%async_computation.1 | async-start | bytes 4194304 | tf_op jit(solution)/shard_map/all_to_all | solution.py:703

commit v6 on v5

--- a/solution.py
+++ b/solution.py
@@ -9,6 +9,7 @@
 
 NT = 16
 UNROLL = 4
+STEPS = 2
 VMEM_BYTES = 60 * 1024 * 1024
 PARTS = (
     ((0, 0), (0, 1), (1, 0), (1, 1)),
@@ -490,54 +491,88 @@
     )(*tables, *anywhere, *blocks)
 
 
-def paired_kernel(first, parts, left_ref, *refs):
-    right_refs, (out_ref, right, sems) = refs[:parts], refs[parts:]
+def paired_kernel(first, steps, parts, columns, where_ref, left_ref, *refs):
+    right_refs, refs = refs[:parts], refs[parts:]
+    base_refs, (out_ref, left, right, total, sums, sems) = refs[:-6], refs[-6:]
     sources, count, rows, tile = left_ref.shape
+    others = right.shape[0]
+    some = count // steps
     copies = []
-    others = 0
-    for at, ref in enumerate(right_refs):
+    for step in range(steps):
+        here = pl.ds(step * some, some)
+        there = pl.ds(first + step * some, some)
+        pairs = [(left_ref.at[:, here], left.at[:, here])]
+        at = 0
+        for ref in right_refs:
+            place_at = (at // 4 ^ where_ref[1]) * 4 + at % 4
+            pairs.append((ref.at[:, there], right.at[pl.ds(place_at, ref.shape[0]), here]))
+            at += ref.shape[0]
         copies.append(
-            pltpu.make_async_copy(
-                ref.at[:, pl.ds(first, count)],
-                right.at[pl.ds(others, ref.shape[0])],
-                sems.at[at],
-            )
+            [
+                pltpu.make_async_copy(source, target, sems.at[step * (parts + 1) + i])
+                for i, (source, target) in enumerate(pairs)
+            ]
         )
-        others += ref.shape[0]
-    start_all(copies)
-    wait_all(copies)
-    left = jnp.concatenate(
-        [left_ref[:, at].reshape(sources * rows, tile) for at in range(count)], axis=1
-    )
-    right = jnp.concatenate(
-        [right[:, at].reshape(others * rows, tile) for at in range(count)], axis=1
-    )
-    total = lax.dot_general(
-        left, right, (((1,), (1,)), ((), ())), preferred_element_type=jnp.float32
-    )
-    down = lax.broadcasted_iota(jnp.int32, total.shape, 0)
-    along = lax.broadcasted_iota(jnp.int32, total.shape, 1)
-    total = jnp.where((down ^ along) % rows == 0, total, 0.0)
-    total = jnp.sum(total.reshape(sources, rows, others * rows), axis=1)
-    out_ref[...] = jnp.sum(total.T.reshape(others, rows, sources), axis=1)
-
-
-def paired(left, rights, first, count):
+    for each in copies:
+        start_all(each)
+    for step, each in enumerate(copies):
+        wait_all(each)
+        strips = range(step * some, (step + 1) * some)
+        values = lax.dot_general(
+            jnp.concatenate([left[:, i].reshape(sources * rows, tile) for i in strips], axis=1),
+            jnp.concatenate([right[:, i].reshape(others * rows, tile) for i in strips], axis=1),
+            (((1,), (1,)), ((), ())),
+            preferred_element_type=jnp.float32,
+        )
+        if step:
+            total[...] += values
+        else:
+            total[...] = values
+    values = total[...]
+    down = lax.broadcasted_iota(jnp.int32, values.shape, 0)
+    along = lax.broadcasted_iota(jnp.int32, values.shape, 1)
+    values = jnp.where((down ^ along) % rows == 0, values, 0.0)
+    values = jnp.sum(values.reshape(sources, rows, others * rows), axis=1)
+    values = jnp.sum(values.T.reshape(others, rows, sources), axis=1).T
+    if not base_refs:
+        out_ref[...] = values
+        return
+    devices = out_ref.shape[0]
+    each = devices // columns
+    start = pl.multiple_of(where_ref[0] // 2 * sources, sources)
+    out_ref[...] = jnp.zeros_like(out_ref)
+    sums[...] = base_refs[0][...]
+    sums[pl.ds(start, sources), :] += values
+    for blk in range(each):
+        values = sums[pl.ds(blk, columns, stride=each), :] * (1.0 / (NT * tile))
+        for plane in range(columns):
+            out_ref[plane * each + blk, :columns, :others] = values
+
+
+def paired(where, left, rights, first, steps, base=None):
     parts = len(rights)
+    sources, count, rows, tile = left.shape
     others = sum(each.shape[0] for each in rights)
+    vmem = pl.BlockSpec(memory_space=pltpu.VMEM)
+    base = () if base is None else (base,)
+    shape = (base[0].shape[0], 8, 128) if base else (sources, others)
     return pl.pallas_call(
-        functools.partial(paired_kernel, first, parts),
-        in_specs=[pl.BlockSpec(memory_space=pltpu.VMEM)]
-        + [pl.BlockSpec(memory_space=pl.ANY)] * parts,
-        out_specs=pl.BlockSpec(memory_space=pltpu.VMEM),
-        out_shape=jax.ShapeDtypeStruct((others, left.shape[0]), jnp.float32),
+        functools.partial(paired_kernel, first, steps, parts, 4),
+        in_specs=[pl.BlockSpec(memory_space=pltpu.SMEM)]
+        + [pl.BlockSpec(memory_space=pl.ANY)] * (parts + 1)
+        + [vmem] * len(base),
+        out_specs=vmem,
+        out_shape=jax.ShapeDtypeStruct(shape, jnp.float32),
         scratch_shapes=[
-            pltpu.VMEM((others, count) + left.shape[2:], jnp.bfloat16),
-            pltpu.SemaphoreType.DMA((parts,)),
+            pltpu.VMEM(left.shape, jnp.bfloat16),
+            pltpu.VMEM((others,) + left.shape[1:], jnp.bfloat16),
+            pltpu.VMEM((sources * rows, others * rows), jnp.float32),
+            pltpu.VMEM((others, others), jnp.float32),
+            pltpu.SemaphoreType.DMA((steps * (parts + 1),)),
         ],
         compiler_params=pltpu.CompilerParams(vmem_limit_bytes=VMEM_BYTES),
         name="paired",
-    )(left, *rights)
+    )(where, left, *rights, *base)
 
 
 def folded_body(
@@ -710,16 +745,9 @@
     rest = everyone(rest, [list(range(2 * parts)), list(range(2 * parts, devices))])
     pairs = [each.reshape((-1,) + each.shape[2:]) for each in pairs]
 
-    partial_sum = paired(sent, pairs, cross, within).reshape(-1, 2, 2, parts)
-    here = (jnp.arange(2, dtype=jnp.int32) == group // 2)[:, None, None]
-    crossing = paired(rest, pairs, 0, cross).reshape(-1, 1, 2, parts)
-    partial_sum = (partial_sum + jnp.where(here, crossing, 0.0)) * (1.0 / basis_size)
-    partial_sum = partial_sum.reshape(parts, aux_local, planes, parts)
-    partial_sum = partial_sum[jnp.arange(parts, dtype=jnp.int32) ^ part]
-    partial_sum = partial_sum.transpose(3, 2, 0, 1).reshape(1, parts, planes, -1)
-    spread = jnp.broadcast_to(partial_sum, (planes,) + partial_sum.shape[1:])
-    spread = everyone(spread.reshape((devices,) + partial_sum.shape[2:]))
-    return jnp.sum(spread, axis=0)
+    total = paired(where, sent, pairs, cross, 1)
+    total = jnp.sum(everyone(paired(where, rest, pairs, 0, STEPS, total)), axis=0)
+    return total[:aux_local, : parts * aux_local]
 
 
 def solution(mesh):

time: 250 us -> 247 us (0.988)
  local copies, waits for them, and re-layouts: 28.3 us -> 24.4 us
  transfers between devices with their start and end apart: 26 -> 26, of which waited for: 9 -> 11; matrix products, arithmetic and copies ran while one was open for 9% -> 9% of each run, Pallas kernels for 30% -> 30%
where the time goes in v6:
time: 247 us; the launch traced here: 246 us
  waiting for transfers between devices  87.8 us (36%)
  Pallas kernels  79.8 us (32%)
  starting transfers between devices  38.7 us (16%)
  local copies, waits for them, and re-layouts  24.4 us (10%)
  blocking collectives  12.3 us (5%)
  other arithmetic  2.53 us (1%)
    ppermute x24, waiting for transfers between devices, swap(): lax.ppermute(values, axis, [(at, at ^ distance) for at in range(size)])  46.3 us
    pallas_call x2, Pallas kernels, kernel_call(): pl.pallas_call(kernel, in_specs=[pl.BlockSpec(memory_space=pltpu.SMEM)] *...  44.6 us
    all_to_all x2, waiting for transfers between devices, everyone(): lax.all_to_all(values, ('grp', 'blk'), split_axis=0, concat_axis=0, tiled...  41.5 us
    ppermute x24, starting transfers between devices, swap(): lax.ppermute(values, axis, [(at, at ^ distance) for at in range(size)])  29.3 us
    all_to_all x1, blocking collectives, everyone(): lax.all_to_all(values, ('grp', 'blk'), split_axis=0, concat_axis=0, tiled...  12.3 us
    pallas_call x2, Pallas kernels, paired(): pl.pallas_call(functools.partial(paired_kernel, first, steps, parts, 4),...  10.6 us
    all_to_all x2, starting transfers between devices, everyone(): lax.all_to_all(values, ('grp', 'blk'), split_axis=0, concat_axis=0, tiled...  9.39 us
    pallas_call x1, Pallas kernels, pair_tiles(): pl.pallas_call(functools.partial(pair_kernel, columns), grid_spec=pltpu.P...  8.65 us
  transfers between devices with their start and end apart: 26, of which 11 were waited for; matrix products, arithmetic and copies ran while one was open for 9% of the time, Pallas kernels for 30%

profile of v6, /device:TPU:0, one launch (start us, length us, event | category | flops | bytes accessed | tf_op | source)
XLA Modules:
  0.0 245.8 jit_solution(7975027029819716676)
XLA Ops:
  0.0 1.0 copy.8
  1.0 0.9 fusion.23
  2.0 4.1 %collective-permute-start.1 = (bf16[2,4,128,128]{3,2,1,0:T(8,128)(2,1)S(1)}, bf16[2,4,128,128]{3,2,1,0:T(8,128)(2,1)S(1)}, u32[]{:S(2)}, u32[]{:S(2)}) collective-permute-start(bf16[2,4,128,128]{3,2,1,0:T(8,128)(2,1)S(1)} %get-tuple-element.140), channel_id=1, source_target_pairs={{0,16},{8,24},{16,0},{24,8},{1,17},{9,25},{17,1},{25,9},{2,18},{10... | collective-permute-start | bytes 786440 | tf_op jit(solution)/shard_map/ppermute | solution.py:602
  6.1 1.6 collective-permute-start
  7.7 1.3 reshape.293.mask_ref
  9.6 8.7 %pair_tiles.1 = (bf16[4,2,49,16,128]{4,3,2,1,0:T(8,128)(2,1)}, bf16[4,2,49,16,128]{4,3,2,1,0:T(8,128)(2,1)}, bf16[4,2,49,16,128]{4,3,2,1,0:T(8,128)(2,1)}, bf16[...) custom-call(s32[2]{0:T(128)} %pad_add_fusion.where_ref.group_ref, s32[16]{0:T(128)} %owner_ref.8, ...), custom_call_target="tpu_custom_call" | custom-call | tf_op jit(solution)/shard_map/pair_tiles/pallas_call | solution.py:278
  18.2 2.7 %collective-permute-start.7 = (bf16[3,2,49,16,128]{4,3,2,1,0:T(8,128)(2,1)}, bf16[3,2,49,16,128]{4,3,2,1,0:T(8,128)(2,1)}, u32[]{:S(2)}, u32[]{:S(2)}) collective-permute-start(bf16[3,2,49,16,128]{4,3,2,1,0:T(8,128)(2,1)} %get-tuple-element.78), channel_id=1, source_target_pairs={{0,6},{1,7},{2,4},{3,5},{4,2},{5,3},{6,0},{7,1},{8,14},{9,15},{10,... | collective-permute-start | bytes 3612680 | tf_op jit(solution)/shard_map/ppermute | solution.py:602
  20.9 3.0 %picked_square.3 = bf16[26,128,128]{2,1,0:T(8,128)(2,1)} custom-call(s32[2]{0:T(128)} %pad_add_fusion.where_ref.group_ref, s32[16]{0:T(128)} %owner_ref.8, s32[256]{0:T(256)} %reshape.293.mask_ref, bf16[4,16,128,512]{3,2,1,0:T(8,128)(2,1)} %bitcast.33, bf16[4,16,128,512]{3,2,1,0:T(8,128)(2,1)} %bitcast.34, bf16[4,16,128,512]{3,2,1,0:T(8,128)(2,1)} %bitcast.35, ...), custom_call_target="tpu_custom_call" | custom-call | tf_op jit(solution)/shard_map/picked_square/pallas_call | solution.py:137
  23.9 2.9 %picked_rows.2 = bf16[8,128,512]{2,1,0:T(8,128)(2,1)} custom-call(s32[2]{0:T(128)} %pad_add_fusion.where_ref.group_ref, s32[16]{0:T(128)} %owner_ref.8, s32[256]{0:T(256)} %reshape.293.mask_ref, bf16[4,16,128,512]{3,2,1,0:T(8,128)(2,1)} %bitcast.42, bf16[4,16,128,512]{3,2,1,0:T(8,128)(2,1)} %bitcast.41, bf16[4,16,128,512]{3,2,1,0:T(8,128)(2,1)} %bitcast.43, ...), custom_call_target="tpu_custom_call" | custom-call | tf_op jit(solution)/shard_map/picked_rows/pallas_call | solution.py:171
  27.0 3.1 %collective-permute-start.5 = (bf16[8,128,512]{2,1,0:T(8,128)(2,1)}, bf16[8,128,512]{2,1,0:T(8,128)(2,1)}, u32[]{:S(2)}, u32[]{:S(2)}) collective-permute-start(bf16[8,128,512]{2,1,0:T(8,128)(2,1)} %picked_rows.2), channel_id=1, source_target_pairs={{0,8},{8,0},{16,24},{24,16},{1,9},{9,1},{17,25},{25,17},{2,10},{10... | collective-permute-start | bytes 3145736 | tf_op jit(solution)/shard_map/ppermute | solution.py:602
  30.2 1.5 collective-permute-start.4
  31.7 1.5 collective-permute-start.3
  33.2 2.0 collective-permute-start.6
  36.2 2.6 %picked_square.5 = bf16[10,128,128]{2,1,0:T(8,128)(2,1)} custom-call(s32[2]{0:T(128)} %pad_add_fusion.where_ref.group_ref, s32[16]{0:T(128)} %owner_ref.8, s32[256]{0:T(256)} %reshape.293.mask_ref, bf16[4,16,128,512]{3,2,1,0:T(8,128)(2,1)} %bitcast.45, bf16[4,16,128,512]{3,2,1,0:T(8,128)(2,1)} %bitcast.46, bf16[4,16,128,512]{3,2,1,0:T(8,128)(2,1)} %bitcast.47, ...), custom_call_target="tpu_custom_call" | custom-call | tf_op jit(solution)/shard_map/picked_square/pallas_call | solution.py:137
  38.8 2.7 %picked_square.4 = bf16[10,128,128]{2,1,0:T(8,128)(2,1)} custom-call(s32[2]{0:T(128)} %pad_add_fusion.where_ref.group_ref, s32[16]{0:T(128)} %owner_ref.8, s32[256]{0:T(256)} %reshape.293.mask_ref, bf16[4,16,128,512]{3,2,1,0:T(8,128)(2,1)} %bitcast.49, bf16[4,16,128,512]{3,2,1,0:T(8,128)(2,1)} %bitcast.50, bf16[4,16,128,512]{3,2,1,0:T(8,128)(2,1)} %bitcast.51, ...), custom_call_target="tpu_custom_call" | custom-call | tf_op jit(solution)/shard_map/picked_square/pallas_call | solution.py:137
  41.5 29.9 %collective-permute-done.6.refs_13_ = bf16[26,128,128]{2,1,0:T(8,128)(2,1)} collective-permute-done((bf16[26,128,128]{2,1,0:T(8,128)(2,1)}, bf16[26,128,128]{2,1,0:T(8,128)(2,1)}, u32[]{:S(2)}, u32[]{:S(2)}) %collective-permute-start.6) | collective-permute-done | bytes 852000 | tf_op jit(solution)/shard_map/ppermute | solution.py:602
  72.5 0.8 scatter_custom_fusion
  73.3 0.8 slice.33
  74.1 0.8 slice.34
  75.0 1.5 collective-permute-start.9
  76.5 1.5 collective-permute-start.10
  78.0 1.8 gather_fusion.1
  79.8 3.8 %collective-permute-start.11 = (bf16[10,128,128]{2,1,0:T(8,128)(2,1)}, bf16[10,128,128]{2,1,0:T(8,128)(2,1)}, u32[]{:S(2)}, u32[]{:S(2)}) collective-permute-start(bf16[10,128,128]{2,1,0:T(8,128)(2,1)} %picked_square.4), channel_id=1, source_target_pairs={{0,8},{8,0},{16,24},{24,16},{1,9},{9,1},{17,25},{25,17},{2,10},{10... | collective-permute-start | bytes 983048 | tf_op jit(solution)/shard_map/ppermute | solution.py:602
  83.9 1.8 gather_fusion.2
  86.3 4.8 %picked_rows.3.refs_10_ = bf16[16,128,512]{2,1,0:T(8,128)(2,1)} custom-call(s32[2]{0:T(128)} %pad_add_fusion.where_ref.group_ref, s32[16]{0:T(128)} %owner_ref.8, s32[256]{0:T(256)} %reshape.293.mask_ref, bf16[4,16,128,512]{3,2,1,0:T(8,128)(2,1)} %bitcast.53, bf16[4,16,128,512]{3,2,1,0:T(8,128)(2,1)} %bitcast.54, bf16[4,16,128,512]{3,2,1,0:T(8,128)(2,1)} %bitcast.55, ...), custom_call_target="tpu_custom_call" | custom-call | tf_op jit(solution)/shard_map/picked_rows/pallas_call | solution.py:171
  91.1 1.6 collective-permute-done.11.refs_11_
  92.7 6.2 %collective-permute-done.12.refs_14_ = bf16[10,128,128]{2,1,0:T(8,128)(2,1)} collective-permute-done((bf16[10,128,128]{2,1,0:T(8,128)(2,1)S(1)}, bf16[10,128,128]{2,1,0:T(8,128)(2,1)}, u32[]{:S(2)}, u32[]{:S(2)}) %collective-permute-start.12) | collective-permute-done | bytes 327712 | tf_op jit(solution)/shard_map/ppermute | solution.py:602
  99.5 0.8 collective-permute-start.18
  100.9 2.2 collective-permute-done.15.refs_8_
  103.3 2.9 %collective-permute-done.16.refs_9_ = bf16[2,2,4,128,128]{4,3,2,1,0:T(8,128)(2,1)S(1)} collective-permute-done((bf16[2,2,4,128,128]{4,3,2,1,0:T(8,128)(2,1)}, bf16[2,2,4,128,128]{4,3,2,1,0:T(8,128)(2,1)S(1)}, u32[]{:S(2)}, u32[]{:S(2)}) %collective-permute-start.16) | collective-permute-done | bytes 524320 | tf_op jit(solution)/shard_map/ppermute | solution.py:602
  107.0 1.0 copy-done.9
  108.0 26.7 %half_and_pairs.1 = (bf16[32,17,16,128]{3,2,1,0:T(8,128)(2,1)}, bf16[16,2048,128]{2,1,0:T(8,128)(2,1)}) custom-call(s32[2]{0:T(128)} %pad_add_fusion.where_ref.group_ref, s32[128]{0:T(128)} %gather_fusion.1, s32[128]{0:T(128)} %get-tuple-element.94.tile_ref, s32[128]{0:T(128)} %gather_fusion.2, s32[128]{0:T(128)} %get-tuple-element.96.virtual_tile_ref, ...), custom_call_target="tpu_custom_call" | custom-call | tf_op jit(solution)/shard_map/half_and_pairs/pallas_call | solution.py:480
  135.5 5.0 %all-to-all-start = ((bf16[32,17,16,128]{3,2,1,0:T(8,128)(2,1)}), bf16[32,17,16,128]{3,2,1,0:T(8,128)(2,1)S(1)}, u32[]{:S(2)}, u32[]{:S(2)}) async-start(bf16[32,17,16,128]{3,2,1,0:T(8,128)(2,1)} %get-tuple-element.115), calls=%async_computation | async-start | bytes 4456448 | tf_op jit(solution)/shard_map/all_to_all | solution.py:738
  140.5 2.3 slice.42
  142.8 2.5 collective-permute-start.22
  145.3 1.4 fusion.26
  147.2 2.8 %fusion.25 = (bf16[2,2,49,16,128]{4,3,2,1,0:T(8,128)(2,1)}, bf16[2,2,49,16,128]{4,3,2,1,0:T(8,128)(2,1)}) fusion(bf16[4,2,49,16,128]{4,3,2,1,0:T(8,128)(2,1)} %collective-permute-done.17), kind=kLoop, calls=%fused_computation.87 | loop fusion | bytes 3211264 | tf_op jit(solution)/shard_map/slice | solution.py:718
  150.0 2.8 %fusion.24 = (bf16[2,2,49,16,128]{4,3,2,1,0:T(8,128)(2,1)}, bf16[2,2,49,16,128]{4,3,2,1,0:T(8,128)(2,1)}) fusion(bf16[4,2,49,16,128]{4,3,2,1,0:T(8,128)(2,1)} %collective-permute-done.18), kind=kLoop, calls=%fused_computation.86 | loop fusion | bytes 3211264 | tf_op jit(solution)/shard_map/slice | solution.py:718
  153.4 17.9 %other_pairs.1 = bf16[16,32,16,128]{3,2,1,0:T(8,128)(2,1)} custom-call(s32[2]{0:T(128)} %pad_add_fusion.where_ref.group_ref, s32[128]{0:T(128)} %gather_fusion.2, s32[128]{0:T(128)} %get-tuple-element.96.virtual_tile_ref, bf16[4,2,4,128,128]{4,3,2,1,0:T(8,128)(2,1)} %copy-done.3, bf16[4,2,4,128,128]{4,3,2,1,0:T(8,128)(2,1)} %copy-done.9, ...), custom_call_target="tpu_custom_call" | custom-call | flops 8589934592 | bytes 16777216 | tf_op jit(solution)/shard_map/other_pairs/pallas_call | solution.py:480
  171.3 1.8 slice.41
  173.0 2.0 collective-permute-done.22
  175.0 17.5 %all-to-all-done.left_ref = bf16[32,17,16,128]{3,2,1,0:T(8,128)(2,1)S(1)} async-done(((bf16[32,17,16,128]{3,2,1,0:T(8,128)(2,1)}), bf16[32,17,16,128]{3,2,1,0:T(8,128)(2,1)S(1)}, u32[]{:S(2)}, u32[]{:S(2)}) %all-to-all-start) | async-done | bytes 2228256 | tf_op jit(solution)/shard_map/all_to_all | solution.py:738
  192.6 1.4 copy-done.2
  193.9 4.4 %all-to-all-start.1 = ((bf16[16,32,16,128]{3,2,1,0:T(8,128)(2,1)}), bf16[16,32,16,128]{3,2,1,0:T(8,128)(2,1)}, u32[]{:S(2)}, u32[]{:S(2)}) async-start(bf16[16,32,16,128]{3,2,1,0:T(8,128)(2,1)} %other_pairs.1), calls=%async_computation.1 | async-start | bytes 4194304 | tf_op jit(solution)/shard_map/all_to_all | solution.py:738
  198.4 5.3 %paired.2.refs_9_ = f32[32,32]{1,0:T(8,128)} custom-call(s32[2]{0:T(128)} %pad_add_fusion.where_ref.group_ref, bf16[32,17,16,128]{3,2,1,0:T(8,128)(2,1)} %copy-done.2, bf16[4,49,16,128]{3,2,1,0:T(8,128)(2,1)} %bitcast.57, bf16[4,49,16,128]{3,2,1,0:T(8,128)(2,1)} %bitcast.13.refs_1_, bf16[4,49,16,128]{3,2,1,0:T(8,128)(2,1)} %bitcast.59, ...), custom_call_target="tpu_custom_call" | custom-call | tf_op jit(solution)/shard_map/paired/pallas_call | solution.py:559
  203.7 23.9 %all-to-all-done.1.left_ref = bf16[16,32,16,128]{3,2,1,0:T(8,128)(2,1)} async-done(((bf16[16,32,16,128]{3,2,1,0:T(8,128)(2,1)}), bf16[16,32,16,128]{3,2,1,0:T(8,128)(2,1)}, u32[]{:S(2)}, u32[]{:S(2)}) %all-to-all-start.1) | async-done | bytes 2097184 | tf_op jit(solution)/shard_map/all_to_all | solution.py:738
  227.7 5.3 %paired.3 = f32[32,8,128]{2,1,0:T(8,128)} custom-call(s32[2]{0:T(128)} %pad_add_fusion.where_ref.group_ref, bf16[16,32,16,128]{3,2,1,0:T(8,128)(2,1)} %all-to-all-done.1.left_ref, bf16[4,49,16,128]{3,2,1,0:T(8,128)(2,1)} %bitcast.58, bf16[4,49,16,128]{3,2,1,0:T(8,128)(2,1)} %bitcast.13.refs_1_, bf16[4,49,16,128]{3,2,1,0:T(8,128)(2,1)} %bitcast.60, ...), custom_call_target="tpu_custom_call" | custom-call | tf_op jit(solution)/shard_map/paired/pallas_call | solution.py:559
  233.0 12.3 %all_to_all.15 = f32[32,8,128]{2,1,0:T(8,128)S(1)} all-to-all(f32[32,8,128]{2,1,0:T(8,128)} %paired.3), channel_id=1, replica_groups=mesh['grp'=4,'blk'=8] {'grp','blk'}, dimensions={0} | all-to-all | bytes 262144 | tf_op jit(solution)/shard_map/all_to_all | solution.py:738
  (79 shorter events, 8.4 us)
Async XLA Ops:
  2.0 24.9 %collective-permute-start.1 = (bf16[2,4,128,128]{3,2,1,0:T(8,128)(2,1)S(1)}, bf16[2,4,128,128]{3,2,1,0:T(8,128)(2,1)S(1)}, u32[]{:S(2)}, u32[]{:S(2)}) collective-permute-start(bf16[2,4,128,128]{3,2,1,0:T(8,128)(2,1)S(1)} %get-tuple-element.140), channel_id=1, source_target_pairs={{0,16},{8,24},{16,0},{24,8},{1,17},{9,25},{17,1},{25,9},{2,18},{10... | collective-permute-start | bytes 786440 | tf_op jit(solution)/shard_map/ppermute | solution.py:602
  6.1 20.8 %collective-permute-start = (bf16[2,4,128,128]{3,2,1,0:T(8,128)(2,1)S(1)}, bf16[2,4,128,128]{3,2,1,0:T(8,128)(2,1)S(1)}, u32[]{:S(2)}, u32[]{:S(2)}) collective-permute-start(bf16[2,4,128,128]{3,2,1,0:T(8,128)(2,1)S(1)} %get-tuple-element.140), channel_id=1, source_target_pairs={{0,8},{8,0},{16,24},{24,16},{1,9},{9,1},{17,25},{25,17},{2,10},{10... | collective-permute-start | bytes 786440 | tf_op jit(solution)/shard_map/ppermute | solution.py:602
  7.7 19.2 %collective-permute-start.2 = (bf16[2,4,128,128]{3,2,1,0:T(8,128)(2,1)S(1)}, bf16[2,4,128,128]{3,2,1,0:T(8,128)(2,1)S(1)}, u32[]{:S(2)}, u32[]{:S(2)}) collective-permute-start(bf16[2,4,128,128]{3,2,1,0:T(8,128)(2,1)S(1)} %get-tuple-element.140), channel_id=1, source_target_pairs={{0,24},{8,16},{16,8},{24,0},{1,25},{9,17},{17,9},{25,1},{2,26},{10... | collective-permute-start | bytes 786440 | tf_op jit(solution)/shard_map/ppermute | solution.py:602
  18.2 53.1 %collective-permute-start.7 = (bf16[3,2,49,16,128]{4,3,2,1,0:T(8,128)(2,1)}, bf16[3,2,49,16,128]{4,3,2,1,0:T(8,128)(2,1)}, u32[]{:S(2)}, u32[]{:S(2)}) collective-permute-start(bf16[3,2,49,16,128]{4,3,2,1,0:T(8,128)(2,1)} %get-tuple-element.78), channel_id=1, source_target_pairs={{0,6},{1,7},{2,4},{3,5},{4,2},{5,3},{6,0},{7,1},{8,14},{9,15},{10,... | collective-permute-start | bytes 3612680 | tf_op jit(solution)/shard_map/ppermute | solution.py:602
  26.8 8.4 %copy-start = (s32[16]{0:T(128)S(1)}, s32[16]{0:T(128)}, u32[]{:S(2)}) copy-start(s32[16]{0:T(128)} %owner_ref.8) | copy-start | bytes 196
  26.8 9.1 %copy-start.13 = (s32[8]{0:T(128)S(1)}, s32[8]{0:T(128)}, u32[]{:S(2)}) copy-start(s32[8]{0:T(128)} %param.13) | copy-start | bytes 100
  26.8 9.2 %copy-start.14 = (s32[8]{0:T(128)S(1)}, s32[8]{0:T(128)}, u32[]{:S(2)}) copy-start(s32[8]{0:T(128)} %param.11) | copy-start | bytes 100
  27.0 73.3 %copy-start.3 = (bf16[4,2,4,128,128]{4,3,2,1,0:T(8,128)(2,1)}, bf16[4,2,4,128,128]{4,3,2,1,0:T(8,128)(2,1)S(1)}, u32[]{:S(2)}) copy-start(bf16[4,2,4,128,128]{4,3,2,1,0:T(8,128)(2,1)S(1)} %pad_maximum_fusion.refs_0_) | copy-start | bytes 3145732
  27.0 45.1 %collective-permute-start.5 = (bf16[8,128,512]{2,1,0:T(8,128)(2,1)}, bf16[8,128,512]{2,1,0:T(8,128)(2,1)}, u32[]{:S(2)}, u32[]{:S(2)}) collective-permute-start(bf16[8,128,512]{2,1,0:T(8,128)(2,1)} %picked_rows.2), channel_id=1, source_target_pairs={{0,8},{8,0},{16,24},{24,16},{1,9},{9,1},{17,25},{25,17},{2,10},{10... | collective-permute-start | bytes 3145736 | tf_op jit(solution)/shard_map/ppermute | solution.py:602
  30.2 41.9 %collective-permute-start.4 = (bf16[4,2,4,128,128]{4,3,2,1,0:T(8,128)(2,1)S(1)}, bf16[4,2,4,128,128]{4,3,2,1,0:T(8,128)(2,1)S(1)}, u32[]{:S(2)}, u32[]{:S(2)}) collective-permute-start(bf16[4,2,4,128,128]{4,3,2,1,0:T(8,128)(2,1)S(1)} %pad_maximum_fusion.refs_0_), channel_id=1, source_target_pairs={{0,4},{1,5},{2,6},{3,7},{4,0},{5,1},{6,2},{7,3},{8,12},{9,13},{10,... | collective-permute-start | bytes 3145736 | tf_op jit(solution)/shard_map/ppermute | solution.py:602
  31.7 40.4 %collective-permute-start.3 = (bf16[4,2,4,128,128]{4,3,2,1,0:T(8,128)(2,1)S(1)}, bf16[4,2,4,128,128]{4,3,2,1,0:T(8,128)(2,1)S(1)}, u32[]{:S(2)}, u32[]{:S(2)}) collective-permute-start(bf16[4,2,4,128,128]{4,3,2,1,0:T(8,128)(2,1)S(1)} %pad_maximum_fusion.refs_0_), channel_id=1, source_target_pairs={{0,2},{1,3},{2,0},{3,1},{4,6},{5,7},{6,4},{7,5},{8,10},{9,11},{10,... | collective-permute-start | bytes 3145736 | tf_op jit(solution)/shard_map/ppermute | solution.py:602
  33.2 38.2 %collective-permute-start.6 = (bf16[26,128,128]{2,1,0:T(8,128)(2,1)}, bf16[26,128,128]{2,1,0:T(8,128)(2,1)}, u32[]{:S(2)}, u32[]{:S(2)}) collective-permute-start(bf16[26,128,128]{2,1,0:T(8,128)(2,1)} %picked_square.3), channel_id=1, source_target_pairs={{0,16},{8,24},{16,0},{24,8},{1,17},{9,25},{17,1},{25,9},{2,18},{10... | collective-permute-start | bytes 2555912 | tf_op jit(solution)/shard_map/ppermute | solution.py:602
  38.8 33.6 %copy-start.1 = (s32[16]{0:T(128)S(1)}, s32[16]{0:T(128)}, u32[]{:S(2)}) copy-start(s32[16]{0:T(128)} %owner_ref.8) | copy-start | bytes 196
  72.1 28.7 %copy-start.5 = (bf16[4,2,4,128,128]{4,3,2,1,0:T(8,128)(2,1)}, bf16[4,2,4,128,128]{4,3,2,1,0:T(8,128)(2,1)S(1)}, u32[]{:S(2)}) copy-start(bf16[4,2,4,128,128]{4,3,2,1,0:T(8,128)(2,1)S(1)} %collective-permute-done.4.refs_4_) | copy-start | bytes 3145732
  72.1 7.7 %copy-start.6 = (bf16[4,2,4,128,128]{4,3,2,1,0:T(8,128)(2,1)}, bf16[4,2,4,128,128]{4,3,2,1,0:T(8,128)(2,1)S(1)}, u32[]{:S(2)}) copy-start(bf16[4,2,4,128,128]{4,3,2,1,0:T(8,128)(2,1)S(1)} %collective-permute-done.3.refs_2_) | copy-start | bytes 3145732
  72.1 26.8 %collective-permute-start.8 = (bf16[4,2,4,128,128]{4,3,2,1,0:T(8,128)(2,1)S(1)}, bf16[4,2,4,128,128]{4,3,2,1,0:T(8,128)(2,1)}, u32[]{:S(2)}, u32[]{:S(2)}) collective-permute-start(bf16[4,2,4,128,128]{4,3,2,1,0:T(8,128)(2,1)S(1)} %collective-permute-done.3.refs_2_), channel_id=1, source_target_pairs={{0,1},{1,0},{2,3},{3,2},{4,5},{5,4},{6,7},{7,6},{8,9},{9,8},{10,11... | collective-permute-start | bytes 3145736 | tf_op jit(solution)/shard_map/ppermute | solution.py:602
  75.0 23.9 %collective-permute-start.9 = (bf16[2,2,4,128,128]{4,3,2,1,0:T(8,128)(2,1)}, bf16[2,2,4,128,128]{4,3,2,1,0:T(8,128)(2,1)}, u32[]{:S(2)}, u32[]{:S(2)}) collective-permute-start(bf16[2,2,4,128,128]{4,3,2,1,0:T(8,128)(2,1)} %slice.33), channel_id=1, source_target_pairs={{0,4},{1,5},{2,6},{3,7},{4,0},{5,1},{6,2},{7,3},{8,12},{9,13},{10,... | collective-permute-start | bytes 1572872 | tf_op jit(solution)/shard_map/ppermute | solution.py:602
  76.5 22.4 %collective-permute-start.10 = (bf16[2,2,4,128,128]{4,3,2,1,0:T(8,128)(2,1)}, bf16[2,2,4,128,128]{4,3,2,1,0:T(8,128)(2,1)}, u32[]{:S(2)}, u32[]{:S(2)}) collective-permute-start(bf16[2,2,4,128,128]{4,3,2,1,0:T(8,128)(2,1)} %slice.34), channel_id=1, source_target_pairs={{0,2},{1,3},{2,0},{3,1},{4,6},{5,7},{6,4},{7,5},{8,10},{9,11},{10,... | collective-permute-start | bytes 1572872 | tf_op jit(solution)/shard_map/ppermute | solution.py:602
  78.0 5.6 %copy-start.12 = (bf16[10,128,128]{2,1,0:T(8,128)(2,1)S(1)}, bf16[10,128,128]{2,1,0:T(8,128)(2,1)}, u32[]{:S(2)}) copy-start(bf16[10,128,128]{2,1,0:T(8,128)(2,1)} %picked_square.5) | copy-start | bytes 983044
  79.8 12.9 %collective-permute-start.11 = (bf16[10,128,128]{2,1,0:T(8,128)(2,1)}, bf16[10,128,128]{2,1,0:T(8,128)(2,1)}, u32[]{:S(2)}, u32[]{:S(2)}) collective-permute-start(bf16[10,128,128]{2,1,0:T(8,128)(2,1)} %picked_square.4), channel_id=1, source_target_pairs={{0,8},{8,0},{16,24},{24,16},{1,9},{9,1},{17,25},{25,17},{2,10},{10... | collective-permute-start | bytes 983048 | tf_op jit(solution)/shard_map/ppermute | solution.py:602
  83.6 15.3 %collective-permute-start.12 = (bf16[10,128,128]{2,1,0:T(8,128)(2,1)S(1)}, bf16[10,128,128]{2,1,0:T(8,128)(2,1)}, u32[]{:S(2)}, u32[]{:S(2)}) collective-permute-start(bf16[10,128,128]{2,1,0:T(8,128)(2,1)S(1)} %copy-done.12), channel_id=1, source_target_pairs={{0,24},{8,16},{16,8},{24,0},{1,25},{9,17},{17,9},{25,1},{2,26},{10... | collective-permute-start | bytes 983048 | tf_op jit(solution)/shard_map/ppermute | solution.py:602
  98.9 36.4 %collective-permute-start.17 = (bf16[4,2,49,16,128]{4,3,2,1,0:T(8,128)(2,1)}, bf16[4,2,49,16,128]{4,3,2,1,0:T(8,128)(2,1)}, u32[]{:S(2)}, u32[]{:S(2)}) collective-permute-start(bf16[4,2,49,16,128]{4,3,2,1,0:T(8,128)(2,1)} %get-tuple-element.111), channel_id=1, source_target_pairs={{0,2},{1,3},{2,0},{3,1},{4,6},{5,7},{6,4},{7,5},{8,10},{9,11},{10,... | collective-permute-start | bytes 4816904 | tf_op jit(solution)/shard_map/ppermute | solution.py:602
  99.5 36.0 %collective-permute-start.18 = (bf16[4,2,49,16,128]{4,3,2,1,0:T(8,128)(2,1)}, bf16[4,2,49,16,128]{4,3,2,1,0:T(8,128)(2,1)}, u32[]{:S(2)}, u32[]{:S(2)}) collective-permute-start(bf16[4,2,49,16,128]{4,3,2,1,0:T(8,128)(2,1)} %get-tuple-element.112), channel_id=1, source_target_pairs={{0,4},{1,5},{2,6},{3,7},{4,0},{5,1},{6,2},{7,3},{8,12},{9,13},{10,... | collective-permute-start | bytes 4816904 | tf_op jit(solution)/shard_map/ppermute | solution.py:602
  100.3 2.8 %collective-permute-start.15 = (bf16[2,2,4,128,128]{4,3,2,1,0:T(8,128)(2,1)}, bf16[2,2,4,128,128]{4,3,2,1,0:T(8,128)(2,1)S(1)}, u32[]{:S(2)}, u32[]{:S(2)}) collective-permute-start(bf16[2,2,4,128,128]{4,3,2,1,0:T(8,128)(2,1)} %collective-permute-done.9.refs_6_), channel_id=1, source_target_pairs={{0,1},{1,0},{2,3},{3,2},{4,5},{5,4},{6,7},{7,6},{8,9},{9,8},{10,11... | collective-permute-start | bytes 1572872 | tf_op jit(solution)/shard_map/ppermute | solution.py:602
  100.3 5.9 %collective-permute-start.13 = (bf16[4,2,4,128,128]{4,3,2,1,0:T(8,128)(2,1)S(1)}, bf16[4,2,4,128,128]{4,3,2,1,0:T(8,128)(2,1)S(1)}, u32[]{:S(2)}, u32[]{:S(2)}) collective-permute-start(bf16[4,2,4,128,128]{4,3,2,1,0:T(8,128)(2,1)S(1)} %pad_maximum_fusion.refs_0_), channel_id=1, source_target_pairs={{0,1},{1,0},{2,3},{3,2},{4,5},{5,4},{6,7},{7,6},{8,9},{9,8},{10,11... | collective-permute-start | bytes 3145736 | tf_op jit(solution)/shard_map/ppermute | solution.py:602
  100.8 6.2 %collective-permute-start.14 = (bf16[4,2,4,128,128]{4,3,2,1,0:T(8,128)(2,1)S(1)}, bf16[4,2,4,128,128]{4,3,2,1,0:T(8,128)(2,1)}, u32[]{:S(2)}, u32[]{:S(2)}) collective-permute-start(bf16[4,2,4,128,128]{4,3,2,1,0:T(8,128)(2,1)S(1)} %collective-permute-done.4.refs_4_), channel_id=1, source_target_pairs={{0,1},{1,0},{2,3},{3,2},{4,5},{5,4},{6,7},{7,6},{8,9},{9,8},{10,11... | collective-permute-start | bytes 3145736 | tf_op jit(solution)/shard_map/ppermute | solution.py:602
  103.1 3.9 %copy-start.10 = (bf16[2,2,4,128,128]{4,3,2,1,0:T(8,128)(2,1)}, bf16[2,2,4,128,128]{4,3,2,1,0:T(8,128)(2,1)S(1)}, u32[]{:S(2)}) copy-start(bf16[2,2,4,128,128]{4,3,2,1,0:T(8,128)(2,1)S(1)} %collective-permute-done.15.refs_8_) | copy-start | bytes 1572868
  103.1 3.1 %collective-permute-start.16 = (bf16[2,2,4,128,128]{4,3,2,1,0:T(8,128)(2,1)}, bf16[2,2,4,128,128]{4,3,2,1,0:T(8,128)(2,1)S(1)}, u32[]{:S(2)}, u32[]{:S(2)}) collective-permute-start(bf16[2,2,4,128,128]{4,3,2,1,0:T(8,128)(2,1)} %collective-permute-done.10.refs_7_), channel_id=1, source_target_pairs={{0,1},{1,0},{2,3},{3,2},{4,5},{5,4},{6,7},{7,6},{8,9},{9,8},{10,11... | collective-permute-start | bytes 1572872 | tf_op jit(solution)/shard_map/ppermute | solution.py:602
  106.2 0.8 copy-start.11
  107.0 1.0 copy-start.9
  135.5 57.0 %all-to-all-start = ((bf16[32,17,16,128]{3,2,1,0:T(8,128)(2,1)}), bf16[32,17,16,128]{3,2,1,0:T(8,128)(2,1)S(1)}, u32[]{:S(2)}, u32[]{:S(2)}) async-start(bf16[32,17,16,128]{3,2,1,0:T(8,128)(2,1)} %get-tuple-element.115), calls=%async_computation | async-start | bytes 4456448 | tf_op jit(solution)/shard_map/all_to_all | solution.py:738
  140.5 4.8 %copy-start.7 = (bf16[4,2,49,16,128]{4,3,2,1,0:T(8,128)(2,1)S(1)}, bf16[4,2,49,16,128]{4,3,2,1,0:T(8,128)(2,1)}, u32[]{:S(2)}) copy-start(bf16[4,2,49,16,128]{4,3,2,1,0:T(8,128)(2,1)} %get-tuple-element.117) | copy-start | bytes 4816900
  142.8 32.2 %collective-permute-start.22 = (bf16[1,2,49,16,128]{4,3,2,1,0:T(8,128)(2,1)}, bf16[1,2,49,16,128]{4,3,2,1,0:T(8,128)(2,1)S(1)}, u32[]{:S(2)}, u32[]{:S(2)}) collective-permute-start(bf16[1,2,49,16,128]{4,3,2,1,0:T(8,128)(2,1)} %get-tuple-element.121), channel_id=1, source_target_pairs={{0,6},{1,7},{2,4},{3,5},{4,2},{5,3},{6,0},{7,1},{8,14},{9,15},{10,... | collective-permute-start | bytes 1204232 | tf_op jit(solution)/shard_map/ppermute | solution.py:602
  145.3 29.7 %collective-permute-start.23 = (bf16[2,2,49,16,128]{4,3,2,1,0:T(8,128)(2,1)}, bf16[2,2,49,16,128]{4,3,2,1,0:T(8,128)(2,1)S(1)}, u32[]{:S(2)}, u32[]{:S(2)}) collective-permute-start(bf16[2,2,49,16,128]{4,3,2,1,0:T(8,128)(2,1)} %slice.42), channel_id=1, source_target_pairs={{0,1},{1,0},{2,3},{3,2},{4,5},{5,4},{6,7},{7,6},{8,9},{9,8},{10,11... | collective-permute-start | bytes 2408456 | tf_op jit(solution)/shard_map/ppermute | solution.py:602
  146.7 28.3 %collective-permute-start.19 = (bf16[2,2,49,16,128]{4,3,2,1,0:T(8,128)(2,1)}, bf16[2,2,49,16,128]{4,3,2,1,0:T(8,128)(2,1)}, u32[]{:S(2)}, u32[]{:S(2)}) collective-permute-start(bf16[2,2,49,16,128]{4,3,2,1,0:T(8,128)(2,1)} %get-tuple-element.137), channel_id=1, source_target_pairs={{0,1},{1,0},{2,3},{3,2},{4,5},{5,4},{6,7},{7,6},{8,9},{9,8},{10,11... | collective-permute-start | bytes 2408456 | tf_op jit(solution)/shard_map/ppermute | solution.py:602
  150.0 25.0 %collective-permute-start.20 = (bf16[2,2,49,16,128]{4,3,2,1,0:T(8,128)(2,1)}, bf16[2,2,49,16,128]{4,3,2,1,0:T(8,128)(2,1)}, u32[]{:S(2)}, u32[]{:S(2)}) collective-permute-start(bf16[2,2,49,16,128]{4,3,2,1,0:T(8,128)(2,1)} %get-tuple-element.135), channel_id=1, source_target_pairs={{0,1},{1,0},{2,3},{3,2},{4,5},{5,4},{6,7},{7,6},{8,9},{9,8},{10,11... | collective-permute-start | bytes 2408456 | tf_op jit(solution)/shard_map/ppermute | solution.py:602
  152.9 22.2 %collective-permute-start.21 = (bf16[2,2,49,16,128]{4,3,2,1,0:T(8,128)(2,1)}, bf16[2,2,49,16,128]{4,3,2,1,0:T(8,128)(2,1)}, u32[]{:S(2)}, u32[]{:S(2)}) collective-permute-start(bf16[2,2,49,16,128]{4,3,2,1,0:T(8,128)(2,1)} %get-tuple-element.133), channel_id=1, source_target_pairs={{0,1},{1,0},{2,3},{3,2},{4,5},{5,4},{6,7},{7,6},{8,9},{9,8},{10,11... | collective-permute-start | bytes 2408456 | tf_op jit(solution)/shard_map/ppermute | solution.py:602
  175.0 17.6 %copy-start.8 = (bf16[1,2,49,16,128]{4,3,2,1,0:T(8,128)(2,1)}, bf16[1,2,49,16,128]{4,3,2,1,0:T(8,128)(2,1)S(1)}, u32[]{:S(2)}) copy-start(bf16[1,2,49,16,128]{4,3,2,1,0:T(8,128)(2,1)S(1)} %collective-permute-done.22) | copy-start | bytes 1204228
  175.0 17.6 %copy-start.4 = (bf16[2,2,49,16,128]{4,3,2,1,0:T(8,128)(2,1)}, bf16[2,2,49,16,128]{4,3,2,1,0:T(8,128)(2,1)S(1)}, u32[]{:S(2)}) copy-start(bf16[2,2,49,16,128]{4,3,2,1,0:T(8,128)(2,1)S(1)} %collective-permute-done.23) | copy-start | bytes 2408452
  192.6 1.4 copy-start.2
  193.9 33.7 %all-to-all-start.1 = ((bf16[16,32,16,128]{3,2,1,0:T(8,128)(2,1)}), bf16[16,32,16,128]{3,2,1,0:T(8,128)(2,1)}, u32[]{:S(2)}, u32[]{:S(2)}) async-start(bf16[16,32,16,128]{3,2,1,0:T(8,128)(2,1)} %other_pairs.1), calls=%async_computation.1 | async-start | bytes 4194304 | tf_op jit(solution)/shard_map/all_to_all | solution.py:738

commit v7 on v6

--- a/solution.py
+++ b/solution.py
@@ -9,7 +9,7 @@
 
 NT = 16
 UNROLL = 4
-STEPS = 2
+PAIRED_BYTES = 24 * 1024 * 1024
 VMEM_BYTES = 60 * 1024 * 1024
 PARTS = (
     ((0, 0), (0, 1), (1, 0), (1, 1)),
@@ -491,44 +491,56 @@
     )(*tables, *anywhere, *blocks)
 
 
-def paired_kernel(first, steps, parts, columns, where_ref, left_ref, *refs):
-    right_refs, refs = refs[:parts], refs[parts:]
-    base_refs, (out_ref, left, right, total, sums, sems) = refs[:-6], refs[-6:]
+def arranged_kernel(first, parts, where_ref, *refs):
+    right_refs, (out_ref, right, sems) = refs[:parts], refs[parts:]
+    others, count, rows, tile = right.shape
+    copies = []
+    at = 0
+    for i, ref in enumerate(right_refs):
+        place_at = (at // 4 ^ where_ref[1]) * 4 + at % 4
+        copies.append(
+            pltpu.make_async_copy(
+                ref.at[:, pl.ds(first, count)],
+                right.at[pl.ds(place_at, ref.shape[0])],
+                sems.at[i],
+            )
+        )
+        at += ref.shape[0]
+    start_all(copies)
+    wait_all(copies)
+    for i in range(count):
+        out_ref[:, i * tile : (i + 1) * tile] = right[:, i].reshape(others * rows, tile)
+
+
+def arranged(where, rights, first, count):
+    parts = len(rights)
+    rows, tile = rights[0].shape[2:]
+    others = sum(each.shape[0] for each in rights)
+    return pl.pallas_call(
+        functools.partial(arranged_kernel, first, parts),
+        in_specs=[pl.BlockSpec(memory_space=pltpu.SMEM)]
+        + [pl.BlockSpec(memory_space=pl.ANY)] * parts,
+        out_specs=pl.BlockSpec(memory_space=pltpu.VMEM),
+        out_shape=jax.ShapeDtypeStruct((others * rows, count * tile), jnp.bfloat16),
+        scratch_shapes=[
+            pltpu.VMEM((others, count, rows, tile), jnp.bfloat16),
+            pltpu.SemaphoreType.DMA((parts,)),
+        ],
+        compiler_params=pltpu.CompilerParams(vmem_limit_bytes=PAIRED_BYTES),
+        name="arranged",
+    )(where, *rights)
+
+
+def paired_kernel(columns, where_ref, left_ref, right_ref, *refs):
+    base_refs, (out_ref, sums) = refs[:-2], refs[-2:]
     sources, count, rows, tile = left_ref.shape
-    others = right.shape[0]
-    some = count // steps
-    copies = []
-    for step in range(steps):
-        here = pl.ds(step * some, some)
-        there = pl.ds(first + step * some, some)
-        pairs = [(left_ref.at[:, here], left.at[:, here])]
-        at = 0
-        for ref in right_refs:
-            place_at = (at // 4 ^ where_ref[1]) * 4 + at % 4
-            pairs.append((ref.at[:, there], right.at[pl.ds(place_at, ref.shape[0]), here]))
-            at += ref.shape[0]
-        copies.append(
-            [
-                pltpu.make_async_copy(source, target, sems.at[step * (parts + 1) + i])
-                for i, (source, target) in enumerate(pairs)
-            ]
-        )
-    for each in copies:
-        start_all(each)
-    for step, each in enumerate(copies):
-        wait_all(each)
-        strips = range(step * some, (step + 1) * some)
-        values = lax.dot_general(
-            jnp.concatenate([left[:, i].reshape(sources * rows, tile) for i in strips], axis=1),
-            jnp.concatenate([right[:, i].reshape(others * rows, tile) for i in strips], axis=1),
-            (((1,), (1,)), ((), ())),
-            preferred_element_type=jnp.float32,
-        )
-        if step:
-            total[...] += values
-        else:
-            total[...] = values
-    values = total[...]
+    others = sums.shape[0]
+    values = lax.dot_general(
+        jnp.concatenate([left_ref[:, i].reshape(sources * rows, tile) for i in range(count)], axis=1),
+        right_ref[...],
+        (((1,), (1,)), ((), ())),
+        preferred_element_type=jnp.float32,
+    )
     down = lax.broadcasted_iota(jnp.int32, values.shape, 0)
     along = lax.broadcasted_iota(jnp.int32, values.shape, 1)
     values = jnp.where((down ^ along) % rows == 0, values, 0.0)
@@ -549,30 +561,28 @@
             out_ref[plane * each + blk, :columns, :others] = values
 
 
-def paired(where, left, rights, first, steps, base=None):
-    parts = len(rights)
+def paired(where, left, rights, first, base=None):
     sources, count, rows, tile = left.shape
     others = sum(each.shape[0] for each in rights)
     vmem = pl.BlockSpec(memory_space=pltpu.VMEM)
     base = () if base is None else (base,)
     shape = (base[0].shape[0], 8, 128) if base else (sources, others)
     return pl.pallas_call(
-        functools.partial(paired_kernel, first, steps, parts, 4),
-        in_specs=[pl.BlockSpec(memory_space=pltpu.SMEM)]
-        + [pl.BlockSpec(memory_space=pl.ANY)] * (parts + 1)
+        functools.partial(paired_kernel, 4),
+        in_specs=[
+            pl.BlockSpec(memory_space=pltpu.SMEM),
+            vmem,
+            vmem,
+        ]
         + [vmem] * len(base),
         out_specs=vmem,
         out_shape=jax.ShapeDtypeStruct(shape, jnp.float32),
         scratch_shapes=[
-            pltpu.VMEM(left.shape, jnp.bfloat16),
-            pltpu.VMEM((others,) + left.shape[1:], jnp.bfloat16),
-            pltpu.VMEM((sources * rows, others * rows), jnp.float32),
             pltpu.VMEM((others, others), jnp.float32),
-            pltpu.SemaphoreType.DMA((steps * (parts + 1),)),
         ],
-        compiler_params=pltpu.CompilerParams(vmem_limit_bytes=VMEM_BYTES),
+        compiler_params=pltpu.CompilerParams(vmem_limit_bytes=PAIRED_BYTES),
         name="paired",
-    )(where, left, *rights, *base)
+    )(where, left, arranged(where, rights, first, count), *base)
 
 
 def folded_body(
@@ -745,8 +755,8 @@
     rest = everyone(rest, [list(range(2 * parts)), list(range(2 * parts, devices))])
     pairs = [each.reshape((-1,) + each.shape[2:]) for each in pairs]
 
-    total = paired(where, sent, pairs, cross, 1)
-    total = jnp.sum(everyone(paired(where, rest, pairs, 0, STEPS, total)), axis=0)
+    total = paired(where, sent, pairs, cross)
+    total = jnp.sum(everyone(paired(where, rest, pairs, 0, total)), axis=0)
     return total[:aux_local, : parts * aux_local]
 
 

time: 247 us -> 245 us (level)
  waiting for transfers between devices: 87.8 us -> 80.1 us
  local copies, waits for them, and re-layouts: 24.4 us -> 30.2 us
    all_to_all x2, waiting for transfers between devices: 41.5 us -> 32.8 us  [everyone(): lax.all_to_all(values, ('grp', 'blk'), split_axis=0, concat_axis=0, tiled...]
    unnamed x30 -> x38, local copies, waits for them, and re-layouts: 3.18 us -> 9.97 us
    pallas_call x2 -> x4, Pallas kernels: 10.6 us -> 11.1 us  [the longest x2 5.71 us: arranged(): pl.pallas_call(functools.partial(arranged_kernel, first, parts), in_specs...]
  transfers between devices with their start and end apart: 26 -> 26, of which waited for: 11 -> 11; matrix products, arithmetic and copies ran while one was open for 9% -> 8% of each run, Pallas kernels for 30% -> 32%
where the time goes in v7:
time: 245 us; the launch traced here: 244 us
  Pallas kernels  80.4 us (33%)
  waiting for transfers between devices  80.1 us (33%)
  starting transfers between devices  38.7 us (16%)
  local copies, waits for them, and re-layouts  30.2 us (12%)
  blocking collectives  12 us (5%)
  other arithmetic  2.57 us (1%)
    ppermute x24, waiting for transfers between devices, swap(): lax.ppermute(values, axis, [(at, at ^ distance) for at in range(size)])  47.4 us
    pallas_call x2, Pallas kernels, kernel_call(): pl.pallas_call(kernel, in_specs=[pl.BlockSpec(memory_space=pltpu.SMEM)] *...  44.6 us
    all_to_all x2, waiting for transfers between devices, everyone(): lax.all_to_all(values, ('grp', 'blk'), split_axis=0, concat_axis=0, tiled...  32.8 us
    ppermute x24, starting transfers between devices, swap(): lax.ppermute(values, axis, [(at, at ^ distance) for at in range(size)])  29.2 us
    all_to_all x1, blocking collectives, everyone(): lax.all_to_all(values, ('grp', 'blk'), split_axis=0, concat_axis=0, tiled...  12 us
    unnamed x38, local copies, waits for them, and re-layouts  9.97 us
    all_to_all x2, starting transfers between devices, everyone(): lax.all_to_all(values, ('grp', 'blk'), split_axis=0, concat_axis=0, tiled...  9.52 us
    pallas_call x1, Pallas kernels, pair_tiles(): pl.pallas_call(functools.partial(pair_kernel, columns), grid_spec=pltpu.P...  8.63 us
  transfers between devices with their start and end apart: 26, of which 11 were waited for; matrix products, arithmetic and copies ran while one was open for 8% of the time, Pallas kernels for 32%

profile of v7, /device:TPU:0, one launch (start us, length us, event | category | flops | bytes accessed | tf_op | source)
XLA Modules:
  0.0 244.4 jit_solution(18072972829934110079)
XLA Ops:
  0.0 1.0 copy.8
  2.0 4.1 %collective-permute-start.1 = (bf16[2,4,128,128]{3,2,1,0:T(8,128)(2,1)S(1)}, bf16[2,4,128,128]{3,2,1,0:T(8,128)(2,1)S(1)}, u32[]{:S(2)}, u32[]{:S(2)}) collective-permute-start(bf16[2,4,128,128]{3,2,1,0:T(8,128)(2,1)S(1)} %get-tuple-element.140), channel_id=1, source_target_pairs={{0,16},{8,24},{16,0},{24,8},{1,17},{9,25},{17,1},{25,9},{2,18},{10... | collective-permute-start | bytes 786440 | tf_op jit(solution)/shard_map/ppermute | solution.py:612
  6.1 1.6 collective-permute-start
  7.7 1.3 reshape.293.mask_ref
  9.7 8.6 %pair_tiles.1 = (bf16[4,2,49,16,128]{4,3,2,1,0:T(8,128)(2,1)}, bf16[4,2,49,16,128]{4,3,2,1,0:T(8,128)(2,1)}, bf16[4,2,49,16,128]{4,3,2,1,0:T(8,128)(2,1)}, bf16[...) custom-call(s32[2]{0:T(128)} %pad_add_fusion.where_ref.group_ref, s32[16]{0:T(128)} %owner_ref.8, ...), custom_call_target="tpu_custom_call" | custom-call | tf_op jit(solution)/shard_map/pair_tiles/pallas_call | solution.py:278
  18.3 2.7 %collective-permute-start.7 = (bf16[3,2,49,16,128]{4,3,2,1,0:T(8,128)(2,1)}, bf16[3,2,49,16,128]{4,3,2,1,0:T(8,128)(2,1)}, u32[]{:S(2)}, u32[]{:S(2)}) collective-permute-start(bf16[3,2,49,16,128]{4,3,2,1,0:T(8,128)(2,1)} %get-tuple-element.78), channel_id=1, source_target_pairs={{0,6},{1,7},{2,4},{3,5},{4,2},{5,3},{6,0},{7,1},{8,14},{9,15},{10,... | collective-permute-start | bytes 3612680 | tf_op jit(solution)/shard_map/ppermute | solution.py:612
  21.0 3.0 %picked_square.3 = bf16[26,128,128]{2,1,0:T(8,128)(2,1)} custom-call(s32[2]{0:T(128)} %pad_add_fusion.where_ref.group_ref, s32[16]{0:T(128)} %owner_ref.8, s32[256]{0:T(256)} %reshape.293.mask_ref, bf16[4,16,128,512]{3,2,1,0:T(8,128)(2,1)} %bitcast.43, bf16[4,16,128,512]{3,2,1,0:T(8,128)(2,1)} %bitcast.44, bf16[4,16,128,512]{3,2,1,0:T(8,128)(2,1)} %bitcast.45, ...), custom_call_target="tpu_custom_call" | custom-call | tf_op jit(solution)/shard_map/picked_square/pallas_call | solution.py:137
  24.0 3.0 %picked_rows.2 = bf16[8,128,512]{2,1,0:T(8,128)(2,1)} custom-call(s32[2]{0:T(128)} %pad_add_fusion.where_ref.group_ref, s32[16]{0:T(128)} %owner_ref.8, s32[256]{0:T(256)} %reshape.293.mask_ref, bf16[4,16,128,512]{3,2,1,0:T(8,128)(2,1)} %bitcast.52, bf16[4,16,128,512]{3,2,1,0:T(8,128)(2,1)} %bitcast.51, bf16[4,16,128,512]{3,2,1,0:T(8,128)(2,1)} %bitcast.53, ...), custom_call_target="tpu_custom_call" | custom-call | tf_op jit(solution)/shard_map/picked_rows/pallas_call | solution.py:171
  27.1 3.0 %collective-permute-start.5 = (bf16[8,128,512]{2,1,0:T(8,128)(2,1)}, bf16[8,128,512]{2,1,0:T(8,128)(2,1)}, u32[]{:S(2)}, u32[]{:S(2)}) collective-permute-start(bf16[8,128,512]{2,1,0:T(8,128)(2,1)} %picked_rows.2), channel_id=1, source_target_pairs={{0,8},{8,0},{16,24},{24,16},{1,9},{9,1},{17,25},{25,17},{2,10},{10... | collective-permute-start | bytes 3145736 | tf_op jit(solution)/shard_map/ppermute | solution.py:612
  30.2 1.5 collective-permute-start.4
  31.7 1.5 collective-permute-start.3
  33.2 2.0 collective-permute-start.6
  36.2 2.6 %picked_square.5 = bf16[10,128,128]{2,1,0:T(8,128)(2,1)} custom-call(s32[2]{0:T(128)} %pad_add_fusion.where_ref.group_ref, s32[16]{0:T(128)} %owner_ref.8, s32[256]{0:T(256)} %reshape.293.mask_ref, bf16[4,16,128,512]{3,2,1,0:T(8,128)(2,1)} %bitcast.55, bf16[4,16,128,512]{3,2,1,0:T(8,128)(2,1)} %bitcast.56, bf16[4,16,128,512]{3,2,1,0:T(8,128)(2,1)} %bitcast.57, ...), custom_call_target="tpu_custom_call" | custom-call | tf_op jit(solution)/shard_map/picked_square/pallas_call | solution.py:137
  38.8 2.7 %picked_square.4 = bf16[10,128,128]{2,1,0:T(8,128)(2,1)} custom-call(s32[2]{0:T(128)} %pad_add_fusion.where_ref.group_ref, s32[16]{0:T(128)} %owner_ref.8, s32[256]{0:T(256)} %reshape.293.mask_ref, bf16[4,16,128,512]{3,2,1,0:T(8,128)(2,1)} %bitcast.59, bf16[4,16,128,512]{3,2,1,0:T(8,128)(2,1)} %bitcast.60, bf16[4,16,128,512]{3,2,1,0:T(8,128)(2,1)} %bitcast.61, ...), custom_call_target="tpu_custom_call" | custom-call | tf_op jit(solution)/shard_map/picked_square/pallas_call | solution.py:137
  41.5 29.8 %collective-permute-done.6.refs_13_ = bf16[26,128,128]{2,1,0:T(8,128)(2,1)} collective-permute-done((bf16[26,128,128]{2,1,0:T(8,128)(2,1)}, bf16[26,128,128]{2,1,0:T(8,128)(2,1)}, u32[]{:S(2)}, u32[]{:S(2)}) %collective-permute-start.6) | collective-permute-done | bytes 852000 | tf_op jit(solution)/shard_map/ppermute | solution.py:612
  75.0 1.5 collective-permute-start.9
  76.5 1.5 collective-permute-start.10
  78.0 1.7 gather_fusion.1
  79.7 3.8 %collective-permute-start.11 = (bf16[10,128,128]{2,1,0:T(8,128)(2,1)}, bf16[10,128,128]{2,1,0:T(8,128)(2,1)}, u32[]{:S(2)}, u32[]{:S(2)}) collective-permute-start(bf16[10,128,128]{2,1,0:T(8,128)(2,1)} %picked_square.4), channel_id=1, source_target_pairs={{0,8},{8,0},{16,24},{24,16},{1,9},{9,1},{17,25},{25,17},{2,10},{10... | collective-permute-start | bytes 983048 | tf_op jit(solution)/shard_map/ppermute | solution.py:612
  83.9 1.8 gather_fusion.2
  86.3 4.7 %picked_rows.3.refs_10_ = bf16[16,128,512]{2,1,0:T(8,128)(2,1)} custom-call(s32[2]{0:T(128)} %pad_add_fusion.where_ref.group_ref, s32[16]{0:T(128)} %owner_ref.8, s32[256]{0:T(256)} %reshape.293.mask_ref, bf16[4,16,128,512]{3,2,1,0:T(8,128)(2,1)} %bitcast.63, bf16[4,16,128,512]{3,2,1,0:T(8,128)(2,1)} %bitcast.64, bf16[4,16,128,512]{3,2,1,0:T(8,128)(2,1)} %bitcast.65, ...), custom_call_target="tpu_custom_call" | custom-call | tf_op jit(solution)/shard_map/picked_rows/pallas_call | solution.py:171
  91.0 1.6 collective-permute-done.11.refs_11_
  92.6 6.2 %collective-permute-done.12.refs_14_ = bf16[10,128,128]{2,1,0:T(8,128)(2,1)} collective-permute-done((bf16[10,128,128]{2,1,0:T(8,128)(2,1)S(1)}, bf16[10,128,128]{2,1,0:T(8,128)(2,1)}, u32[]{:S(2)}, u32[]{:S(2)}) %collective-permute-start.12) | collective-permute-done | bytes 327712 | tf_op jit(solution)/shard_map/ppermute | solution.py:612
  100.9 2.2 collective-permute-done.15.refs_8_
  103.2 2.9 %collective-permute-done.16.refs_9_ = bf16[2,2,4,128,128]{4,3,2,1,0:T(8,128)(2,1)S(1)} collective-permute-done((bf16[2,2,4,128,128]{4,3,2,1,0:T(8,128)(2,1)}, bf16[2,2,4,128,128]{4,3,2,1,0:T(8,128)(2,1)S(1)}, u32[]{:S(2)}, u32[]{:S(2)}) %collective-permute-start.16) | collective-permute-done | bytes 524320 | tf_op jit(solution)/shard_map/ppermute | solution.py:612
  107.9 26.8 %half_and_pairs.1 = (bf16[32,17,16,128]{3,2,1,0:T(8,128)(2,1)}, bf16[16,2048,128]{2,1,0:T(8,128)(2,1)}) custom-call(s32[2]{0:T(128)} %pad_add_fusion.where_ref.group_ref, s32[128]{0:T(128)} %gather_fusion.1, s32[128]{0:T(128)} %get-tuple-element.94.tile_ref, s32[128]{0:T(128)} %gather_fusion.2, s32[128]{0:T(128)} %get-tuple-element.96.virtual_tile_ref, ...), custom_call_target="tpu_custom_call" | custom-call | tf_op jit(solution)/shard_map/half_and_pairs/pallas_call | solution.py:480
  135.5 5.0 %all-to-all-start = ((bf16[32,17,16,128]{3,2,1,0:T(8,128)(2,1)}), bf16[32,17,16,128]{3,2,1,0:T(8,128)(2,1)S(1)}, u32[]{:S(2)}, u32[]{:S(2)}) async-start(bf16[32,17,16,128]{3,2,1,0:T(8,128)(2,1)} %get-tuple-element.115), calls=%async_computation | async-start | bytes 4456448 | tf_op jit(solution)/shard_map/all_to_all | solution.py:748
  140.5 2.3 slice.42
  142.8 2.5 %collective-permute-start.22 = (bf16[1,2,49,16,128]{4,3,2,1,0:T(8,128)(2,1)}, bf16[1,2,49,16,128]{4,3,2,1,0:T(8,128)(2,1)S(1)}, u32[]{:S(2)}, u32[]{:S(2)}) collective-permute-start(bf16[1,2,49,16,128]{4,3,2,1,0:T(8,128)(2,1)} %get-tuple-element.121), channel_id=1, source_target_pairs={{0,6},{1,7},{2,4},{3,5},{4,2},{5,3},{6,0},{7,1},{8,14},{9,15},{10,... | collective-permute-start | bytes 1204232 | tf_op jit(solution)/shard_map/ppermute | solution.py:612
  145.2 1.2 fusion.26
  146.9 2.8 %fusion.25 = (bf16[2,2,49,16,128]{4,3,2,1,0:T(8,128)(2,1)}, bf16[2,2,49,16,128]{4,3,2,1,0:T(8,128)(2,1)}) fusion(bf16[4,2,49,16,128]{4,3,2,1,0:T(8,128)(2,1)} %collective-permute-done.17), kind=kLoop, calls=%fused_computation.87 | loop fusion | bytes 3211264 | tf_op jit(solution)/shard_map/slice | solution.py:728
  149.8 2.8 %fusion.24 = (bf16[2,2,49,16,128]{4,3,2,1,0:T(8,128)(2,1)}, bf16[2,2,49,16,128]{4,3,2,1,0:T(8,128)(2,1)}) fusion(bf16[4,2,49,16,128]{4,3,2,1,0:T(8,128)(2,1)} %collective-permute-done.18), kind=kLoop, calls=%fused_computation.86 | loop fusion | bytes 3211264 | tf_op jit(solution)/shard_map/slice | solution.py:728
  153.1 17.8 %other_pairs.1 = bf16[16,32,16,128]{3,2,1,0:T(8,128)(2,1)} custom-call(s32[2]{0:T(128)} %pad_add_fusion.where_ref.group_ref, s32[128]{0:T(128)} %gather_fusion.2, s32[128]{0:T(128)} %get-tuple-element.96.virtual_tile_ref, bf16[4,2,4,128,128]{4,3,2,1,0:T(8,128)(2,1)} %copy-done.9, bf16[4,2,4,128,128]{4,3,2,1,0:T(8,128)(2,1)} %copy-done.13, ...), custom_call_target="tpu_custom_call" | custom-call | flops 8589934592 | bytes 16777216 | tf_op jit(solution)/shard_map/other_pairs/pallas_call | solution.py:480
  170.9 1.0 slice.41
  172.0 3.0 %collective-permute-done.22 = bf16[1,2,49,16,128]{4,3,2,1,0:T(8,128)(2,1)S(1)} collective-permute-done((bf16[1,2,49,16,128]{4,3,2,1,0:T(8,128)(2,1)}, bf16[1,2,49,16,128]{4,3,2,1,0:T(8,128)(2,1)S(1)}, u32[]{:S(2)}, u32[]{:S(2)}) %collective-permute-start.22) | collective-permute-done | bytes 401440 | tf_op jit(solution)/shard_map/ppermute | solution.py:612
  175.7 16.8 %all-to-all-done.left_ref = bf16[32,17,16,128]{3,2,1,0:T(8,128)(2,1)S(1)} async-done(((bf16[32,17,16,128]{3,2,1,0:T(8,128)(2,1)}), bf16[32,17,16,128]{3,2,1,0:T(8,128)(2,1)S(1)}, u32[]{:S(2)}, u32[]{:S(2)}) %all-to-all-start) | async-done | bytes 2228256 | tf_op jit(solution)/shard_map/all_to_all | solution.py:748
  192.5 4.6 %all-to-all-start.1 = ((bf16[16,32,16,128]{3,2,1,0:T(8,128)(2,1)}), bf16[16,32,16,128]{3,2,1,0:T(8,128)(2,1)}, u32[]{:S(2)}, u32[]{:S(2)}) async-start(bf16[16,32,16,128]{3,2,1,0:T(8,128)(2,1)} %other_pairs.1), calls=%async_computation.1 | async-start | bytes 4194304 | tf_op jit(solution)/shard_map/all_to_all | solution.py:748
  197.1 1.1 copy-done.2
  198.2 1.1 copy-done.3
  199.4 1.0 copy-done.5
  200.4 2.3 arranged.3.right_ref
  202.7 3.4 %arranged.2.right_ref = bf16[512,4096]{1,0:T(8,128)(2,1)S(1)} custom-call(s32[2]{0:T(128)S(1)} %copy-done.6, bf16[4,49,16,128]{3,2,1,0:T(8,128)(2,1)S(1)} %bitcast.30, bf16[4,49,16,128]{3,2,1,0:T(8,128)(2,1)} %bitcast.13.refs_1_, bf16[4,49,16,128]{3,2,1,0:T(8,128)(2,1)S(1)} %bitcast.32, bf16[4,49,16,128]{3,2,1,0:T(8,128)(2,1)} %bitcast.15.refs_3_, ...), custom_call_target="tpu_custom_call" | custom-call | tf_op jit(solution)/shard_map/arranged/pallas_call | solution.py:519
  206.1 2.0 copy-done
  208.1 2.3 paired.2.refs_0_
  210.4 16.0 %all-to-all-done.1.left_ref = bf16[16,32,16,128]{3,2,1,0:T(8,128)(2,1)} async-done(((bf16[16,32,16,128]{3,2,1,0:T(8,128)(2,1)}), bf16[16,32,16,128]{3,2,1,0:T(8,128)(2,1)}, u32[]{:S(2)}, u32[]{:S(2)}) %all-to-all-start.1) | async-done | bytes 2097184 | tf_op jit(solution)/shard_map/all_to_all | solution.py:748
  226.4 2.2 copy-done.1
  228.6 3.2 %paired.3 = f32[32,8,128]{2,1,0:T(8,128)S(1)} custom-call(s32[2]{0:T(128)S(1)} %copy-done.6, bf16[16,32,16,128]{3,2,1,0:T(8,128)(2,1)} %all-to-all-done.1.left_ref, bf16[512,4096]{1,0:T(8,128)(2,1)S(1)} %copy-done.1, f32[32,32]{1,0:T(8,128)S(1)} %paired.2.refs_0_), custom_call_target="tpu_custom_call" | custom-call | tf_op jit(solution)/shard_map/paired/pallas_call | solution.py:570
  231.7 12.0 %all_to_all.15 = f32[32,8,128]{2,1,0:T(8,128)S(1)} all-to-all(f32[32,8,128]{2,1,0:T(8,128)S(1)} %paired.3), channel_id=1, replica_groups=mesh['grp'=4,'blk'=8] {'grp','blk'}, dimensions={0} | all-to-all | bytes 262144 | tf_op jit(solution)/shard_map/all_to_all | solution.py:748
  (89 shorter events, 14.4 us)
Async XLA Ops:
  2.0 25.0 %collective-permute-start.1 = (bf16[2,4,128,128]{3,2,1,0:T(8,128)(2,1)S(1)}, bf16[2,4,128,128]{3,2,1,0:T(8,128)(2,1)S(1)}, u32[]{:S(2)}, u32[]{:S(2)}) collective-permute-start(bf16[2,4,128,128]{3,2,1,0:T(8,128)(2,1)S(1)} %get-tuple-element.140), channel_id=1, source_target_pairs={{0,16},{8,24},{16,0},{24,8},{1,17},{9,25},{17,1},{25,9},{2,18},{10... | collective-permute-start | bytes 786440 | tf_op jit(solution)/shard_map/ppermute | solution.py:612
  6.1 20.9 %collective-permute-start = (bf16[2,4,128,128]{3,2,1,0:T(8,128)(2,1)S(1)}, bf16[2,4,128,128]{3,2,1,0:T(8,128)(2,1)S(1)}, u32[]{:S(2)}, u32[]{:S(2)}) collective-permute-start(bf16[2,4,128,128]{3,2,1,0:T(8,128)(2,1)S(1)} %get-tuple-element.140), channel_id=1, source_target_pairs={{0,8},{8,0},{16,24},{24,16},{1,9},{9,1},{17,25},{25,17},{2,10},{10... | collective-permute-start | bytes 786440 | tf_op jit(solution)/shard_map/ppermute | solution.py:612
  7.7 19.3 %collective-permute-start.2 = (bf16[2,4,128,128]{3,2,1,0:T(8,128)(2,1)S(1)}, bf16[2,4,128,128]{3,2,1,0:T(8,128)(2,1)S(1)}, u32[]{:S(2)}, u32[]{:S(2)}) collective-permute-start(bf16[2,4,128,128]{3,2,1,0:T(8,128)(2,1)S(1)} %get-tuple-element.140), channel_id=1, source_target_pairs={{0,24},{8,16},{16,8},{24,0},{1,25},{9,17},{17,9},{25,1},{2,26},{10... | collective-permute-start | bytes 786440 | tf_op jit(solution)/shard_map/ppermute | solution.py:612
  18.3 53.1 %collective-permute-start.7 = (bf16[3,2,49,16,128]{4,3,2,1,0:T(8,128)(2,1)}, bf16[3,2,49,16,128]{4,3,2,1,0:T(8,128)(2,1)}, u32[]{:S(2)}, u32[]{:S(2)}) collective-permute-start(bf16[3,2,49,16,128]{4,3,2,1,0:T(8,128)(2,1)} %get-tuple-element.78), channel_id=1, source_target_pairs={{0,6},{1,7},{2,4},{3,5},{4,2},{5,3},{6,0},{7,1},{8,14},{9,15},{10,... | collective-permute-start | bytes 3612680 | tf_op jit(solution)/shard_map/ppermute | solution.py:612
  26.9 8.3 %copy-start.7 = (s32[16]{0:T(128)S(1)}, s32[16]{0:T(128)}, u32[]{:S(2)}) copy-start(s32[16]{0:T(128)} %owner_ref.8) | copy-start | bytes 196
  26.9 9.0 %copy-start.17 = (s32[8]{0:T(128)S(1)}, s32[8]{0:T(128)}, u32[]{:S(2)}) copy-start(s32[8]{0:T(128)} %param.13) | copy-start | bytes 100
  26.9 9.1 %copy-start.18 = (s32[8]{0:T(128)S(1)}, s32[8]{0:T(128)}, u32[]{:S(2)}) copy-start(s32[8]{0:T(128)} %param.11) | copy-start | bytes 100
  27.1 73.2 %copy-start.9 = (bf16[4,2,4,128,128]{4,3,2,1,0:T(8,128)(2,1)}, bf16[4,2,4,128,128]{4,3,2,1,0:T(8,128)(2,1)S(1)}, u32[]{:S(2)}) copy-start(bf16[4,2,4,128,128]{4,3,2,1,0:T(8,128)(2,1)S(1)} %pad_maximum_fusion.refs_0_) | copy-start | bytes 3145732
  27.1 45.0 %collective-permute-start.5 = (bf16[8,128,512]{2,1,0:T(8,128)(2,1)}, bf16[8,128,512]{2,1,0:T(8,128)(2,1)}, u32[]{:S(2)}, u32[]{:S(2)}) collective-permute-start(bf16[8,128,512]{2,1,0:T(8,128)(2,1)} %picked_rows.2), channel_id=1, source_target_pairs={{0,8},{8,0},{16,24},{24,16},{1,9},{9,1},{17,25},{25,17},{2,10},{10... | collective-permute-start | bytes 3145736 | tf_op jit(solution)/shard_map/ppermute | solution.py:612
  30.2 41.9 %collective-permute-start.4 = (bf16[4,2,4,128,128]{4,3,2,1,0:T(8,128)(2,1)S(1)}, bf16[4,2,4,128,128]{4,3,2,1,0:T(8,128)(2,1)S(1)}, u32[]{:S(2)}, u32[]{:S(2)}) collective-permute-start(bf16[4,2,4,128,128]{4,3,2,1,0:T(8,128)(2,1)S(1)} %pad_maximum_fusion.refs_0_), channel_id=1, source_target_pairs={{0,4},{1,5},{2,6},{3,7},{4,0},{5,1},{6,2},{7,3},{8,12},{9,13},{10,... | collective-permute-start | bytes 3145736 | tf_op jit(solution)/shard_map/ppermute | solution.py:612
  31.7 40.4 %collective-permute-start.3 = (bf16[4,2,4,128,128]{4,3,2,1,0:T(8,128)(2,1)S(1)}, bf16[4,2,4,128,128]{4,3,2,1,0:T(8,128)(2,1)S(1)}, u32[]{:S(2)}, u32[]{:S(2)}) collective-permute-start(bf16[4,2,4,128,128]{4,3,2,1,0:T(8,128)(2,1)S(1)} %pad_maximum_fusion.refs_0_), channel_id=1, source_target_pairs={{0,2},{1,3},{2,0},{3,1},{4,6},{5,7},{6,4},{7,5},{8,10},{9,11},{10,... | collective-permute-start | bytes 3145736 | tf_op jit(solution)/shard_map/ppermute | solution.py:612
  33.2 38.2 %collective-permute-start.6 = (bf16[26,128,128]{2,1,0:T(8,128)(2,1)}, bf16[26,128,128]{2,1,0:T(8,128)(2,1)}, u32[]{:S(2)}, u32[]{:S(2)}) collective-permute-start(bf16[26,128,128]{2,1,0:T(8,128)(2,1)} %picked_square.3), channel_id=1, source_target_pairs={{0,16},{8,24},{16,0},{24,8},{1,17},{9,25},{17,1},{25,9},{2,18},{10... | collective-permute-start | bytes 2555912 | tf_op jit(solution)/shard_map/ppermute | solution.py:612
  38.8 33.6 %copy-start.8 = (s32[16]{0:T(128)S(1)}, s32[16]{0:T(128)}, u32[]{:S(2)}) copy-start(s32[16]{0:T(128)} %owner_ref.8) | copy-start | bytes 196
  72.1 28.7 %copy-start.10 = (bf16[4,2,4,128,128]{4,3,2,1,0:T(8,128)(2,1)}, bf16[4,2,4,128,128]{4,3,2,1,0:T(8,128)(2,1)S(1)}, u32[]{:S(2)}) copy-start(bf16[4,2,4,128,128]{4,3,2,1,0:T(8,128)(2,1)S(1)} %collective-permute-done.4.refs_4_) | copy-start | bytes 3145732
  72.1 7.6 %copy-start.11 = (bf16[4,2,4,128,128]{4,3,2,1,0:T(8,128)(2,1)}, bf16[4,2,4,128,128]{4,3,2,1,0:T(8,128)(2,1)S(1)}, u32[]{:S(2)}) copy-start(bf16[4,2,4,128,128]{4,3,2,1,0:T(8,128)(2,1)S(1)} %collective-permute-done.3.refs_2_) | copy-start | bytes 3145732
  72.1 26.7 %collective-permute-start.8 = (bf16[4,2,4,128,128]{4,3,2,1,0:T(8,128)(2,1)S(1)}, bf16[4,2,4,128,128]{4,3,2,1,0:T(8,128)(2,1)}, u32[]{:S(2)}, u32[]{:S(2)}) collective-permute-start(bf16[4,2,4,128,128]{4,3,2,1,0:T(8,128)(2,1)S(1)} %collective-permute-done.3.refs_2_), channel_id=1, source_target_pairs={{0,1},{1,0},{2,3},{3,2},{4,5},{5,4},{6,7},{7,6},{8,9},{9,8},{10,11... | collective-permute-start | bytes 3145736 | tf_op jit(solution)/shard_map/ppermute | solution.py:612
  75.0 23.9 %collective-permute-start.9 = (bf16[2,2,4,128,128]{4,3,2,1,0:T(8,128)(2,1)}, bf16[2,2,4,128,128]{4,3,2,1,0:T(8,128)(2,1)}, u32[]{:S(2)}, u32[]{:S(2)}) collective-permute-start(bf16[2,2,4,128,128]{4,3,2,1,0:T(8,128)(2,1)} %slice.33), channel_id=1, source_target_pairs={{0,4},{1,5},{2,6},{3,7},{4,0},{5,1},{6,2},{7,3},{8,12},{9,13},{10,... | collective-permute-start | bytes 1572872 | tf_op jit(solution)/shard_map/ppermute | solution.py:612
  76.5 22.3 %collective-permute-start.10 = (bf16[2,2,4,128,128]{4,3,2,1,0:T(8,128)(2,1)}, bf16[2,2,4,128,128]{4,3,2,1,0:T(8,128)(2,1)}, u32[]{:S(2)}, u32[]{:S(2)}) collective-permute-start(bf16[2,2,4,128,128]{4,3,2,1,0:T(8,128)(2,1)} %slice.34), channel_id=1, source_target_pairs={{0,2},{1,3},{2,0},{3,1},{4,6},{5,7},{6,4},{7,5},{8,10},{9,11},{10,... | collective-permute-start | bytes 1572872 | tf_op jit(solution)/shard_map/ppermute | solution.py:612
  78.0 5.5 %copy-start.16 = (bf16[10,128,128]{2,1,0:T(8,128)(2,1)S(1)}, bf16[10,128,128]{2,1,0:T(8,128)(2,1)}, u32[]{:S(2)}) copy-start(bf16[10,128,128]{2,1,0:T(8,128)(2,1)} %picked_square.5) | copy-start | bytes 983044
  79.7 12.9 %collective-permute-start.11 = (bf16[10,128,128]{2,1,0:T(8,128)(2,1)}, bf16[10,128,128]{2,1,0:T(8,128)(2,1)}, u32[]{:S(2)}, u32[]{:S(2)}) collective-permute-start(bf16[10,128,128]{2,1,0:T(8,128)(2,1)} %picked_square.4), channel_id=1, source_target_pairs={{0,8},{8,0},{16,24},{24,16},{1,9},{9,1},{17,25},{25,17},{2,10},{10... | collective-permute-start | bytes 983048 | tf_op jit(solution)/shard_map/ppermute | solution.py:612
  83.5 15.3 %collective-permute-start.12 = (bf16[10,128,128]{2,1,0:T(8,128)(2,1)S(1)}, bf16[10,128,128]{2,1,0:T(8,128)(2,1)}, u32[]{:S(2)}, u32[]{:S(2)}) collective-permute-start(bf16[10,128,128]{2,1,0:T(8,128)(2,1)S(1)} %copy-done.16), channel_id=1, source_target_pairs={{0,24},{8,16},{16,8},{24,0},{1,25},{9,17},{17,9},{25,1},{2,26},{10... | collective-permute-start | bytes 983048 | tf_op jit(solution)/shard_map/ppermute | solution.py:612
  98.8 36.4 %collective-permute-start.17 = (bf16[4,2,49,16,128]{4,3,2,1,0:T(8,128)(2,1)}, bf16[4,2,49,16,128]{4,3,2,1,0:T(8,128)(2,1)}, u32[]{:S(2)}, u32[]{:S(2)}) collective-permute-start(bf16[4,2,49,16,128]{4,3,2,1,0:T(8,128)(2,1)} %get-tuple-element.111), channel_id=1, source_target_pairs={{0,2},{1,3},{2,0},{3,1},{4,6},{5,7},{6,4},{7,5},{8,10},{9,11},{10,... | collective-permute-start | bytes 4816904 | tf_op jit(solution)/shard_map/ppermute | solution.py:612
  99.4 36.0 %collective-permute-start.18 = (bf16[4,2,49,16,128]{4,3,2,1,0:T(8,128)(2,1)}, bf16[4,2,49,16,128]{4,3,2,1,0:T(8,128)(2,1)}, u32[]{:S(2)}, u32[]{:S(2)}) collective-permute-start(bf16[4,2,49,16,128]{4,3,2,1,0:T(8,128)(2,1)} %get-tuple-element.112), channel_id=1, source_target_pairs={{0,4},{1,5},{2,6},{3,7},{4,0},{5,1},{6,2},{7,3},{8,12},{9,13},{10,... | collective-permute-start | bytes 4816904 | tf_op jit(solution)/shard_map/ppermute | solution.py:612
  100.3 2.8 %collective-permute-start.15 = (bf16[2,2,4,128,128]{4,3,2,1,0:T(8,128)(2,1)}, bf16[2,2,4,128,128]{4,3,2,1,0:T(8,128)(2,1)S(1)}, u32[]{:S(2)}, u32[]{:S(2)}) collective-permute-start(bf16[2,2,4,128,128]{4,3,2,1,0:T(8,128)(2,1)} %collective-permute-done.9.refs_6_), channel_id=1, source_target_pairs={{0,1},{1,0},{2,3},{3,2},{4,5},{5,4},{6,7},{7,6},{8,9},{9,8},{10,11... | collective-permute-start | bytes 1572872 | tf_op jit(solution)/shard_map/ppermute | solution.py:612
  100.3 5.9 %collective-permute-start.13 = (bf16[4,2,4,128,128]{4,3,2,1,0:T(8,128)(2,1)S(1)}, bf16[4,2,4,128,128]{4,3,2,1,0:T(8,128)(2,1)S(1)}, u32[]{:S(2)}, u32[]{:S(2)}) collective-permute-start(bf16[4,2,4,128,128]{4,3,2,1,0:T(8,128)(2,1)S(1)} %pad_maximum_fusion.refs_0_), channel_id=1, source_target_pairs={{0,1},{1,0},{2,3},{3,2},{4,5},{5,4},{6,7},{7,6},{8,9},{9,8},{10,11... | collective-permute-start | bytes 3145736 | tf_op jit(solution)/shard_map/ppermute | solution.py:612
  100.8 6.2 %collective-permute-start.14 = (bf16[4,2,4,128,128]{4,3,2,1,0:T(8,128)(2,1)S(1)}, bf16[4,2,4,128,128]{4,3,2,1,0:T(8,128)(2,1)}, u32[]{:S(2)}, u32[]{:S(2)}) collective-permute-start(bf16[4,2,4,128,128]{4,3,2,1,0:T(8,128)(2,1)S(1)} %collective-permute-done.4.refs_4_), channel_id=1, source_target_pairs={{0,1},{1,0},{2,3},{3,2},{4,5},{5,4},{6,7},{7,6},{8,9},{9,8},{10,11... | collective-permute-start | bytes 3145736 | tf_op jit(solution)/shard_map/ppermute | solution.py:612
  103.1 3.9 %copy-start.14 = (bf16[2,2,4,128,128]{4,3,2,1,0:T(8,128)(2,1)}, bf16[2,2,4,128,128]{4,3,2,1,0:T(8,128)(2,1)S(1)}, u32[]{:S(2)}) copy-start(bf16[2,2,4,128,128]{4,3,2,1,0:T(8,128)(2,1)S(1)} %collective-permute-done.15.refs_8_) | copy-start | bytes 1572868
  103.1 3.1 %collective-permute-start.16 = (bf16[2,2,4,128,128]{4,3,2,1,0:T(8,128)(2,1)}, bf16[2,2,4,128,128]{4,3,2,1,0:T(8,128)(2,1)S(1)}, u32[]{:S(2)}, u32[]{:S(2)}) collective-permute-start(bf16[2,2,4,128,128]{4,3,2,1,0:T(8,128)(2,1)} %collective-permute-done.10.refs_7_), channel_id=1, source_target_pairs={{0,1},{1,0},{2,3},{3,2},{4,5},{5,4},{6,7},{7,6},{8,9},{9,8},{10,11... | collective-permute-start | bytes 1572872 | tf_op jit(solution)/shard_map/ppermute | solution.py:612
  106.1 0.8 copy-start.15
  106.9 1.0 copy-start.13
  135.5 57.0 %all-to-all-start = ((bf16[32,17,16,128]{3,2,1,0:T(8,128)(2,1)}), bf16[32,17,16,128]{3,2,1,0:T(8,128)(2,1)S(1)}, u32[]{:S(2)}, u32[]{:S(2)}) async-start(bf16[32,17,16,128]{3,2,1,0:T(8,128)(2,1)} %get-tuple-element.115), calls=%async_computation | async-start | bytes 4456448 | tf_op jit(solution)/shard_map/all_to_all | solution.py:748
  140.5 4.8 %copy-start.12 = (bf16[4,2,49,16,128]{4,3,2,1,0:T(8,128)(2,1)S(1)}, bf16[4,2,49,16,128]{4,3,2,1,0:T(8,128)(2,1)}, u32[]{:S(2)}) copy-start(bf16[4,2,49,16,128]{4,3,2,1,0:T(8,128)(2,1)} %get-tuple-element.117) | copy-start | bytes 4816900
  142.8 32.2 %collective-permute-start.22 = (bf16[1,2,49,16,128]{4,3,2,1,0:T(8,128)(2,1)}, bf16[1,2,49,16,128]{4,3,2,1,0:T(8,128)(2,1)S(1)}, u32[]{:S(2)}, u32[]{:S(2)}) collective-permute-start(bf16[1,2,49,16,128]{4,3,2,1,0:T(8,128)(2,1)} %get-tuple-element.121), channel_id=1, source_target_pairs={{0,6},{1,7},{2,4},{3,5},{4,2},{5,3},{6,0},{7,1},{8,14},{9,15},{10,... | collective-permute-start | bytes 1204232 | tf_op jit(solution)/shard_map/ppermute | solution.py:612
  145.2 30.5 %collective-permute-start.23 = (bf16[2,2,49,16,128]{4,3,2,1,0:T(8,128)(2,1)}, bf16[2,2,49,16,128]{4,3,2,1,0:T(8,128)(2,1)}, u32[]{:S(2)}, u32[]{:S(2)}) collective-permute-start(bf16[2,2,49,16,128]{4,3,2,1,0:T(8,128)(2,1)} %slice.42), channel_id=1, source_target_pairs={{0,1},{1,0},{2,3},{3,2},{4,5},{5,4},{6,7},{7,6},{8,9},{9,8},{10,11... | collective-permute-start | bytes 2408456 | tf_op jit(solution)/shard_map/ppermute | solution.py:612
  146.4 29.3 %collective-permute-start.19 = (bf16[2,2,49,16,128]{4,3,2,1,0:T(8,128)(2,1)}, bf16[2,2,49,16,128]{4,3,2,1,0:T(8,128)(2,1)}, u32[]{:S(2)}, u32[]{:S(2)}) collective-permute-start(bf16[2,2,49,16,128]{4,3,2,1,0:T(8,128)(2,1)} %get-tuple-element.137), channel_id=1, source_target_pairs={{0,1},{1,0},{2,3},{3,2},{4,5},{5,4},{6,7},{7,6},{8,9},{9,8},{10,11... | collective-permute-start | bytes 2408456 | tf_op jit(solution)/shard_map/ppermute | solution.py:612
  149.8 26.0 %collective-permute-start.20 = (bf16[2,2,49,16,128]{4,3,2,1,0:T(8,128)(2,1)}, bf16[2,2,49,16,128]{4,3,2,1,0:T(8,128)(2,1)}, u32[]{:S(2)}, u32[]{:S(2)}) collective-permute-start(bf16[2,2,49,16,128]{4,3,2,1,0:T(8,128)(2,1)} %get-tuple-element.135), channel_id=1, source_target_pairs={{0,1},{1,0},{2,3},{3,2},{4,5},{5,4},{6,7},{7,6},{8,9},{9,8},{10,11... | collective-permute-start | bytes 2408456 | tf_op jit(solution)/shard_map/ppermute | solution.py:612
  152.6 23.2 %collective-permute-start.21 = (bf16[2,2,49,16,128]{4,3,2,1,0:T(8,128)(2,1)}, bf16[2,2,49,16,128]{4,3,2,1,0:T(8,128)(2,1)}, u32[]{:S(2)}, u32[]{:S(2)}) collective-permute-start(bf16[2,2,49,16,128]{4,3,2,1,0:T(8,128)(2,1)} %get-tuple-element.133), channel_id=1, source_target_pairs={{0,1},{1,0},{2,3},{3,2},{4,5},{5,4},{6,7},{7,6},{8,9},{9,8},{10,11... | collective-permute-start | bytes 2408456 | tf_op jit(solution)/shard_map/ppermute | solution.py:612
  175.0 0.8 copy-start.4
  192.5 4.6 %copy-start.6 = (s32[2]{0:T(128)S(1)}, s32[2]{0:T(128)}, u32[]{:S(2)}) copy-start(s32[2]{0:T(128)} %pad_add_fusion.where_ref.group_ref) | copy-start | bytes 28
  192.5 33.9 %all-to-all-start.1 = ((bf16[16,32,16,128]{3,2,1,0:T(8,128)(2,1)}), bf16[16,32,16,128]{3,2,1,0:T(8,128)(2,1)}, u32[]{:S(2)}, u32[]{:S(2)}) async-start(bf16[16,32,16,128]{3,2,1,0:T(8,128)(2,1)} %other_pairs.1), calls=%async_computation.1 | async-start | bytes 4194304 | tf_op jit(solution)/shard_map/all_to_all | solution.py:748
  197.1 1.1 copy-start.2
  198.2 1.1 copy-start.3
  199.4 1.0 copy-start.5
  206.1 2.0 copy-start
  226.4 2.2 copy-start.1
